TPU v7x, 256 devices: a whole 4x4x8 slice. The times are simulated.
256 devices in a mesh: outer: 16 (over z_hi, y), inner: 8 (over x, z_lo), section: 2 (over core).
Axes of the slice: x: 4, y: 4, z: 8 (z_hi: 4, z_lo: 2; z = z_hi * 2 + z_lo), core: 2. Of those that a mesh axis runs over, the one named last changes fastest.
Arguments:
- grad_out: bfloat16 [2, 16384, 2560], P('section', ('outer', 'inner')), may hold values from -6 to 6
- route_ids: int32 [2, 16384, 6], P('section', ('outer', 'inner')), may hold values from 0 to 127, as said below
- route_w: float32 [2, 16384, 6], P('section', ('outer', 'inner')), may hold values from 0.05 to 0.6
- saved: bfloat16 [2, 128, 896, 1536], P('section', ('outer', 'inner')), may hold values from -6 to 6
- w_up: bfloat16 [2, 128, 2560, 768], P('section', ('outer', 'inner')), may hold values from -0.125 to 0.125
- w_down: bfloat16 [2, 128, 768, 2560], P('section', ('outer', 'inner')), may hold values from -0.21875 to 0.21875
Outputs:
- input_grad: bfloat16 [2, 16384, 2560], P('section', ('outer', 'inner'))
- gate_grad: bfloat16 [2, 128, 896, 768], P('section', ('outer', 'inner'))
Inputs may be any that keep to these rules, and one draw needn't show every extreme that they name: `route_ids`: each row names 6 different experts, 2 in each of 3 groups of 8 consecutive numbers; the routes of one group stand next to each other in route order. In each layer one expert is named by exactly 28 of the 128 rows of every index of outer and inner, and its group by no other rows.
All inputs are finite; a program needn't handle non-finite values.
Results may differ from a plain program's by a relative error of at most 0.012.
Values may be sent and summed in bfloat16 or wider, within the bound.
No kernel may reach another device: no remote copies, remote signals or barrier semaphores. Data moves between devices by JAX's collectives and lax.ppermute only.
A program may use at most 128 MiB of HBM per device.

v0:
```python
import jax
import jax.numpy as jnp
from jax import lax
from jax.sharding import PartitionSpec as P

ROUTE_GROUPS = 3


def from_behind(block, axis, distance):
    devices = range(lax.axis_size(axis))
    route = [((i - distance) % len(devices), i) for i in devices]
    return lax.ppermute(block, axis, route)


def on_device(grad_out, route_ids, route_w, saved, w_up, w_down):
    groups_outer = lax.axis_size("outer")
    groups_inner = lax.axis_size("inner")
    experts = groups_outer * groups_inner
    tok_rows = grad_out.shape[1]
    features = grad_out.shape[2]
    per_token = route_ids.shape[2]
    slots_all = saved.shape[2]
    capacity = slots_all // experts
    hidden = w_up.shape[3]
    routes = tok_rows * per_token
    route_groups = ROUTE_GROUPS
    per_group = per_token // route_groups
    group_cap = max(2, 7 * tok_rows * route_groups // (6 * groups_outer))
    block_ids = route_ids[0]
    pair_group = block_ids[:, ::per_group] // groups_inner
    group_hot = (
        pair_group[:, :, None] == jnp.arange(groups_outer, dtype=jnp.int32)[None, None, :]
    ).astype(jnp.int32)
    token_groups = jnp.sum(group_hot, axis=1)
    earlier = jnp.cumsum(token_groups, axis=0) - token_groups
    group_rank = jnp.sum(earlier[:, None, :] * group_hot, axis=2)
    admitted = group_rank < group_cap
    route_adm = jnp.repeat(admitted.astype(jnp.int32), per_group, axis=1).reshape(routes)
    expert_ids = block_ids.reshape(routes)
    one_hot = (expert_ids[:, None] == jnp.arange(experts, dtype=jnp.int32)[None, :]).astype(
        jnp.int32
    ) * route_adm[:, None]
    slot_rank = jnp.sum(jnp.cumsum(one_hot, axis=0) * one_hot, axis=1) - 1
    kept = (route_adm > 0) & (slot_rank < capacity)
    slot_index = jnp.where(kept, expert_ids * capacity + slot_rank, slots_all)
    padded_rows = jnp.concatenate([grad_out[0], jnp.zeros((1, features), jnp.bfloat16)], axis=0)
    source_route = (
        jnp.full((slots_all + 1,), routes, jnp.int32)
        .at[slot_index]
        .set(jnp.arange(routes, dtype=jnp.int32))[:slots_all]
    )
    padded_weight = jnp.concatenate(
        [route_w[0].reshape(routes), jnp.zeros((per_token,), jnp.float32)], axis=0
    )
    outgoing = (
        padded_rows[source_route // per_token].astype(jnp.float32)
        * padded_weight[source_route][:, None]
    ).astype(jnp.bfloat16)
    arrived = lax.all_to_all(
        outgoing.reshape(experts, capacity, features),
        ("outer", "inner"),
        split_axis=0,
        concat_axis=0,
        tiled=True,
    )
    arrived = arrived.reshape(slots_all, features)
    hidden_grad = lax.dot_general(
        arrived, w_down[0, 0], (((1,), (1,)), ((), ())), preferred_element_type=jnp.float32
    )
    gate_act = saved[0, 0, :, :hidden].astype(jnp.float32)
    up_value = saved[0, 0, :, hidden:].astype(jnp.float32)
    up_grad = (hidden_grad * gate_act).astype(jnp.bfloat16)
    gate_grad = (hidden_grad * up_value).astype(jnp.bfloat16)
    input_rows = lax.dot_general(
        up_grad, w_up[0, 0], (((1,), (1,)), ((), ())), preferred_element_type=jnp.float32
    ).astype(jnp.bfloat16)
    returned = lax.all_to_all(
        input_rows.reshape(experts, capacity, features),
        ("outer", "inner"),
        split_axis=0,
        concat_axis=0,
        tiled=True,
    )
    padded_back = jnp.concatenate(
        [returned.reshape(slots_all, features), jnp.zeros((1, features), jnp.bfloat16)], axis=0
    )
    picked = padded_back[slot_index].reshape(tok_rows, route_groups, per_group, features)
    group_part = jnp.sum(picked.astype(jnp.float32), axis=2).astype(jnp.bfloat16)
    token_grad = jnp.sum(group_part.astype(jnp.float32), axis=1).astype(jnp.bfloat16)
    received = from_behind(token_grad, "section", -1)
    return (received[None], gate_grad[None, None])


def solution(mesh):
    return jax.shard_map(
        on_device,
        mesh=mesh,
        in_specs=(
            P("section", ("outer", "inner"), None),
            P("section", ("outer", "inner"), None),
            P("section", ("outer", "inner"), None),
            P("section", ("outer", "inner"), None, None),
            P("section", ("outer", "inner"), None, None),
            P("section", ("outer", "inner"), None, None),
        ),
        out_specs=(
            P("section", ("outer", "inner"), None),
            P("section", ("outer", "inner"), None, None),
        ),
        check_vma=False,
    )
```

profile of v0, /device:TPU:1, one launch (start us, length us, event | category | flops | bytes accessed | tf_op | source)
XLA Modules:
  0.0 369.1 jit_solution(7745770829625390228)
XLA Ops:
  0.6 0.7 broadcast_multiply_fusion
  1.3 0.7 copy.35
  2.0 0.8 copy.25
  5.1 0.8 copy.32
  7.1 3.4 scatter_custom_fusion
  10.5 3.7 gather_fusion.1
  14.4 5.3 %gather_fusion = bf16[896,2560]{1,0:T(8,128)(2,1)} fusion(bf16[129,2560]{1,0:T(8,128)(2,1)S(1)} %concatenate.9, s32[1024]{0:T(1024)S(1)} %get-tuple-element.7), kind=kCustom, calls=%fused_computation | custom fusion | bytes 9178624 | tf_op jit(solution)/shard_map/gather | solution.py:56
  19.8 8.0 %reshape.123 = f32[128,7,2560]{2,1,0:T(8,128)} reshape(bf16[896,2560]{1,0:T(8,128)(2,1)} %gather_fusion) | data formatting | bytes 13762560 | tf_op jit(solution)/shard_map/convert_element_type | solution.py:56
  27.8 4.6 %multiply_convert_fusion = bf16[128,7,2560]{2,1,0:T(8,128)(2,1)S(1)} fusion(f32[128,7,2560]{2,1,0:T(8,128)} %reshape.123, f32[128,7]{1,0:T(8,128)S(1)} %mul.68), kind=kLoop, calls=%fused_computation.4 | loop fusion | flops 4587520 | bytes 13766144 | tf_op jit(solution)/shard_map/convert_element_type | solution.py:58
  32.5 136.2 %all_to_all.10 = bf16[128,7,2560]{2,1,0:T(8,128)(2,1)} all-to-all(bf16[128,7,2560]{2,1,0:T(8,128)(2,1)S(1)} %multiply_convert_fusion), channel_id=1, replica_groups=mesh['outer'=16,'inner'=8,'section'=2] {'outer','inner'}, dimensions={0} | all-to-all | bytes 9175040 | tf_op jit(solution)/shard_map/all_to_all | solution.py:59
  168.7 7.5 %reshape.119 = bf16[896,2560]{1,0:T(8,128)(2,1)} reshape(bf16[128,7,2560]{2,1,0:T(8,128)(2,1)} %all_to_all.10) | data formatting | bytes 9175040 | tf_op jit(solution)/shard_map/reshape | solution.py:66
  176.2 6.9 %fusion.1 = f32[896,768]{1,0:T(8,128)S(1)} fusion(bf16[896,2560]{1,0:T(8,128)(2,1)} %reshape.119, bf16[1,1,768,2560]{3,2,1,0:T(8,128)(2,1)} %param.11), kind=kOutput, calls=%fused_computation.7 | convolution fusion | flops 3523215360 | bytes 11272192 | tf_op jit(solution)/shard_map/dot_general | solution.py:67
  183.1 5.4 %convolution_convert_fusion = bf16[896,2560]{1,0:T(8,128)(2,1)} fusion(bf16[1,1,2560,768]{3,2,1,0:T(8,128)(2,1)S(1)} %copy-done.2, f32[896,768]{1,0:T(8,128)S(1)} %fusion.1, bf16[1,1,896,1536]{3,2,1,0:T(8,128)(2,1)S(1)} %copy-done), kind=kOutput, calls=%fused_computation.5 | convolution fusion | flops 3527573504 | bytes 12648448 | tf_op jit(solution)/shard_map/dot_general | solution.py:74
  188.5 7.4 %reshape.120 = bf16[128,7,2560]{2,1,0:T(8,128)(2,1)} reshape(bf16[896,2560]{1,0:T(8,128)(2,1)} %convolution_convert_fusion) | data formatting | bytes 9175040 | tf_op jit(solution)/shard_map/reshape | solution.py:78
  196.0 7.5 %all-to-all-start.1 = ((bf16[128,7,2560]{2,1,0:T(8,128)(2,1)}), bf16[128,7,2560]{2,1,0:T(8,128)(2,1)}, u32[]{:S(2)}, u32[]{:S(2)}) async-start(bf16[128,7,2560]{2,1,0:T(8,128)(2,1)} %reshape.120), calls=%async_computation.1 | async-start | bytes 10485760 | tf_op jit(solution)/shard_map/all_to_all | solution.py:77
  203.5 117.5 %all-to-all-done.1 = bf16[128,7,2560]{2,1,0:T(8,128)(2,1)} async-done(((bf16[128,7,2560]{2,1,0:T(8,128)(2,1)}), bf16[128,7,2560]{2,1,0:T(8,128)(2,1)}, u32[]{:S(2)}, u32[]{:S(2)}) %all-to-all-start.1) | async-done | bytes 4587552 | tf_op jit(solution)/shard_map/all_to_all | solution.py:77
  321.0 7.5 %reshape.121 = bf16[896,2560]{1,0:T(8,128)(2,1)} reshape(bf16[128,7,2560]{2,1,0:T(8,128)(2,1)} %all-to-all-done.1) | data formatting | bytes 9175040 | tf_op jit(solution)/shard_map/reshape | solution.py:85
  328.5 4.7 %concatenate.11 = bf16[897,2560]{1,0:T(8,128)(2,1)} pad(bf16[896,2560]{1,0:T(8,128)(2,1)} %reshape.121, bf16[]{:T(256)} %constant.24.clone.1), padding=0_1x0_0 | pad | bytes 9180162 | tf_op jit(solution)/shard_map/concatenate | solution.py:84
  333.2 11.3 %gather_fusion.2 = bf16[768,2560]{1,0:T(8,128)(2,1)} fusion(bf16[897,2560]{1,0:T(8,128)(2,1)} %concatenate.11, s32[1024]{0:T(1024)S(1)} %pad_clamp_fusion), kind=kCustom, calls=%fused_computation.2 | custom fusion | bytes 7867392 | tf_op jit(solution)/shard_map/gather | solution.py:87
  344.5 8.7 %reshape.122 = bf16[128,3,2,2560]{3,2,1,0:T(2,128)(2,1)} reshape(bf16[768,2560]{1,0:T(8,128)(2,1)} %gather_fusion.2) | data formatting | bytes 7864320 | tf_op jit(solution)/shard_map/reshape | solution.py:87
  353.2 7.5 %reduce_sum.49 = bf16[128,2560]{1,0:T(8,128)(2,1)S(1)} reduce(bf16[128,3,2,2560]{3,2,1,0:T(2,128)(2,1)} %reshape.122, bf16[]{:T(256)} %constant.24.clone.1), dimensions={1,2}, to_apply=%region_7.8 | reduce | flops 1638400 | bytes 4587522 | tf_op jit(solution)/shard_map/reduce_sum | solution.py:89
  360.7 4.8 %collective-permute-start = (bf16[128,2560]{1,0:T(8,128)(2,1)S(1)}, bf16[128,2560]{1,0:T(8,128)(2,1)S(1)}, u32[]{:S(2)}, u32[]{:S(2)}) collective-permute-start(bf16[128,2560]{1,0:T(8,128)(2,1)S(1)} %reduce_sum.49), channel_id=1, source_target_pairs={{1,0},{0,1},{3,2},{2,3},{5,4},{4,5},{7,6},{6,7},{9,8},{8,9},{11,10... | collective-permute-start | bytes 1966088 | tf_op jit(solution)/shard_map/ppermute | solution.py:12
  365.5 2.7 fusion.6
  368.3 0.8 copy.37
  (45 shorter events, 3.7 us)
Async XLA Ops:
  4.4 9.9 %copy-start.1 = (bf16[1,128,2560]{2,1,0:T(8,128)(2,1)S(1)}, bf16[1,128,2560]{2,1,0:T(8,128)(2,1)}, u32[]{:S(2)}) copy-start(bf16[1,128,2560]{2,1,0:T(8,128)(2,1)} %param.6) | copy-start | bytes 1966084
  176.2 6.9 %copy-start = (bf16[1,1,896,1536]{3,2,1,0:T(8,128)(2,1)S(1)}, bf16[1,1,896,1536]{3,2,1,0:T(8,128)(2,1)}, u32[]{:S(2)}) copy-start(bf16[1,1,896,1536]{3,2,1,0:T(8,128)(2,1)} %param.9) | copy-start | bytes 8257540
  176.2 6.9 %copy-start.2 = (bf16[1,1,2560,768]{3,2,1,0:T(8,128)(2,1)S(1)}, bf16[1,1,2560,768]{3,2,1,0:T(8,128)(2,1)}, u32[]{:S(2)}) copy-start(bf16[1,1,2560,768]{3,2,1,0:T(8,128)(2,1)} %param.10) | copy-start | bytes 11796484
  196.0 125.0 %all-to-all-start.1 = ((bf16[128,7,2560]{2,1,0:T(8,128)(2,1)}), bf16[128,7,2560]{2,1,0:T(8,128)(2,1)}, u32[]{:S(2)}, u32[]{:S(2)}) async-start(bf16[128,7,2560]{2,1,0:T(8,128)(2,1)} %reshape.120), calls=%async_computation.1 | async-start | bytes 10485760 | tf_op jit(solution)/shard_map/all_to_all | solution.py:77
  360.7 7.6 %collective-permute-start = (bf16[128,2560]{1,0:T(8,128)(2,1)S(1)}, bf16[128,2560]{1,0:T(8,128)(2,1)S(1)}, u32[]{:S(2)}, u32[]{:S(2)}) collective-permute-start(bf16[128,2560]{1,0:T(8,128)(2,1)S(1)} %reduce_sum.49), channel_id=1, source_target_pairs={{1,0},{0,1},{3,2},{2,3},{5,4},{4,5},{7,6},{6,7},{9,8},{8,9},{11,10... | collective-permute-start | bytes 1966088 | tf_op jit(solution)/shard_map/ppermute | solution.py:12
where the time goes:
time: 370 us; the launch traced here: 369 us
  blocking collectives  136 us (37%)
  waiting for transfers between devices  117 us (32%)
  local copies, waits for them, and re-layouts  73.2 us (20%)
  other arithmetic  16.6 us (4%)
  matrix products  12.4 us (3%)
  starting transfers between devices  12.4 us (3%)
    all_to_all x1, blocking collectives, on_device(): lax.all_to_all(outgoing.reshape(experts, capacity, features), ('outer', '...  136 us
    all_to_all x1, waiting for transfers between devices, on_device(): lax.all_to_all(input_rows.reshape(experts, capacity, features), ('outer',...  117 us
    gather x1, local copies, waits for them, and re-layouts, on_device(): padded_back[slot_index].reshape(tok_rows, route_groups, per_group, features)  11.3 us
    reshape x1, local copies, waits for them, and re-layouts, on_device(): padded_back[slot_index].reshape(tok_rows, route_groups, per_group, features)  8.72 us
    convert_element_type x1, local copies, waits for them, and re-layouts, on_device(): padded_rows[source_route // per_token].astype(jnp.float32)  8.04 us
    all_to_all x1, starting transfers between devices, on_device(): lax.all_to_all(input_rows.reshape(experts, capacity, features), ('outer',...  7.53 us
    reduce_sum x1, other arithmetic, on_device(): jnp.sum(group_part.astype(jnp.float32), axis=1).astype(jnp.bfloat16)  7.52 us
    reshape x1, local copies, waits for them, and re-layouts, on_device(): arrived = arrived.reshape(slots_all, features)  7.5 us
  transfers between devices with their start and end apart: 2, of which 1 were waited for; matrix products, arithmetic and copies ran while one was open for 1% of the time, Pallas kernels for 0%

commit v1 on v0

v1 whole, which is shorter than its diff:
```python
import functools
import jax
import jax.numpy as jnp
from jax import lax
from jax.experimental import pallas as pl
from jax.experimental.pallas import tpu as pltpu
from jax.sharding import PartitionSpec as P

ROUTE_GROUPS = 3
F32 = jnp.float32
BF16 = jnp.bfloat16
I32 = jnp.int32
SUB = 8
TAIL = 256


def iota(shape, dim):
    return lax.broadcasted_iota(I32, shape, dim)


def dot(a, b):
    return lax.dot_general(a, b, (((1,), (0,)), ((), ())), preferred_element_type=F32)


def dot_t(a, b):
    return lax.dot_general(a, b, (((1,), (1,)), ((), ())), preferred_element_type=F32)


def flag(mask, kind=BF16):
    return jnp.where(mask, 1.0, 0.0).astype(kind)


def dispatch_kernel(dims, ids_ref, w_ref, g_ref, out_ref, rank_ref, lhs_ref, scale_ref, tails_ref):
    experts, tok, routes, in_group, group_cap, cap, main, width = dims
    step = pl.program_id(0)
    rows = experts * SUB

    @pl.when(step == 0)
    def _():
        e = iota((experts, tok), 0)
        named = jnp.zeros((experts, tok), F32)
        weight = jnp.zeros((experts, tok), F32)
        near = jnp.zeros((experts, tok), F32)
        for k in range(routes):
            ids = ids_ref[k : k + 1, :]
            hit = ids == e
            named += flag(hit, F32)
            weight += jnp.where(hit, w_ref[k : k + 1, :], 0.0)
            if k % (routes // ROUTE_GROUPS) == 0:
                near += flag(ids // in_group == e // in_group, F32)
        before = flag(iota((tok, tok), 0) < iota((tok, tok), 1))
        group_rank = dot(near.astype(BF16), before)
        admitted = (named > 0) & (group_rank < group_cap)
        slot_rank = dot(flag(admitted), before)
        rank = jnp.where(admitted & (slot_rank < cap), slot_rank, -1.0)
        rank_ref[...] = rank
        row = iota((rows, experts), 0)
        col = iota((rows, experts), 1)
        spread = flag(row // SUB == col)
        rank_rows = dot(spread, rank.astype(BF16))
        slot = flag(rank_rows == (iota((rows, tok), 0) % SUB).astype(F32), F32)
        high = weight.astype(BF16)
        rest = weight - high.astype(F32)
        mid = rest.astype(BF16)
        low = (rest - mid.astype(F32)).astype(BF16)
        weight_rows = (dot(spread, high) + dot(spread, mid)) + dot(spread, low)
        last = iota((rows, 1), 0) % SUB == SUB - 1
        scale_ref[...] = jnp.sum(slot * weight_rows, axis=1, keepdims=True) + flag(last, F32)
        lhs_ref[:, :tok] = slot.astype(BF16)
        lhs_ref[:, tok:] = flag((row // SUB == col) & (row % SUB == SUB - 1))
        g_tail = g_ref[:, main:]
        for j in range(main // TAIL):
            if j < cap:
                here = rank == float(j)
                w_slot = jnp.sum(jnp.where(here, weight, 0.0), axis=1, keepdims=True)
                tails_ref[:, j * TAIL : (j + 1) * TAIL] = (dot(flag(here), g_tail) * w_slot).astype(BF16)
            else:
                tails_ref[:, j * TAIL : (j + 1) * TAIL] = jnp.zeros((experts, TAIL), BF16)

    for j in range(width // TAIL):
        at = pl.ds(pl.multiple_of(step * width + j * TAIL, TAIL), TAIL)
        right = jnp.concatenate([g_ref[:, at], tails_ref[:, at]], axis=0)
        out_ref[:, j * TAIL : (j + 1) * TAIL] = (dot(lhs_ref[...], right) * scale_ref[...]).astype(BF16)


def picks_kernel(dims, ids_ref, rank_ref, pick_ref, pick_tail_ref):
    experts, tok, routes, parts = dims
    e = iota((experts, tok), 0)
    per = routes // ROUTE_GROUPS
    rows = experts * SUB
    spread = flag(iota((experts, rows), 0) == iota((experts, rows), 1) // SUB)
    lane = (iota((tok, rows), 1) % SUB).astype(F32)
    for j in range(ROUTE_GROUPS):
        hit = ids_ref[j * per : j * per + 1, :] == e
        for k in range(1, per):
            hit = hit | (ids_ref[j * per + k : j * per + k + 1, :] == e)
        rank = jnp.where(hit, rank_ref[...], -1.0).T
        pick_ref[j * tok : (j + 1) * tok, :] = flag(dot(rank.astype(BF16), spread) == lane)
        for r in range(parts):
            pick_tail_ref[r, j * tok : (j + 1) * tok, :] = flag(rank == float(r))


def expert_kernel(dims, a_ref, saved_ref, wd_ref, wu_ref, out_ref, gate_ref, place_ref, fetch_ref):
    rows, slots, cap, hidden, main = dims

    @pl.when(pl.program_id(0) == 0)
    def _():
        a, b = iota((rows, rows), 0), iota((rows, rows), 1)
        same = a // SUB == b // SUB
        for r in range(cap):
            place_ref[r] = flag(same & (a % SUB == SUB - 1) & (b % SUB == r))
            fetch_ref[r] = flag(same & (b % SUB == SUB - 1) & (a % SUB == r))

    tail = dot(fetch_ref[0], a_ref[:, :TAIL])
    for r in range(1, cap):
        tail += dot(fetch_ref[r], a_ref[:, r * TAIL : (r + 1) * TAIL])
    hidden_grad = dot_t(a_ref[...], wd_ref[:, :main]) + dot_t(tail.astype(BF16), wd_ref[:, main:])
    a, c = iota((rows, slots), 0), iota((rows, slots), 1)
    widen = flag((a % SUB < cap) & (c == a // SUB * cap + a % SUB))
    c, a = iota((slots, rows), 0), iota((slots, rows), 1)
    narrow = flag((a % SUB < cap) & (c == a // SUB * cap + a % SUB))
    gate_act = dot(widen, saved_ref[:, :hidden])
    up_grad = (hidden_grad * gate_act).astype(BF16)
    up_value = dot(widen, saved_ref[:, hidden:])
    gate_grad = (hidden_grad * up_value).astype(BF16)
    gate_ref[...] = dot(narrow, gate_grad).astype(BF16)
    tail = dot_t(up_grad, wu_ref[main:, :]).astype(BF16)
    for j in range(main // TAIL):
        part = dot_t(up_grad, wu_ref[j * TAIL : (j + 1) * TAIL, :])
        if j < cap:
            part += dot(place_ref[j], tail)
        out_ref[:, j * TAIL : (j + 1) * TAIL] = part.astype(BF16)


def combine_kernel(dims, pick_ref, pick_tail_ref, back_ref, out_ref, tail_ref):
    experts, tok, main, width, steps = dims
    step = pl.program_id(0)
    rows = experts * SUB

    def joined(part):
        part = part.astype(BF16).astype(F32)
        total = part[:tok]
        for j in range(1, ROUTE_GROUPS):
            total += part[j * tok : (j + 1) * tok]
        return total.astype(BF16)

    @pl.when(step == 0)
    def _():
        tail_ref[...] = jnp.zeros_like(tail_ref)

    lasts = flag(iota((experts, rows), 1) == iota((experts, rows), 0) * SUB + SUB - 1)
    for j in range(width // TAIL):
        block = back_ref[:, j * TAIL : (j + 1) * TAIL]
        at = pl.ds(pl.multiple_of(step * width + j * TAIL, TAIL), TAIL)
        out_ref[:, at] = joined(dot(pick_ref[...], block))
        tails = dot(lasts, block).astype(BF16)
        tail_ref[...] += dot(pick_tail_ref[step * (width // TAIL) + j], tails)

    @pl.when(step == steps - 1)
    def _():
        out_ref[:, main:] = joined(tail_ref[...])


def whole(shape):
    return pl.BlockSpec(shape, lambda *_: (0,) * len(shape), pipeline_mode=pl.Buffered(1))


def params(mib):
    return pltpu.CompilerParams(vmem_limit_bytes=mib * 2**20, dimension_semantics=("arbitrary",))


def cost(flops, moved):
    return pl.CostEstimate(flops=flops, bytes_accessed=moved, transcendentals=0)


def on_device(grad_out, route_ids, route_w, saved, w_up, w_down):
    groups_outer = lax.axis_size("outer")
    groups_inner = lax.axis_size("inner")
    experts = groups_outer * groups_inner
    tok, features = grad_out.shape[1:]
    routes = route_ids.shape[2]
    slots_all = saved.shape[2]
    cap = slots_all // experts
    hidden = w_up.shape[3]
    group_cap = max(2, 7 * tok * ROUTE_GROUPS // (6 * groups_outer))
    main = features - TAIL
    rows = experts * SUB
    steps = 3
    width = main // steps
    parts = main // TAIL
    ids = route_ids[0].T
    weights = route_w[0].T

    with jax.named_scope("dispatch"):
        outgoing, rank = pl.pallas_call(
            functools.partial(
                dispatch_kernel, (experts, tok, routes, groups_inner, group_cap, cap, main, width)
            ),
            grid=(steps,),
            in_specs=[whole((routes, tok)), whole((routes, tok)), whole((tok, features))],
            out_specs=[pl.BlockSpec((rows, width), lambda i: (0, i)), whole((experts, tok))],
            out_shape=[
                jax.ShapeDtypeStruct((rows, main), BF16),
                jax.ShapeDtypeStruct((experts, tok), F32),
            ],
            scratch_shapes=[
                pltpu.VMEM((rows, 2 * tok), BF16),
                pltpu.VMEM((rows, 1), F32),
                pltpu.VMEM((experts, main), BF16),
            ],
            compiler_params=params(24),
            cost_estimate=cost(2 * rows * 2 * tok * main, 2 * rows * main),
        )(ids, weights, grad_out[0])

    with jax.named_scope("picks"):
        pick, pick_tail = pl.pallas_call(
            functools.partial(picks_kernel, (experts, tok, routes, parts)),
            out_shape=[
                jax.ShapeDtypeStruct((ROUTE_GROUPS * tok, rows), BF16),
                jax.ShapeDtypeStruct((parts, ROUTE_GROUPS * tok, experts), BF16),
            ],
            compiler_params=pltpu.CompilerParams(vmem_limit_bytes=16 * 2**20),
            cost_estimate=cost(2 * ROUTE_GROUPS * tok * experts * rows, 4 * ROUTE_GROUPS * tok * rows),
        )(ids, rank)

    def exchange(block):
        moved = lax.all_to_all(
            block.reshape(experts, SUB, main), ("outer", "inner"), split_axis=0, concat_axis=0, tiled=True
        )
        return moved.reshape(rows, main)

    arrived = exchange(outgoing)

    with jax.named_scope("expert"):
        blocks = 4
        part, slots = rows // blocks, slots_all // blocks
        expert_rows, gate_grad = pl.pallas_call(
            functools.partial(expert_kernel, (part, slots, cap, hidden, main)),
            grid=(blocks,),
            in_specs=[
                pl.BlockSpec((part, main), lambda i: (i, 0)),
                pl.BlockSpec((slots, 2 * hidden), lambda i: (i, 0)),
                whole((hidden, features)),
                whole((features, hidden)),
            ],
            out_specs=[
                pl.BlockSpec((part, main), lambda i: (i, 0)),
                pl.BlockSpec((slots, hidden), lambda i: (i, 0)),
            ],
            out_shape=[
                jax.ShapeDtypeStruct((rows, main), BF16),
                jax.ShapeDtypeStruct((slots_all, hidden), BF16),
            ],
            scratch_shapes=[pltpu.VMEM((cap, part, part), BF16), pltpu.VMEM((cap, part, part), BF16)],
            compiler_params=params(40),
            cost_estimate=cost(4 * rows * features * hidden, 4 * (rows * main + features * hidden)),
        )(arrived, saved[0, 0], w_down[0, 0], w_up[0, 0])

    returned = exchange(expert_rows)

    with jax.named_scope("combine"):
        token_grad = pl.pallas_call(
            functools.partial(combine_kernel, (experts, tok, main, width, steps)),
            grid=(steps,),
            in_specs=[
                whole((ROUTE_GROUPS * tok, rows)),
                whole((parts, ROUTE_GROUPS * tok, experts)),
                pl.BlockSpec((rows, width), lambda i: (0, i)),
            ],
            out_specs=whole((tok, features)),
            out_shape=jax.ShapeDtypeStruct((tok, features), BF16),
            scratch_shapes=[pltpu.VMEM((ROUTE_GROUPS * tok, TAIL), F32)],
            compiler_params=params(24),
            cost_estimate=cost(2 * ROUTE_GROUPS * tok * rows * main, 2 * rows * main),
        )(pick, pick_tail, returned)

    count = lax.axis_size("section")
    received = lax.ppermute(token_grad, "section", [((i + 1) % count, i) for i in range(count)])
    return (received[None], gate_grad[None, None])


def solution(mesh):
    return jax.shard_map(
        on_device,
        mesh=mesh,
        in_specs=(
            P("section", ("outer", "inner"), None),
            P("section", ("outer", "inner"), None),
            P("section", ("outer", "inner"), None),
            P("section", ("outer", "inner"), None, None),
            P("section", ("outer", "inner"), None, None),
            P("section", ("outer", "inner"), None, None),
        ),
        out_specs=(
            P("section", ("outer", "inner"), None),
            P("section", ("outer", "inner"), None, None),
        ),
        check_vma=False,
    )
```

time: 370 us -> 280 us (0.76)
  local copies, waits for them, and re-layouts: 73.2 us -> 3.31 us
  Pallas kernels: 0 us -> 31.2 us
  other arithmetic: 16.6 us -> 0 us
  matrix products: 12.4 us -> 0 us
  blocking collectives: 136 us -> 125 us
  waiting for transfers between devices: 117 us -> 108 us
    pallas_call x0 -> x4, Pallas kernels: none -> 31.2 us  [the longest x1 22 us: on_device(): pl.pallas_call(functools.partial(expert_kernel, (part, slots, cap, hidden...]
    reshape x4 -> x0, local copies, waits for them, and re-layouts: 31.2 us -> none  [the longest x1 8.72 us: on_device(): padded_back[slot_index].reshape(tok_rows, route_groups, per_group, features)]
    gather x3 -> x0, local copies, waits for them, and re-layouts: 20.3 us -> none  [the longest x1 11.3 us: on_device(): padded_back[slot_index].reshape(tok_rows, route_groups, per_group, features)]
    dot_general x2 -> x0, matrix products: 12.4 us -> none  [the longest x1 6.91 us: on_device(): lax.dot_general(arrived, w_down[0, 0], (((1,), (1,)), ((), ())), preferre...]
    all_to_all x1, waiting for transfers between devices: 117 us -> 106 us  [exchange(): lax.all_to_all(block.reshape(experts, SUB, main), ('outer', 'inner'), spl...]
    all_to_all x1, blocking collectives: 136 us -> 125 us  [exchange(): lax.all_to_all(block.reshape(experts, SUB, main), ('outer', 'inner'), spl...]
    convert_element_type x2 -> x0, local copies, waits for them, and re-layouts: 8.15 us -> none  [the longest x1 8.04 us: on_device(): padded_rows[source_route // per_token].astype(jnp.float32)]
    reduce_sum x4 -> x0, other arithmetic: 7.96 us -> none  [the longest x1 7.52 us: on_device(): jnp.sum(group_part.astype(jnp.float32), axis=1).astype(jnp.bfloat16)]
  transfers between devices with their start and end apart: 2 -> 2, of which waited for: 1 -> 2; matrix products, arithmetic and copies ran while one was open for 1% -> 0% of each run, Pallas kernels for 0% -> 0%
where the time goes in v1:
time: 280 us
  blocking collectives  125 us (45%)
  waiting for transfers between devices  108 us (39%)
  Pallas kernels  31.2 us (11%)
  starting transfers between devices  12.1 us (4%)
  local copies, waits for them, and re-layouts  3.31 us (1%)
    all_to_all x1, blocking collectives, exchange(): lax.all_to_all(block.reshape(experts, SUB, main), ('outer', 'inner'), spl...  125 us
    all_to_all x1, waiting for transfers between devices, exchange(): lax.all_to_all(block.reshape(experts, SUB, main), ('outer', 'inner'), spl...  106 us
    pallas_call x1, Pallas kernels, on_device(): pl.pallas_call(functools.partial(expert_kernel, (part, slots, cap, hidden...  22 us
    all_to_all x1, starting transfers between devices, exchange(): lax.all_to_all(block.reshape(experts, SUB, main), ('outer', 'inner'), spl...  7.34 us
    pallas_call x1, Pallas kernels, on_device(): pl.pallas_call(functools.partial(combine_kernel, (experts, tok, main, wid...  5.73 us
  transfers between devices with their start and end apart: 2, of which 2 were waited for; matrix products, arithmetic and copies ran while one was open for 0% of the time, Pallas kernels for 0%

profile of v1, /device:TPU:1, one launch (start us, length us, event | category | flops | bytes accessed | tf_op | source)
XLA Modules:
  0.0 280.0 jit_solution(812526165120573585)
XLA Ops:
  0.6 0.7 copy.13
  1.3 0.7 copy.12
  2.0 0.0 copy-start.3
  2.0 1.1 copy-done.3
  3.1 0.0 copy-start.2
  3.1 3.0 %dispatch.1 = (bf16[1024,2304]{1,0:T(8,128)(2,1)S(1)}, f32[128,128]{1,0:T(8,128)S(1)}) custom-call(s32[6,128]{1,0:T(8,128)S(1)} %bitcast.21, f32[6,128]{1,0:T(8,128)S(1)} %bitcast.23, bf16[128,2560]{1,0:T(8,128)(2,1)S(1)} %bitcast.27), custom_call_target="tpu_custom_call" | custom-call | flops 1207959552 | bytes 4718592 | tf_op jit(solution)/shard_map/dispatch/pallas_call | solution.py:195
  6.1 0.0 copy-start
  6.2 0.0 copy-start.1
  6.2 125.1 %all_to_all.10 = bf16[128,8,2304]{2,1,0:T(8,128)(2,1)} all-to-all(bf16[128,8,2304]{2,1,0:T(8,128)(2,1)S(1)} %bitcast.20), channel_id=1, replica_groups=mesh['outer'=16,'inner'=8,'section'=2] {'outer','inner'}, dimensions={0} | all-to-all | bytes 9437184 | tf_op jit(solution)/shard_map/all_to_all | solution.py:227
  131.3 0.0 copy-done.2
  131.3 0.0 copy-done
  131.3 0.0 copy-done.1
  131.3 22.0 %expert.1 = (bf16[1024,2304]{1,0:T(8,128)(2,1)}, bf16[896,768]{1,0:T(8,128)(2,1)}) custom-call(bf16[1024,2304]{1,0:T(8,128)(2,1)} %bitcast.29, bf16[896,1536]{1,0:T(8,128)(2,1)S(1)} %bitcast.26, bf16[768,2560]{1,0:T(8,128)(2,1)S(1)} %bitcast.24, bf16[2560,768]{1,0:T(8,128)(2,1)S(1)} %bitcast.25), custom_call_target="tpu_custom_call" | custom-call | flops 8053063680 | bytes 17301504 | tf_op jit(solution)/shard_map/expert/pallas_call | solution.py:237
  153.3 7.3 %all-to-all-start.1 = ((bf16[128,8,2304]{2,1,0:T(8,128)(2,1)}), bf16[128,8,2304]{2,1,0:T(8,128)(2,1)}, u32[]{:S(2)}, u32[]{:S(2)}) async-start(bf16[128,8,2304]{2,1,0:T(8,128)(2,1)} %bitcast.28), calls=%async_computation.1 | async-start | bytes 9437184 | tf_op jit(solution)/shard_map/all_to_all | solution.py:227
  160.6 0.5 picks.1
  161.1 105.8 %all-to-all-done.1 = bf16[128,8,2304]{2,1,0:T(8,128)(2,1)} async-done(((bf16[128,8,2304]{2,1,0:T(8,128)(2,1)}), bf16[128,8,2304]{2,1,0:T(8,128)(2,1)}, u32[]{:S(2)}, u32[]{:S(2)}) %all-to-all-start.1) | async-done | bytes 4718624 | tf_op jit(solution)/shard_map/all_to_all | solution.py:227
  266.9 5.7 %combine.1 = bf16[128,2560]{1,0:T(8,128)(2,1)S(1)} custom-call(bf16[384,1024]{1,0:T(8,128)(2,1)S(1)} %get-tuple-element.9.pick_ref, bf16[9,384,128]{2,1,0:T(8,128)(2,1)S(1)} %get-tuple-element.10.pick_tail_ref, bf16[1024,2304]{1,0:T(8,128)(2,1)} %bitcast.9.back_ref), custom_call_target="tpu_custom_call" | custom-call | flops 1811939328 | bytes 4718592 | tf_op jit(solution)/shard_map/combine/pallas_call | solution.py:262
  272.7 4.8 %collective-permute-start = (bf16[128,2560]{1,0:T(8,128)(2,1)S(1)}, bf16[128,2560]{1,0:T(8,128)(2,1)S(1)}, u32[]{:S(2)}, u32[]{:S(2)}) collective-permute-start(bf16[128,2560]{1,0:T(8,128)(2,1)S(1)} %combine.1), channel_id=1, source_target_pairs={{1,0},{0,1},{3,2},{2,3},{5,4},{4,5},{7,6},{6,7},{9,8},{8,9},{11,10... | collective-permute-start | bytes 1966088 | tf_op jit(solution)/shard_map/ppermute | solution.py:278
  277.5 1.7 collective-permute-done
  279.2 0.8 copy.15
Async XLA Ops:
  2.0 1.1 copy-start.3
  3.1 128.2 %copy-start.2 = (bf16[1,1,896,1536]{3,2,1,0:T(8,128)(2,1)S(1)}, bf16[1,1,896,1536]{3,2,1,0:T(8,128)(2,1)}, u32[]{:S(2)}) copy-start(bf16[1,1,896,1536]{3,2,1,0:T(8,128)(2,1)} %param.9) | copy-start | bytes 8257540
  6.1 125.2 %copy-start = (bf16[1,1,768,2560]{3,2,1,0:T(8,128)(2,1)S(1)}, bf16[1,1,768,2560]{3,2,1,0:T(8,128)(2,1)}, u32[]{:S(2)}) copy-start(bf16[1,1,768,2560]{3,2,1,0:T(8,128)(2,1)} %param.11) | copy-start | bytes 11796484
  6.2 125.2 %copy-start.1 = (bf16[1,1,2560,768]{3,2,1,0:T(8,128)(2,1)S(1)}, bf16[1,1,2560,768]{3,2,1,0:T(8,128)(2,1)}, u32[]{:S(2)}) copy-start(bf16[1,1,2560,768]{3,2,1,0:T(8,128)(2,1)} %param.10) | copy-start | bytes 11796484
  153.3 113.7 %all-to-all-start.1 = ((bf16[128,8,2304]{2,1,0:T(8,128)(2,1)}), bf16[128,8,2304]{2,1,0:T(8,128)(2,1)}, u32[]{:S(2)}, u32[]{:S(2)}) async-start(bf16[128,8,2304]{2,1,0:T(8,128)(2,1)} %bitcast.28), calls=%async_computation.1 | async-start | bytes 9437184 | tf_op jit(solution)/shard_map/all_to_all | solution.py:227
  272.7 6.5 %collective-permute-start = (bf16[128,2560]{1,0:T(8,128)(2,1)S(1)}, bf16[128,2560]{1,0:T(8,128)(2,1)S(1)}, u32[]{:S(2)}, u32[]{:S(2)}) collective-permute-start(bf16[128,2560]{1,0:T(8,128)(2,1)S(1)} %combine.1), channel_id=1, source_target_pairs={{1,0},{0,1},{3,2},{2,3},{5,4},{4,5},{7,6},{6,7},{9,8},{8,9},{11,10... | collective-permute-start | bytes 1966088 | tf_op jit(solution)/shard_map/ppermute | solution.py:278

commit v2 on v0

v2 whole, which is shorter than its diff:
```python
import functools
import jax
import jax.numpy as jnp
from jax import lax
from jax.experimental import pallas as pl
from jax.experimental.pallas import tpu as pltpu
from jax.sharding import PartitionSpec as P

NZ, NY, NX = 8, 4, 4
ROUTE_GROUPS = 3
SUB = 8
SLABS = 3
FIELDS = 128
BLOCKS = 16
F32 = jnp.float32
BF16 = jnp.bfloat16
I32 = jnp.int32


def iota(shape, dim):
    return lax.broadcasted_iota(I32, shape, dim)


def dot(a, b):
    return lax.dot_general(a, b, (((1,), (0,)), ((), ())), preferred_element_type=F32)


def dot_t(a, b):
    return lax.dot_general(a, b, (((1,), (1,)), ((), ())), preferred_element_type=F32)


def t_dot(a, b):
    return lax.dot_general(a, b, (((0,), (0,)), ((), ())), preferred_element_type=F32)


def flag(mask, kind=BF16):
    return jnp.where(mask, 1.0, 0.0).astype(kind)


def over(value, divisor):
    return jnp.floor((value.astype(F32) + 0.5) * (1.0 / divisor)).astype(I32)


def top_bits(value):
    wide = value * 65537.0
    return wide - (wide - value)


def block_group(where_ref, block):
    odd, even, mid, far, y = (where_ref[i] for i in range(5))
    z = jnp.where(block < 4, odd, jnp.where(block < 8, even, jnp.where(block < 12, mid, far)))
    return (z // 2) * NY + jnp.where(block < 8, block % NY, (block + y) % NY)


def slots_in_group(member, group_cap):
    tok = member.shape[1]
    before = flag(iota((tok, tok), 0) < iota((tok, tok), 1))
    rank = dot(member.astype(BF16), before)
    return jnp.where((member > 0) & (rank < group_cap), rank, -1.0)


def token_lines(where_ref, group_slot):
    groups, tok = group_slot.shape
    rows = (SLABS + 1) * BLOCKS * SUB
    r = iota((rows, groups), 0)
    chosen = flag(block_group(where_ref, (r // SUB) % BLOCKS) == iota((rows, groups), 1))
    r = iota((rows, tok), 0)
    slab, sub = r // (BLOCKS * SUB), r % SUB
    slot = jnp.where(slab == SLABS, SLABS * SUB + sub % 4, slab * SUB + sub)
    return flag(dot(chosen, group_slot.astype(BF16)) == slot.astype(F32))


def half_rows(value, second):
    sub = iota(value.shape, 0) % SUB
    return jnp.where(sub >= 4 if second else sub < 4, value, jnp.zeros_like(value))


def half_right(block_ref, second):
    features = block_ref.shape[1] // (2 * SLABS + 1) // FIELDS * FIELDS * 2
    half, tail = features // 2, SLABS * features
    c = half if second else 0
    last = half_rows(block_ref[:, tail : tail + half].astype(F32), second).astype(BF16)
    return jnp.concatenate([*(block_ref[:, n * features + c : n * features + c + half] for n in range(SLABS)), last], axis=0)


def lines_kernel(dims, where_ref, ids_ref, line_ref):
    groups, in_group, group_cap = dims
    routes, _, tok = ids_ref.shape
    member = jnp.zeros((groups, tok), F32)
    for k in range(0, routes, routes // ROUTE_GROUPS):
        member += flag(ids_ref[k] // in_group == iota((groups, tok), 0), F32)
    line_ref[...] = token_lines(where_ref, slots_in_group(member, group_cap))


def put_blocks(block_refs, value, start):
    value, row = value.astype(BF16), 0
    for ref in block_refs:
        ref[:, start : start + value.shape[1]] = value[row : row + ref.shape[0]]
        row += ref.shape[0]


def stack_blocks(block_refs, stacked_ref):
    width, row, first = stacked_ref.shape[1], 0, None
    for ref in block_refs:
        if ref.shape[0] > SUB:
            stacked_ref[row : row + ref.shape[0], :] = ref[:, :width]
            row += ref.shape[0]
        elif first is None:
            first = ref
        else:
            pair = jnp.concatenate([first[:, :width].astype(F32), ref[:, :width].astype(F32)], axis=0)
            stacked_ref[row : row + 2 * SUB, :] = pair.astype(BF16)
            row, first = row + 2 * SUB, None


def dispatch_kernel(dims, where_ref, ids_ref, w_ref, g_ref, *block_refs):
    groups, in_group, group_cap, cap = dims
    routes, _, tok = ids_ref.shape
    features, experts = g_ref.shape[1], groups * in_group
    half, per = features // 2, routes // ROUTE_GROUPS
    e, group = iota((experts, tok), 0), iota((groups, tok), 0)
    before = flag(iota((tok, tok), 0) < iota((tok, tok), 1))
    ids = [ids_ref[k] for k in range(routes)]
    named = jnp.zeros((experts, tok), F32)
    mine = jnp.zeros((experts, tok), F32)
    member = jnp.zeros((groups, tok), F32)
    for k in range(routes):
        named += flag(ids[k] == e, F32)
        if k % per == 0:
            mine += flag(ids[k] // in_group == e // in_group, F32)
            member += flag(ids[k] // in_group == group, F32)
    admitted = (named > 0) & (dot(mine.astype(BF16), before) < group_cap)
    slot_rank = dot(flag(admitted), before)
    rank = jnp.where(admitted & (slot_rank < cap), slot_rank, -1.0)
    group_slot = slots_in_group(member, group_cap)
    fields = [jnp.zeros((groups, tok), F32) for _ in range(SUB)]
    for k in range(routes):
        own = jnp.sum(jnp.where(ids[k] == e, rank, 0.0), axis=0, keepdims=True)
        place = jnp.where(own >= 0, (ids[k] % in_group).astype(F32) * cap + own + 1.0, 0.0)
        weight = w_ref[k]
        first = top_bits(weight)
        second = top_bits(weight - first)
        third = (weight - first) - second
        at = ids[k] // in_group == group
        for f, value in ((k % per, place), *((per + 3 * (k % per) + i, v) for i, v in enumerate((first, second, third)))):
            fields[f] += jnp.where(at, value, 0.0)
    stacked = jnp.concatenate([f.astype(BF16) for f in fields], axis=0)
    line = token_lines(where_ref, group_slot)
    rows, part = line.shape[0], groups * SUB
    r, c = iota((part, part), 0), iota((part, part), 1)
    choose = flag((block_group(where_ref, r // SUB) == c % groups) & (r % SUB == c // groups))
    by_block = dot(choose, stacked).astype(BF16)
    by_slot = dot_t(by_block, line)
    r, c = iota((part, rows), 0), iota((part, rows), 1)
    by_slot = jnp.where((c // SUB) % groups == r // SUB, by_slot, 0.0).astype(BF16)
    r, c = iota((rows, FIELDS), 0), iota((rows, FIELDS), 1)
    fold = flag(c == (r // part) * SUB + r % SUB)
    block_fields = dot(by_slot, fold)

    def put(value, start, width):
        put_blocks(block_refs, value, start)

    for n in range(SLABS):
        for c in (0, half):
            put(dot(line[n * part : (n + 1) * part], g_ref[:, c : c + half]), n * features + c, half)
    line = line[SLABS * part :]
    put(
        half_rows(dot(line, g_ref[:, :half]), False) + half_rows(dot(line, g_ref[:, half:]), True),
        SLABS * features, half,
    )
    put(block_fields, SLABS * features + half, FIELDS)


def spread_kernel(dims, *refs):
    *block_refs, out_hbm, hit_ref, block_ref, out_ref, sems = refs
    stack_blocks(block_refs, block_ref)
    in_group, cap = dims
    height, features = block_ref.shape[0], out_ref.shape[1]
    sources = height // SUB
    half, tail = features // 2, SLABS * features

    deep = (SLABS + 1) * height
    l, c = iota((FIELDS, deep), 0), iota((FIELDS, deep), 1)
    unfold = flag((l == (c // height) * SUB + c % SUB) & (l < (SLABS + 1) * SUB))
    wide = dot(block_ref[:, tail + half :], unfold)
    r, c = iota((height, deep), 0), iota((height, deep), 1)
    wide = jnp.where(r // SUB == (c // SUB) % sources, wide, 0.0)
    fields = wide[:SUB]
    for q in range(1, sources):
        fields += wide[q * SUB : (q + 1) * SUB]
    places = [fields[k : k + 1].astype(I32) for k in range(2)]
    weights = [(fields[2 + 3 * k : 3 + 3 * k] + fields[3 + 3 * k : 4 + 3 * k]) + fields[4 + 3 * k : 5 + 3 * k] for k in range(2)]
    rows = out_ref.shape[0]
    s = iota((rows, 1), 0)
    each = rows // in_group
    expert = over(s, each)
    inside = s - expert * each
    source = over(inside, cap)
    key = source * 64 + expert * cap + (inside - source * cap) + 1
    key = jnp.where(source < sources, key, -2)
    c = iota((1, deep), 1)
    base = ((c // SUB) % sources) * 64
    hits = [key == jnp.where(place > 0, base + place, -1) for place in places]
    once = iota((1, deep), 1)
    once = (once < SLABS * height) | (once % SUB < 4)
    hit_ref[...] = flag(hits[0] | hits[1])
    scale = jnp.where(hits[0], jnp.where(once, weights[0], 0.0), 0.0)
    scale += jnp.where(hits[1], jnp.where(once, weights[1], 0.0), 0.0)
    scale = jnp.sum(scale, axis=1, keepdims=True)
    copies = []
    for c in (0, half):
        out_ref[:, c : c + half] = (dot(hit_ref[...], half_right(block_ref, c > 0)) * scale).astype(BF16)
        copies.append(
            pltpu.make_async_copy(out_ref.at[:, pl.ds(c, half)], out_hbm.at[:, pl.ds(c, half)], sems.at[c // half])
        )
        copies[-1].start()
    for copy in copies:
        copy.wait()


def gather_kernel(rows_hbm, hit_ref, *refs):
    *block_refs, rows_ref, sems = refs
    features, height = rows_ref.shape[1], hit_ref.shape[1] // (SLABS + 1)
    half = features // 2
    copies = [
        pltpu.make_async_copy(rows_hbm.at[:, pl.ds(c, half)], rows_ref.at[:, pl.ds(c, half)], sems.at[c // half])
        for c in (0, half)
    ]
    for copy in copies:
        copy.start()
    tail = jnp.zeros((height, half), F32)
    for copy, c in zip(copies, (0, half), strict=True):
        copy.wait()
        got = t_dot(hit_ref[...], rows_ref[:, c : c + half])
        for n in range(SLABS):
            put_blocks(block_refs, got[n * height : (n + 1) * height], n * features + c)
        tail += half_rows(got[SLABS * height :], c > 0)
    put_blocks(block_refs, tail, SLABS * features)


def combine_kernel(*refs):
    *block_refs, line_ref, out_ref, block_ref = refs
    stack_blocks(block_refs, block_ref)
    half = out_ref.shape[1] // 2
    for c in (0, half):
        out_ref[:, c : c + half] = t_dot(line_ref[...], half_right(block_ref, c > 0)).astype(BF16)


def true_rows(where_ref, row, part, each, cap):
    y, z_hi = where_ref[4], where_ref[5]
    sender = over(row, each)
    inside = row - sender * each
    q = over(inside, cap)
    slot = inside - q * cap
    z = z_hi * 2 + sender % 2
    up = jnp.where(sender % 2 == 1, 1, -1)
    if part == 0:
        sources = 12
        odd = jnp.where(sender % 2 == 1, z, z - 1)
        z = jnp.where(q < 4, odd, jnp.where(q < 8, odd + 1, z + 2 * up))
        at_y = jnp.where(q < 8, q, y - q + 4 * NY)
    else:
        sources = 4
        z = z + 3 * up
        at_y = y - q + 4 * NY
    z = (z + NZ) % NZ
    source = (((z // 2) * NY + at_y % NY) * NX + sender // 2) * 2 + z % 2
    return jnp.where(q < sources, source * cap + slot, -1)


def align_kernel(dims, where_ref, saved_ref, *part_refs):
    in_group, cap = dims
    slots = saved_ref.shape[0]
    for part, ref in enumerate(part_refs):
        rows = ref.shape[0]
        true = true_rows(where_ref, iota((rows, 1), 0), part, rows // in_group, cap)
        ref[...] = dot(flag(true == iota((rows, slots), 1)), saved_ref[...]).astype(BF16)


def restore_kernel(dims, where_ref, *refs):
    in_group, cap = dims
    *part_refs, out_ref = refs
    slots = out_ref.shape[0]
    total = jnp.zeros(out_ref.shape, F32)
    for part, ref in enumerate(part_refs):
        rows = ref.shape[0]
        true = true_rows(where_ref, iota((1, rows), 1), part, rows // in_group, cap)
        total += dot(flag(true == iota((slots, rows), 0)), ref[...])
    out_ref[...] = total.astype(BF16)


def expert_kernel(x_hbm, kept_hbm, wd_hbm, wu_hbm, out_hbm, gate_hbm, x_ref, kept_ref, wd_ref, wu_ref, up_ref, out_ref, gate_ref, sems):
    hidden, features = wd_ref.shape
    rows = x_ref.shape[0]
    step, wide, tall = hidden // 3, features // 5, rows // 2 if rows > 256 else rows
    count = iter(range(sems.shape[0]))

    def copy(source, target, index):
        return pltpu.make_async_copy(source.at[index], target.at[index], sems.at[next(count)])

    tops = [pl.ds(r, tall) for r in range(0, rows, tall)]
    x = [copy(x_hbm, x_ref, t) for t in tops]
    kept = [copy(kept_hbm, kept_ref, t) for t in tops]
    down = [copy(wd_hbm, wd_ref, pl.ds(n, step)) for n in range(0, hidden, step)]
    up = [copy(wu_hbm, wu_ref, pl.ds(n, wide)) for n in range(0, features, wide)]
    for c in (x[0], down[0], kept[0], *down[1:], *x[1:], *kept[1:], *up):
        c.start()
    out = []
    for i, r in enumerate(range(0, rows, tall)):
        x[i].wait()
        for j, n in enumerate(range(0, hidden, step)):
            if i == 0:
                down[j].wait()
            grad = dot_t(x_ref[r : r + tall, :], wd_ref[n : n + step, :])
            if j == 0:
                kept[i].wait()
            act = kept_ref[r : r + tall, n : n + step].astype(F32)
            up_ref[r : r + tall, n : n + step] = (grad * act).astype(BF16)
            value = kept_ref[r : r + tall, hidden + n : hidden + n + step].astype(F32)
            gate_ref[r : r + tall, n : n + step] = (grad * value).astype(BF16)
        out.append(copy(gate_ref, gate_hbm, tops[i]))
        out[-1].start()
    for i, n in enumerate(range(0, features, wide)):
        up[i].wait()
        out_ref[:, n : n + wide] = dot_t(up_ref[...], wu_ref[n : n + wide, :]).astype(BF16)
        out.append(copy(out_ref, out_hbm, (slice(None), pl.ds(n, wide))))
        out[-1].start()
    for c in out:
        c.wait()


def device_at(z, y, x):
    return (((z // 2) % (NZ // 2) * NY + y % NY) * NX + x) * 2 + z % 2


PAIR_SETS = [
    [device_at(z % NZ, y, x) for z in (odd, odd + 1) for y in range(NY)]
    for x in range(NX)
    for odd in range(1, NZ, 2)
]


def routes_over(hops, dy, back):
    pairs = []
    for z in range(NZ):
        to = (z + (hops if (z % 2 == 1) == (hops == 3) else -hops)) % NZ
        pairs += [(device_at(z, y, x), device_at(to, y + dy, x)) for y in range(NY) for x in range(NX)]
    return [(b, a) for a, b in pairs] if back else pairs


def on_device(grad_out, route_ids, route_w, saved, w_up, w_down):
    both = ("outer", "inner")
    groups, in_group = lax.axis_size("outer"), lax.axis_size("inner")
    tok, features = grad_out.shape[1:]
    routes = route_ids.shape[2]
    slots_all = saved.shape[2]
    cap = slots_all // (groups * in_group)
    hidden = w_up.shape[3]
    group_cap = max(2, 7 * tok * ROUTE_GROUPS // (6 * groups))
    wide = SLABS * features + features // 2
    sent = wide + FIELDS
    deep = (SLABS + 1) * BLOCKS * SUB
    heights = [in_group * -(-(sources * cap) // SUB) * SUB for sources in (12, 4)]
    outer, inner = lax.axis_index("outer"), lax.axis_index("inner")
    z_hi, y, z_lo = outer // NY, outer % NY, inner % 2
    z = z_hi * 2 + z_lo
    up = 2 * z_lo - 1
    odd = (z + z_lo - 1) % NZ
    where = jnp.stack([odd, (odd + 1) % NZ, (z - 2 * up) % NZ, (z + 3 * up) % NZ, y, z_hi]).astype(I32)
    vmem, hbm = pl.BlockSpec(memory_space=pltpu.VMEM), pl.BlockSpec(memory_space=pltpu.HBM)
    smem = pl.BlockSpec(memory_space=pltpu.SMEM)

    def array(*shape):
        return jax.ShapeDtypeStruct(shape, BF16)

    def call(kernel, name, n_in, outs, mib, flops, out_specs=None, scratch=(), scalars=True):
        moved = 2 * sum(functools.reduce(lambda a, b: a * b, o.shape) for o in outs)
        return pl.pallas_call(
            kernel,
            name=name,
            in_specs=[smem] * scalars + [vmem] * n_in,
            out_specs=out_specs or [vmem] * len(outs),
            out_shape=list(outs),
            scratch_shapes=list(scratch),
            compiler_params=pltpu.CompilerParams(vmem_limit_bytes=mib * 2**20),
            cost_estimate=pl.CostEstimate(flops=flops, bytes_accessed=moved, transcendentals=0),
        )

    def near_swap(block):
        width = block.shape[1]
        moved = lax.all_to_all(block.reshape(8, SUB, width), both, 0, 0, axis_index_groups=PAIR_SETS, tiled=True)
        return moved.reshape(8 * SUB, width)

    def hop(blocks, hops, back=False):
        return [lax.ppermute(b, both, routes_over(hops, dy, back)) for dy, b in enumerate(blocks)]

    def in_groups(rows):
        moved = lax.all_to_all(rows.reshape(in_group, -1, features), "inner", 0, 0, tiled=True)
        return moved.reshape(rows.shape)

    def spread(name, blocks, rows):
        height = sum(b.shape[0] for b in blocks)
        depth = (SLABS + 1) * height
        return call(
            functools.partial(spread_kernel, (in_group, cap)), name, len(blocks),
            [array(rows, features), array(rows, depth)], 48, 2 * rows * depth * features,
            [hbm, vmem],
            [pltpu.VMEM((height, sent), BF16), pltpu.VMEM((rows, features), BF16), pltpu.SemaphoreType.DMA((2,))],
            scalars=False,
        )(*blocks)

    def gather(name, rows, hit, shapes):
        return pl.pallas_call(
            gather_kernel,
            name=name,
            in_specs=[hbm, vmem],
            out_specs=[vmem] * len(shapes),
            out_shape=[array(h, wide) for h in shapes],
            scratch_shapes=[pltpu.VMEM(rows.shape, BF16), pltpu.SemaphoreType.DMA((2,))],
            compiler_params=pltpu.CompilerParams(vmem_limit_bytes=20 * 2**20),
            cost_estimate=pl.CostEstimate(
                flops=2 * hit.shape[0] * hit.shape[1] * features, bytes_accessed=2 * rows.shape[0] * features, transcendentals=0
            ),
        )(rows, hit)

    def after(first, *values):
        *values, first = lax.optimization_barrier((*values, first))
        return first, *values

    ids = route_ids[0].T.reshape(routes, 1, tok)
    shapes = [8 * SUB] + [SUB] * 8
    near, *others = call(
        functools.partial(dispatch_kernel, (groups, in_group, group_cap, cap)), "dispatch", 3,
        [array(h, sent) for h in shapes], 12, 2 * deep * tok * features,
    )(where, ids, route_w[0].T.reshape(routes, 1, tok), grad_out[0])
    [line] = call(
        functools.partial(lines_kernel, (groups, in_group, group_cap)), "lines", 1,
        [array(deep, tok)], 8, 4 * deep * tok * tok,
    )(where, ids)
    kept = call(
        functools.partial(align_kernel, (in_group, cap)), "align", 1, [array(h, 2 * hidden) for h in heights], 16,
        4 * sum(heights) * slots_all * hidden,
    )(where, saved[0, 0])

    near, mid, far = near_swap(near), hop(others[:4], 2), others[4:]
    near, *ready = after(near, *mid, *far)
    mid, far = ready[:4], hop(ready[4:], 3)
    rows_n, hit_n = spread("spread_near", [near, *mid], heights[0])
    rows_n = in_groups(rows_n)
    rows_f, hit_f = spread("spread_far", far, heights[1])
    rows_n, rows_f = after(rows_n, rows_f)
    rows_f = in_groups(rows_f)
    rows_n, gate_n = expert_call("expert_near", rows_n, kept[0], w_down[0, 0], w_up[0, 0])
    rows_f, gate_f = expert_call("expert_far", rows_f, kept[1], w_down[0, 0], w_up[0, 0])
    rows_f = in_groups(rows_f)
    far = gather("gather_far", rows_f, hit_f, [SUB] * 4)
    rows_n, *far = after(rows_n, *far)
    far = hop(far, 3, True)
    rows_n = in_groups(rows_n)
    rows_n, *far = after(rows_n, *far)
    [gate_grad] = call(
        functools.partial(restore_kernel, (in_group, cap)), "restore", 2, [array(slots_all, hidden)], 12,
        2 * sum(heights) * slots_all * hidden,
    )(where, gate_n, gate_f)
    near, *mid = gather("gather_near", rows_n, hit_n, [8 * SUB] + [SUB] * 4)
    near, mid = near_swap(near), hop(mid, 2, True)
    gate_grad, line = after(gate_grad, line)
    [token_grad] = call(
        combine_kernel, "combine", 10, [array(tok, features)], 12, 2 * deep * tok * features,
        scratch=[pltpu.VMEM((BLOCKS * SUB, wide), BF16)], scalars=False,
    )(near, *mid, *far, line)
    count = lax.axis_size("section")
    received = lax.ppermute(token_grad, "section", [((i + 1) % count, i) for i in range(count)])
    return (received[None], gate_grad[None, None])


def expert_call(name, rows, kept, w_down, w_up):
    hidden, features = w_down.shape
    height = rows.shape[0]
    hbm = pl.BlockSpec(memory_space=pltpu.HBM)
    return pl.pallas_call(
        expert_kernel,
        name=name,
        in_specs=[hbm] * 4,
        out_specs=[hbm] * 2,
        out_shape=[jax.ShapeDtypeStruct((height, features), BF16), jax.ShapeDtypeStruct((height, hidden), BF16)],
        scratch_shapes=[
            pltpu.VMEM((height, features), BF16),
            pltpu.VMEM((height, 2 * hidden), BF16),
            pltpu.VMEM((hidden, features), BF16),
            pltpu.VMEM((features, hidden), BF16),
            pltpu.VMEM((height, hidden), BF16),
            pltpu.VMEM((height, features), BF16),
            pltpu.VMEM((height, hidden), BF16),
            pltpu.SemaphoreType.DMA((19,)),
        ],
        compiler_params=pltpu.CompilerParams(vmem_limit_bytes=56 * 2**20),
        cost_estimate=pl.CostEstimate(
            flops=4 * height * features * hidden, bytes_accessed=4 * (height + hidden) * features, transcendentals=0
        ),
    )(rows, kept, w_down, w_up)


def solution(mesh):
    return jax.shard_map(
        on_device,
        mesh=mesh,
        in_specs=(
            P("section", ("outer", "inner"), None),
            P("section", ("outer", "inner"), None),
            P("section", ("outer", "inner"), None),
            P("section", ("outer", "inner"), None, None),
            P("section", ("outer", "inner"), None, None),
            P("section", ("outer", "inner"), None, None),
        ),
        out_specs=(
            P("section", ("outer", "inner"), None),
            P("section", ("outer", "inner"), None, None),
        ),
        check_vma=False,
    )
```

time: 370 us -> 264 us (0.71)
  blocking collectives: 136 us -> 0 us
  starting transfers between devices: 12.4 us -> 91.8 us
  local copies, waits for them, and re-layouts: 73.2 us -> 12.3 us
  Pallas kernels: 0 us -> 43.4 us
  other arithmetic: 16.6 us -> 0 us
  matrix products: 12.4 us -> 0 us
    all_to_all x1 -> x0, blocking collectives: 136 us -> none  [on_device(): lax.all_to_all(outgoing.reshape(experts, capacity, features), ('outer', '...]
    all_to_all x1 -> x6, waiting for transfers between devices: 117 us -> 66.3 us  [the longest x4 57.8 us: in_groups(): lax.all_to_all(rows.reshape(in_group, -1, features), 'inner', 0, 0, tiled...]
    ppermute x1 -> x17, starting transfers between devices: 4.85 us -> 54 us  [the longest x16 52 us: hop(): lax.ppermute(b, both, routes_over(hops, dy, back))]
    ppermute x1 -> x17, waiting for transfers between devices: 0.01 us -> 48.2 us  [the longest x16 46.5 us: hop(): lax.ppermute(b, both, routes_over(hops, dy, back))]
    pallas_call x0 -> x11, Pallas kernels: none -> 43.4 us  [the longest x2 20.1 us: expert_call(): pl.pallas_call(expert_kernel, name=name, in_specs=[hbm] * 4, out_specs=[h...]
    reshape x4 -> x2, local copies, waits for them, and re-layouts: 31.2 us -> 0.01 us  [the longest x1 0.01 us: on_device(): ids = route_ids[0].T.reshape(routes, 1, tok)]
    all_to_all x1 -> x6, starting transfers between devices: 7.53 us -> 37.8 us  [the longest x2 21.4 us: near_swap(): lax.all_to_all(block.reshape(8, SUB, width), both, 0, 0, axis_index_group...]
    gather x3 -> x0, local copies, waits for them, and re-layouts: 20.3 us -> none  [the longest x1 11.3 us: on_device(): padded_back[slot_index].reshape(tok_rows, route_groups, per_group, features)]
  transfers between devices with their start and end apart: 2 -> 23, of which waited for: 1 -> 18; matrix products, arithmetic and copies ran while one was open for 1% -> 0% of each run, Pallas kernels for 0% -> 9%
where the time goes in v2:
time: 264 us; the launch traced here: 263 us
  waiting for transfers between devices  115 us (44%)
  starting transfers between devices  91.8 us (35%)
  Pallas kernels  43.4 us (16%)
  local copies, waits for them, and re-layouts  12.3 us (5%)
    all_to_all x4, waiting for transfers between devices, in_groups(): lax.all_to_all(rows.reshape(in_group, -1, features), 'inner', 0, 0, tiled...  57.8 us
    ppermute x16, starting transfers between devices, hop(): lax.ppermute(b, both, routes_over(hops, dy, back))  52 us
    ppermute x16, waiting for transfers between devices, hop(): lax.ppermute(b, both, routes_over(hops, dy, back))  46.5 us
    all_to_all x2, starting transfers between devices, near_swap(): lax.all_to_all(block.reshape(8, SUB, width), both, 0, 0, axis_index_group...  21.4 us
    pallas_call x2, Pallas kernels, expert_call(): pl.pallas_call(expert_kernel, name=name, in_specs=[hbm] * 4, out_specs=[h...  20.1 us
    all_to_all x4, starting transfers between devices, in_groups(): lax.all_to_all(rows.reshape(in_group, -1, features), 'inner', 0, 0, tiled...  16.4 us
    unnamed x23, local copies, waits for them, and re-layouts  12.2 us
    all_to_all x2, waiting for transfers between devices, near_swap(): lax.all_to_all(block.reshape(8, SUB, width), both, 0, 0, axis_index_group...  8.49 us
  transfers between devices with their start and end apart: 23, of which 18 were waited for; matrix products, arithmetic and copies ran while one was open for 0% of the time, Pallas kernels for 9%

profile of v2, /device:TPU:1, one launch (start us, length us, event | category | flops | bytes accessed | tf_op | source)
XLA Modules:
  0.0 262.9 jit_solution(4675432345051197800)
XLA Ops:
  6.3 10.6 %all-to-all-start = ((bf16[8,8,9088]{2,1,0:T(8,128)(2,1)}), bf16[8,8,9088]{2,1,0:T(8,128)(2,1)S(1)}, u32[]{:S(2)}, u32[]{:S(2)}) async-start(bf16[8,8,9088]{2,1,0:T(8,128)(2,1)} %bitcast.9), calls=%async_computation | async-start | bytes 2326528 | tf_op jit(solution)/shard_map/all_to_all | solution.py:391
  16.9 4.9 %collective-permute-start.1 = (bf16[8,9088]{1,0:T(8,128)(2,1)S(1)}, bf16[8,9088]{1,0:T(8,128)(2,1)S(1)}, u32[]{:S(2)}, u32[]{:S(2)}) collective-permute-start(bf16[8,9088]{1,0:T(8,128)(2,1)S(1)} %get-tuple-element.54), channel_id=1, source_target_pairs={{0,80},{4,84},{8,88},{12,92},{16,96},{20,100},{24,104},{28,108},{3... | collective-permute-start | bytes 436232 | tf_op jit(solution)/shard_map/ppermute | solution.py:395
  28.2 4.1 %collective-permute-done.2.refs_3_ = bf16[8,9088]{1,0:T(8,128)(2,1)S(1)} collective-permute-done((bf16[8,9088]{1,0:T(8,128)(2,1)S(1)}, bf16[8,9088]{1,0:T(8,128)(2,1)S(1)}, u32[]{:S(2)}, u32[]{:S(2)}) %collective-permute-start.2) | collective-permute-done | bytes 145440 | tf_op jit(solution)/shard_map/ppermute | solution.py:395
  33.7 8.5 %all-to-all-done = bf16[8,8,9088]{2,1,0:T(8,128)(2,1)S(1)} async-done(((bf16[8,8,9088]{2,1,0:T(8,128)(2,1)}), bf16[8,8,9088]{2,1,0:T(8,128)(2,1)S(1)}, u32[]{:S(2)}, u32[]{:S(2)}) %all-to-all-start) | async-done | bytes 1163296 | tf_op jit(solution)/shard_map/all_to_all | solution.py:391
  48.1 4.5 %all-to-all-start.1 = ((bf16[8,88,2560]{2,1,0:T(8,128)(2,1)}), bf16[8,88,2560]{2,1,0:T(8,128)(2,1)}, u32[]{:S(2)}, u32[]{:S(2)}) async-start(bf16[8,88,2560]{2,1,0:T(8,128)(2,1)} %bitcast.36), calls=%async_computation.1 | async-start | bytes 7208960 | tf_op jit(solution)/shard_map/all_to_all | solution.py:398
  52.6 4.4 %collective-permute-start.4 = (bf16[8,9088]{1,0:T(8,128)(2,1)S(1)}, bf16[8,9088]{1,0:T(8,128)(2,1)S(1)}, u32[]{:S(2)}, u32[]{:S(2)}) collective-permute-start(bf16[8,9088]{1,0:T(8,128)(2,1)S(1)} %get-tuple-element.62), channel_id=1, source_target_pairs={{0,130},{4,134},{8,138},{12,142},{16,146},{20,150},{24,154},{28,15... | collective-permute-start | bytes 436232 | tf_op jit(solution)/shard_map/ppermute | solution.py:395
  58.1 5.8 %collective-permute-start.6 = (bf16[8,9088]{1,0:T(8,128)(2,1)S(1)}, bf16[8,9088]{1,0:T(8,128)(2,1)S(1)}, u32[]{:S(2)}, u32[]{:S(2)}) collective-permute-start(bf16[8,9088]{1,0:T(8,128)(2,1)S(1)} %get-tuple-element.64), channel_id=1, source_target_pairs={{0,162},{4,166},{8,170},{12,174},{16,178},{20,182},{24,186},{28,19... | collective-permute-start | bytes 436232 | tf_op jit(solution)/shard_map/ppermute | solution.py:395
  66.5 5.7 %collective-permute-done.6.refs_2_ = bf16[8,9088]{1,0:T(8,128)(2,1)S(1)} collective-permute-done((bf16[8,9088]{1,0:T(8,128)(2,1)S(1)}, bf16[8,9088]{1,0:T(8,128)(2,1)S(1)}, u32[]{:S(2)}, u32[]{:S(2)}) %collective-permute-start.6) | collective-permute-done | bytes 145440 | tf_op jit(solution)/shard_map/ppermute | solution.py:395
  72.3 6.3 %collective-permute-done.7.refs_3_ = bf16[8,9088]{1,0:T(8,128)(2,1)S(1)} collective-permute-done((bf16[8,9088]{1,0:T(8,128)(2,1)S(1)}, bf16[8,9088]{1,0:T(8,128)(2,1)S(1)}, u32[]{:S(2)}, u32[]{:S(2)}) %collective-permute-start.7) | collective-permute-done | bytes 145440 | tf_op jit(solution)/shard_map/ppermute | solution.py:395
  80.2 25.7 %all-to-all-done.1 = bf16[8,88,2560]{2,1,0:T(8,128)(2,1)} async-done(((bf16[8,88,2560]{2,1,0:T(8,128)(2,1)}), bf16[8,88,2560]{2,1,0:T(8,128)(2,1)}, u32[]{:S(2)}, u32[]{:S(2)}) %all-to-all-start.1) | async-done | bytes 3604512 | tf_op jit(solution)/shard_map/all_to_all | solution.py:398
  111.4 5.2 %align.1 = (bf16[704,1536]{1,0:T(8,128)(2,1)S(1)}, bf16[256,1536]{1,0:T(8,128)(2,1)S(1)}) custom-call(s32[6]{0:T(128)S(1)} %stack.27.where_ref, bf16[896,1536]{1,0:T(8,128)(2,1)S(1)} %bitcast.38), custom_call_target="tpu_custom_call" | custom-call | flops 2642411520 | bytes 2949120 | tf_op jit(solution)/shard_map/align/pallas_call | solution.py:440
  118.9 5.9 %all-to-all-done.2 = bf16[8,32,2560]{2,1,0:T(8,128)(2,1)S(1)} async-done(((bf16[8,32,2560]{2,1,0:T(8,128)(2,1)}), bf16[8,32,2560]{2,1,0:T(8,128)(2,1)S(1)}, u32[]{:S(2)}, u32[]{:S(2)}) %all-to-all-start.2) | async-done | bytes 1310752 | tf_op jit(solution)/shard_map/all_to_all | solution.py:398
  125.8 7.6 %expert_far.1 = (bf16[256,2560]{1,0:T(8,128)(2,1)}, bf16[256,768]{1,0:T(8,128)(2,1)}) custom-call(bf16[256,2560]{1,0:T(8,128)(2,1)} %bitcast.40, bf16[256,1536]{1,0:T(8,128)(2,1)} %copy-done.1, bf16[768,2560]{1,0:T(8,128)(2,1)} %bitcast.41, bf16[2560,768]{1,0:T(8,128)(2,1)} %bitcast.43), custom_call_target="tpu_custom_call" | custom-call | flops 2013265920 | bytes 10485760 | tf_op jit(solution)/shard_map/expert_far/pallas_call | solution.py:481
  137.0 12.5 %expert_near.1 = (bf16[704,2560]{1,0:T(8,128)(2,1)}, bf16[704,768]{1,0:T(8,128)(2,1)}) custom-call(bf16[704,2560]{1,0:T(8,128)(2,1)} %bitcast.12.x_hbm, bf16[704,1536]{1,0:T(8,128)(2,1)} %copy-done.8, bf16[768,2560]{1,0:T(8,128)(2,1)} %bitcast.42, bf16[2560,768]{1,0:T(8,128)(2,1)} %bitcast.44), custom_call_target="tpu_custom_call" | custom-call | flops 5536481280 | bytes 15073280 | tf_op jit(solution)/shard_map/expert_near/pallas_call | solution.py:481
  152.0 4.6 %all-to-all-start.4 = ((bf16[8,88,2560]{2,1,0:T(8,128)(2,1)}), bf16[8,88,2560]{2,1,0:T(8,128)(2,1)}, u32[]{:S(2)}, u32[]{:S(2)}) async-start(bf16[8,88,2560]{2,1,0:T(8,128)(2,1)} %bitcast.45), calls=%async_computation.4 | async-start | bytes 7208960 | tf_op jit(solution)/shard_map/all_to_all | solution.py:398
  156.7 5.7 %collective-permute-start.8 = (bf16[8,8960]{1,0:T(8,128)(2,1)S(1)}, bf16[8,8960]{1,0:T(8,128)(2,1)S(1)}, u32[]{:S(2)}, u32[]{:S(2)}) collective-permute-start(bf16[8,8960]{1,0:T(8,128)(2,1)S(1)} %get-tuple-element.84), channel_id=1, source_target_pairs={{130,0},{134,4},{138,8},{142,12},{146,16},{150,20},{154,24},{158,2... | collective-permute-start | bytes 430088 | tf_op jit(solution)/shard_map/ppermute | solution.py:395
  171.2 7.6 %collective-permute-done.10.refs_7_ = bf16[8,8960]{1,0:T(8,128)(2,1)S(1)} collective-permute-done((bf16[8,8960]{1,0:T(8,128)(2,1)S(1)}, bf16[8,8960]{1,0:T(8,128)(2,1)S(1)}, u32[]{:S(2)}, u32[]{:S(2)}) %collective-permute-start.10) | collective-permute-done | bytes 143392 | tf_op jit(solution)/shard_map/ppermute | solution.py:395
  182.4 24.4 %all-to-all-done.4 = bf16[8,88,2560]{2,1,0:T(8,128)(2,1)} async-done(((bf16[8,88,2560]{2,1,0:T(8,128)(2,1)}), bf16[8,88,2560]{2,1,0:T(8,128)(2,1)}, u32[]{:S(2)}, u32[]{:S(2)}) %all-to-all-start.4) | async-done | bytes 3604512 | tf_op jit(solution)/shard_map/all_to_all | solution.py:398
  206.8 4.8 %gather_near.1 = (bf16[64,8960]{1,0:T(8,128)(2,1)}, bf16[8,8960]{1,0:T(8,128)(2,1)S(1)}, bf16[8,8960]{1,0:T(8,128)(2,1)S(1)}, bf16[8,8960]{1,0:T(8,128)(2,1)S(1)}, bf16[8,8960]{1,0:T(8,128)(2,1)S(1)}) custom-call(bf16[704,2560]{1,0:T(8,128)(2,1)} %bitcast.21.rows_hbm, bf16[704,384]{1,0:T(8,128)(2,1)S(1)} %copy-done.6), custom_call_target="tpu_custom_call" | custom-call | flops 1384120320 | bytes 3604480 | tf_op jit(solution)/shard_map/gather_near/pallas_call | solution.py:413
  211.5 10.8 %all-to-all-start.5 = ((bf16[8,8,8960]{2,1,0:T(8,128)(2,1)}), bf16[8,8,8960]{2,1,0:T(8,128)(2,1)S(1)}, u32[]{:S(2)}, u32[]{:S(2)}) async-start(bf16[8,8,8960]{2,1,0:T(8,128)(2,1)} %bitcast.22), calls=%async_computation.5 | async-start | bytes 2293760 | tf_op jit(solution)/shard_map/all_to_all | solution.py:391
  222.3 4.4 %collective-permute-start.12 = (bf16[8,8960]{1,0:T(8,128)(2,1)S(1)}, bf16[8,8960]{1,0:T(8,128)(2,1)S(1)}, u32[]{:S(2)}, u32[]{:S(2)}) collective-permute-start(bf16[8,8960]{1,0:T(8,128)(2,1)S(1)} %get-tuple-element.92), channel_id=1, source_target_pairs={{64,0},{68,4},{72,8},{76,12},{80,16},{84,20},{88,24},{92,28},{96,3... | collective-permute-start | bytes 430088 | tf_op jit(solution)/shard_map/ppermute | solution.py:395
  226.7 7.0 %collective-permute-start.13 = (bf16[8,8960]{1,0:T(8,128)(2,1)S(1)}, bf16[8,8960]{1,0:T(8,128)(2,1)S(1)}, u32[]{:S(2)}, u32[]{:S(2)}) collective-permute-start(bf16[8,8960]{1,0:T(8,128)(2,1)S(1)} %get-tuple-element.93), channel_id=1, source_target_pairs={{80,0},{84,4},{88,8},{92,12},{96,16},{100,20},{104,24},{108,28},{1... | collective-permute-start | bytes 430088 | tf_op jit(solution)/shard_map/ppermute | solution.py:395
  242.4 4.0 %collective-permute-done.12.refs_1_ = bf16[8,8960]{1,0:T(8,128)(2,1)S(1)} collective-permute-done((bf16[8,8960]{1,0:T(8,128)(2,1)S(1)}, bf16[8,8960]{1,0:T(8,128)(2,1)S(1)}, u32[]{:S(2)}, u32[]{:S(2)}) %collective-permute-start.12) | collective-permute-done | bytes 143392 | tf_op jit(solution)/shard_map/ppermute | solution.py:395
  250.4 4.6 %collective-permute-done.14.refs_3_ = bf16[8,8960]{1,0:T(8,128)(2,1)S(1)} collective-permute-done((bf16[8,8960]{1,0:T(8,128)(2,1)S(1)}, bf16[8,8960]{1,0:T(8,128)(2,1)S(1)}, u32[]{:S(2)}, u32[]{:S(2)}) %collective-permute-start.14) | collective-permute-done | bytes 143392 | tf_op jit(solution)/shard_map/ppermute | solution.py:395
  (59 shorter events, 72.6 us)
Async XLA Ops:
  6.3 35.8 %all-to-all-start = ((bf16[8,8,9088]{2,1,0:T(8,128)(2,1)}), bf16[8,8,9088]{2,1,0:T(8,128)(2,1)S(1)}, u32[]{:S(2)}, u32[]{:S(2)}) async-start(bf16[8,8,9088]{2,1,0:T(8,128)(2,1)} %bitcast.9), calls=%async_computation | async-start | bytes 2326528 | tf_op jit(solution)/shard_map/all_to_all | solution.py:391
  16.9 9.9 %collective-permute-start = (bf16[8,9088]{1,0:T(8,128)(2,1)S(1)}, bf16[8,9088]{1,0:T(8,128)(2,1)S(1)}, u32[]{:S(2)}, u32[]{:S(2)}) collective-permute-start(bf16[8,9088]{1,0:T(8,128)(2,1)S(1)} %get-tuple-element.53), channel_id=1, source_target_pairs={{0,64},{4,68},{8,72},{12,76},{16,80},{20,84},{24,88},{28,92},{32,9... | collective-permute-start | bytes 436232 | tf_op jit(solution)/shard_map/ppermute | solution.py:395
  16.9 11.3 %collective-permute-start.1 = (bf16[8,9088]{1,0:T(8,128)(2,1)S(1)}, bf16[8,9088]{1,0:T(8,128)(2,1)S(1)}, u32[]{:S(2)}, u32[]{:S(2)}) collective-permute-start(bf16[8,9088]{1,0:T(8,128)(2,1)S(1)} %get-tuple-element.54), channel_id=1, source_target_pairs={{0,80},{4,84},{8,88},{12,92},{16,96},{20,100},{24,104},{28,108},{3... | collective-permute-start | bytes 436232 | tf_op jit(solution)/shard_map/ppermute | solution.py:395
  21.8 10.4 %collective-permute-start.2 = (bf16[8,9088]{1,0:T(8,128)(2,1)S(1)}, bf16[8,9088]{1,0:T(8,128)(2,1)S(1)}, u32[]{:S(2)}, u32[]{:S(2)}) collective-permute-start(bf16[8,9088]{1,0:T(8,128)(2,1)S(1)} %get-tuple-element.55), channel_id=1, source_target_pairs={{0,96},{4,100},{8,104},{12,108},{16,112},{20,116},{24,120},{28,124... | collective-permute-start | bytes 436232 | tf_op jit(solution)/shard_map/ppermute | solution.py:395
  24.0 9.7 %collective-permute-start.3 = (bf16[8,9088]{1,0:T(8,128)(2,1)S(1)}, bf16[8,9088]{1,0:T(8,128)(2,1)S(1)}, u32[]{:S(2)}, u32[]{:S(2)}) collective-permute-start(bf16[8,9088]{1,0:T(8,128)(2,1)S(1)} %get-tuple-element.56), channel_id=1, source_target_pairs={{0,112},{4,116},{8,120},{12,124},{16,64},{20,68},{24,72},{28,76},{... | collective-permute-start | bytes 436232 | tf_op jit(solution)/shard_map/ppermute | solution.py:395
  48.1 57.7 %all-to-all-start.1 = ((bf16[8,88,2560]{2,1,0:T(8,128)(2,1)}), bf16[8,88,2560]{2,1,0:T(8,128)(2,1)}, u32[]{:S(2)}, u32[]{:S(2)}) async-start(bf16[8,88,2560]{2,1,0:T(8,128)(2,1)} %bitcast.36), calls=%async_computation.1 | async-start | bytes 7208960 | tf_op jit(solution)/shard_map/all_to_all | solution.py:398
  52.6 12.9 %collective-permute-start.4 = (bf16[8,9088]{1,0:T(8,128)(2,1)S(1)}, bf16[8,9088]{1,0:T(8,128)(2,1)S(1)}, u32[]{:S(2)}, u32[]{:S(2)}) collective-permute-start(bf16[8,9088]{1,0:T(8,128)(2,1)S(1)} %get-tuple-element.62), channel_id=1, source_target_pairs={{0,130},{4,134},{8,138},{12,142},{16,146},{20,150},{24,154},{28,15... | collective-permute-start | bytes 436232 | tf_op jit(solution)/shard_map/ppermute | solution.py:395
  56.9 9.6 %collective-permute-start.5 = (bf16[8,9088]{1,0:T(8,128)(2,1)S(1)}, bf16[8,9088]{1,0:T(8,128)(2,1)S(1)}, u32[]{:S(2)}, u32[]{:S(2)}) collective-permute-start(bf16[8,9088]{1,0:T(8,128)(2,1)S(1)} %get-tuple-element.63), channel_id=1, source_target_pairs={{0,146},{4,150},{8,154},{12,158},{16,162},{20,166},{24,170},{28,17... | collective-permute-start | bytes 436232 | tf_op jit(solution)/shard_map/ppermute | solution.py:395
  58.1 14.1 %collective-permute-start.6 = (bf16[8,9088]{1,0:T(8,128)(2,1)S(1)}, bf16[8,9088]{1,0:T(8,128)(2,1)S(1)}, u32[]{:S(2)}, u32[]{:S(2)}) collective-permute-start(bf16[8,9088]{1,0:T(8,128)(2,1)S(1)} %get-tuple-element.64), channel_id=1, source_target_pairs={{0,162},{4,166},{8,170},{12,174},{16,178},{20,182},{24,186},{28,19... | collective-permute-start | bytes 436232 | tf_op jit(solution)/shard_map/ppermute | solution.py:395
  63.9 14.6 %collective-permute-start.7 = (bf16[8,9088]{1,0:T(8,128)(2,1)S(1)}, bf16[8,9088]{1,0:T(8,128)(2,1)S(1)}, u32[]{:S(2)}, u32[]{:S(2)}) collective-permute-start(bf16[8,9088]{1,0:T(8,128)(2,1)S(1)} %get-tuple-element.65), channel_id=1, source_target_pairs={{0,178},{4,182},{8,186},{12,190},{16,130},{20,134},{24,138},{28,14... | collective-permute-start | bytes 436232 | tf_op jit(solution)/shard_map/ppermute | solution.py:395
  105.8 18.9 %all-to-all-start.2 = ((bf16[8,32,2560]{2,1,0:T(8,128)(2,1)}), bf16[8,32,2560]{2,1,0:T(8,128)(2,1)S(1)}, u32[]{:S(2)}, u32[]{:S(2)}) async-start(bf16[8,32,2560]{2,1,0:T(8,128)(2,1)} %bitcast.13), calls=%async_computation.2 | async-start | bytes 2621440 | tf_op jit(solution)/shard_map/all_to_all | solution.py:398
  133.4 18.0 %all-to-all-start.3 = ((bf16[8,32,2560]{2,1,0:T(8,128)(2,1)}), bf16[8,32,2560]{2,1,0:T(8,128)(2,1)S(1)}, u32[]{:S(2)}, u32[]{:S(2)}) async-start(bf16[8,32,2560]{2,1,0:T(8,128)(2,1)} %bitcast.46), calls=%async_computation.3 | async-start | bytes 2621440 | tf_op jit(solution)/shard_map/all_to_all | solution.py:398
  152.0 54.7 %copy-start.6 = (bf16[704,384]{1,0:T(8,128)(2,1)S(1)}, bf16[704,384]{1,0:T(8,128)(2,1)}, u32[]{:S(2)}) copy-start(bf16[704,384]{1,0:T(8,128)(2,1)} %copy-done.5) | copy-start | bytes 1622020
  152.0 54.7 %all-to-all-start.4 = ((bf16[8,88,2560]{2,1,0:T(8,128)(2,1)}), bf16[8,88,2560]{2,1,0:T(8,128)(2,1)}, u32[]{:S(2)}, u32[]{:S(2)}) async-start(bf16[8,88,2560]{2,1,0:T(8,128)(2,1)} %bitcast.45), calls=%async_computation.4 | async-start | bytes 7208960 | tf_op jit(solution)/shard_map/all_to_all | solution.py:398
  156.7 14.5 %collective-permute-start.8 = (bf16[8,8960]{1,0:T(8,128)(2,1)S(1)}, bf16[8,8960]{1,0:T(8,128)(2,1)S(1)}, u32[]{:S(2)}, u32[]{:S(2)}) collective-permute-start(bf16[8,8960]{1,0:T(8,128)(2,1)S(1)} %get-tuple-element.84), channel_id=1, source_target_pairs={{130,0},{134,4},{138,8},{142,12},{146,16},{150,20},{154,24},{158,2... | collective-permute-start | bytes 430088 | tf_op jit(solution)/shard_map/ppermute | solution.py:395
  162.4 8.9 %collective-permute-start.9 = (bf16[8,8960]{1,0:T(8,128)(2,1)S(1)}, bf16[8,8960]{1,0:T(8,128)(2,1)S(1)}, u32[]{:S(2)}, u32[]{:S(2)}) collective-permute-start(bf16[8,8960]{1,0:T(8,128)(2,1)S(1)} %get-tuple-element.85), channel_id=1, source_target_pairs={{146,0},{150,4},{154,8},{158,12},{162,16},{166,20},{170,24},{174,2... | collective-permute-start | bytes 430088 | tf_op jit(solution)/shard_map/ppermute | solution.py:395
  166.2 12.7 %collective-permute-start.10 = (bf16[8,8960]{1,0:T(8,128)(2,1)S(1)}, bf16[8,8960]{1,0:T(8,128)(2,1)S(1)}, u32[]{:S(2)}, u32[]{:S(2)}) collective-permute-start(bf16[8,8960]{1,0:T(8,128)(2,1)S(1)} %get-tuple-element.86), channel_id=1, source_target_pairs={{162,0},{166,4},{170,8},{174,12},{178,16},{182,20},{186,24},{190,2... | collective-permute-start | bytes 430088 | tf_op jit(solution)/shard_map/ppermute | solution.py:395
  170.0 12.4 %collective-permute-start.11 = (bf16[8,8960]{1,0:T(8,128)(2,1)S(1)}, bf16[8,8960]{1,0:T(8,128)(2,1)S(1)}, u32[]{:S(2)}, u32[]{:S(2)}) collective-permute-start(bf16[8,8960]{1,0:T(8,128)(2,1)S(1)} %get-tuple-element.87), channel_id=1, source_target_pairs={{178,0},{182,4},{186,8},{190,12},{130,16},{134,20},{138,24},{142,2... | collective-permute-start | bytes 430088 | tf_op jit(solution)/shard_map/ppermute | solution.py:395
  211.5 46.2 %all-to-all-start.5 = ((bf16[8,8,8960]{2,1,0:T(8,128)(2,1)}), bf16[8,8,8960]{2,1,0:T(8,128)(2,1)S(1)}, u32[]{:S(2)}, u32[]{:S(2)}) async-start(bf16[8,8,8960]{2,1,0:T(8,128)(2,1)} %bitcast.22), calls=%async_computation.5 | async-start | bytes 2293760 | tf_op jit(solution)/shard_map/all_to_all | solution.py:391
  222.3 24.1 %collective-permute-start.12 = (bf16[8,8960]{1,0:T(8,128)(2,1)S(1)}, bf16[8,8960]{1,0:T(8,128)(2,1)S(1)}, u32[]{:S(2)}, u32[]{:S(2)}) collective-permute-start(bf16[8,8960]{1,0:T(8,128)(2,1)S(1)} %get-tuple-element.92), channel_id=1, source_target_pairs={{64,0},{68,4},{72,8},{76,12},{80,16},{84,20},{88,24},{92,28},{96,3... | collective-permute-start | bytes 430088 | tf_op jit(solution)/shard_map/ppermute | solution.py:395
  226.7 23.7 %collective-permute-start.13 = (bf16[8,8960]{1,0:T(8,128)(2,1)S(1)}, bf16[8,8960]{1,0:T(8,128)(2,1)S(1)}, u32[]{:S(2)}, u32[]{:S(2)}) collective-permute-start(bf16[8,8960]{1,0:T(8,128)(2,1)S(1)} %get-tuple-element.93), channel_id=1, source_target_pairs={{80,0},{84,4},{88,8},{92,12},{96,16},{100,20},{104,24},{108,28},{1... | collective-permute-start | bytes 430088 | tf_op jit(solution)/shard_map/ppermute | solution.py:395
  233.7 21.3 %collective-permute-start.14 = (bf16[8,8960]{1,0:T(8,128)(2,1)S(1)}, bf16[8,8960]{1,0:T(8,128)(2,1)S(1)}, u32[]{:S(2)}, u32[]{:S(2)}) collective-permute-start(bf16[8,8960]{1,0:T(8,128)(2,1)S(1)} %get-tuple-element.94), channel_id=1, source_target_pairs={{96,0},{100,4},{104,8},{108,12},{112,16},{116,20},{120,24},{124,28... | collective-permute-start | bytes 430088 | tf_op jit(solution)/shard_map/ppermute | solution.py:395
  236.8 21.0 %collective-permute-start.15 = (bf16[8,8960]{1,0:T(8,128)(2,1)S(1)}, bf16[8,8960]{1,0:T(8,128)(2,1)S(1)}, u32[]{:S(2)}, u32[]{:S(2)}) collective-permute-start(bf16[8,8960]{1,0:T(8,128)(2,1)S(1)} %get-tuple-element.95), channel_id=1, source_target_pairs={{112,0},{116,4},{120,8},{124,12},{64,16},{68,20},{72,24},{76,28},{... | collective-permute-start | bytes 430088 | tf_op jit(solution)/shard_map/ppermute | solution.py:395
  258.3 3.7 %collective-permute-start.16 = (bf16[128,2560]{1,0:T(8,128)(2,1)S(1)}, bf16[128,2560]{1,0:T(8,128)(2,1)S(1)}, u32[]{:S(2)}, u32[]{:S(2)}) collective-permute-start(bf16[128,2560]{1,0:T(8,128)(2,1)S(1)} %combine.1), channel_id=1, source_target_pairs={{1,0},{0,1},{3,2},{2,3},{5,4},{4,5},{7,6},{6,7},{9,8},{8,9},{11,10... | collective-permute-start | bytes 1966088 | tf_op jit(solution)/shard_map/ppermute | solution.py:473
  (9 other events, 36.4 us)

commit v3 on v2

--- a/solution.py
+++ b/solution.py
@@ -93,9 +93,9 @@
 
 
 def put_blocks(block_refs, value, start):
-    value, row = value.astype(BF16), 0
+    row = 0
     for ref in block_refs:
-        ref[:, start : start + value.shape[1]] = value[row : row + ref.shape[0]]
+        ref[:, start : start + value.shape[1]] = value[row : row + ref.shape[0]].astype(BF16)
         row += ref.shape[0]
 
 
@@ -427,12 +427,12 @@
         *values, first = lax.optimization_barrier((*values, first))
         return first, *values
 
-    ids = route_ids[0].T.reshape(routes, 1, tok)
+    ids, weights = (jnp.transpose(a, (2, 0, 1)) for a in (route_ids, route_w))
     shapes = [8 * SUB] + [SUB] * 8
     near, *others = call(
         functools.partial(dispatch_kernel, (groups, in_group, group_cap, cap)), "dispatch", 3,
         [array(h, sent) for h in shapes], 12, 2 * deep * tok * features,
-    )(where, ids, route_w[0].T.reshape(routes, 1, tok), grad_out[0])
+    )(where, ids, weights, grad_out[0])
     [line] = call(
         functools.partial(lines_kernel, (groups, in_group, group_cap)), "lines", 1,
         [array(deep, tok)], 8, 4 * deep * tok * tok,
@@ -448,22 +448,24 @@
     rows_n, hit_n = spread("spread_near", [near, *mid], heights[0])
     rows_n = in_groups(rows_n)
     rows_f, hit_f = spread("spread_far", far, heights[1])
-    rows_n, rows_f = after(rows_n, rows_f)
+    rows_n, rows_f, *kept = after(rows_n, rows_f, *kept)
     rows_f = in_groups(rows_f)
     rows_n, gate_n = expert_call("expert_near", rows_n, kept[0], w_down[0, 0], w_up[0, 0])
+    rows_f, rows_n = after(rows_f, rows_n)
+    rows_n = in_groups(rows_n)
     rows_f, gate_f = expert_call("expert_far", rows_f, kept[1], w_down[0, 0], w_up[0, 0])
+    near, *mid = gather("gather_near", rows_n, hit_n, [8 * SUB] + [SUB] * 4)
+    near, rows_f, *mid = after(near, rows_f, *mid)
+    mid = hop(mid, 2, True)
     rows_f = in_groups(rows_f)
     far = gather("gather_far", rows_f, hit_f, [SUB] * 4)
-    rows_n, *far = after(rows_n, *far)
-    far = hop(far, 3, True)
-    rows_n = in_groups(rows_n)
-    rows_n, *far = after(rows_n, *far)
+    near, *ready = after(near, *mid, *far)
+    mid, far = ready[:4], hop(ready[4:], 3, True)
+    near = near_swap(near)
     [gate_grad] = call(
         functools.partial(restore_kernel, (in_group, cap)), "restore", 2, [array(slots_all, hidden)], 12,
         2 * sum(heights) * slots_all * hidden,
     )(where, gate_n, gate_f)
-    near, *mid = gather("gather_near", rows_n, hit_n, [8 * SUB] + [SUB] * 4)
-    near, mid = near_swap(near), hop(mid, 2, True)
     gate_grad, line = after(gate_grad, line)
     [token_grad] = call(
         combine_kernel, "combine", 10, [array(tok, features)], 12, 2 * deep * tok * features,

time: 264 us -> 266 us (level)
    all_to_all x4, waiting for transfers between devices: 57.8 us -> 72.9 us  [in_groups(): lax.all_to_all(rows.reshape(in_group, -1, features), 'inner', 0, 0, tiled...]
    ppermute x16, waiting for transfers between devices: 46.5 us -> 32.7 us  [hop(): lax.ppermute(b, both, routes_over(hops, dy, back))]
    all_to_all x2, starting transfers between devices: 21.4 us -> 18 us  [near_swap(): lax.all_to_all(block.reshape(8, SUB, width), both, 0, 0, axis_index_group...]
    all_to_all x4, starting transfers between devices: 16.4 us -> 19.7 us  [in_groups(): lax.all_to_all(rows.reshape(in_group, -1, features), 'inner', 0, 0, tiled...]
    ppermute x1, starting transfers between devices: 2.01 us -> 4.69 us  [on_device(): lax.ppermute(token_grad, 'section', [((i + 1) % count, i) for i in range(...]
    unnamed x23 -> x27, local copies, waits for them, and re-layouts: 12.2 us -> 12.2 us
  transfers between devices with their start and end apart: 23 -> 23, of which waited for: 18 -> 13; matrix products, arithmetic and copies ran while one was open for 0% -> 0% of each run, Pallas kernels for 9% -> 12%
where the time goes in v3:
time: 266 us; the launch traced here: 265 us
  waiting for transfers between devices  116 us (44%)
  starting transfers between devices  92.5 us (35%)
  Pallas kernels  43.4 us (16%)
  local copies, waits for them, and re-layouts  12.3 us (5%)
    all_to_all x4, waiting for transfers between devices, in_groups(): lax.all_to_all(rows.reshape(in_group, -1, features), 'inner', 0, 0, tiled...  72.9 us
    ppermute x16, starting transfers between devices, hop(): lax.ppermute(b, both, routes_over(hops, dy, back))  50.1 us
    ppermute x16, waiting for transfers between devices, hop(): lax.ppermute(b, both, routes_over(hops, dy, back))  32.7 us
    pallas_call x2, Pallas kernels, expert_call(): pl.pallas_call(expert_kernel, name=name, in_specs=[hbm] * 4, out_specs=[h...  20.1 us
    all_to_all x4, starting transfers between devices, in_groups(): lax.all_to_all(rows.reshape(in_group, -1, features), 'inner', 0, 0, tiled...  19.7 us
    all_to_all x2, starting transfers between devices, near_swap(): lax.all_to_all(block.reshape(8, SUB, width), both, 0, 0, axis_index_group...  18 us
    unnamed x27, local copies, waits for them, and re-layouts  12.2 us
    all_to_all x2, waiting for transfers between devices, near_swap(): lax.all_to_all(block.reshape(8, SUB, width), both, 0, 0, axis_index_group...  8.5 us
  transfers between devices with their start and end apart: 23, of which 13 were waited for; matrix products, arithmetic and copies ran while one was open for 0% of the time, Pallas kernels for 12%

profile of v3, /device:TPU:1, one launch (start us, length us, event | category | flops | bytes accessed | tf_op | source)
XLA Modules:
  0.0 265.0 jit_solution(6244423028394412394)
XLA Ops:
  6.3 10.6 %all-to-all-start = ((bf16[8,8,9088]{2,1,0:T(8,128)(2,1)}), bf16[8,8,9088]{2,1,0:T(8,128)(2,1)S(1)}, u32[]{:S(2)}, u32[]{:S(2)}) async-start(bf16[8,8,9088]{2,1,0:T(8,128)(2,1)} %bitcast.9), calls=%async_computation | async-start | bytes 2326528 | tf_op jit(solution)/shard_map/all_to_all | solution.py:391
  16.9 4.9 %collective-permute-start.1 = (bf16[8,9088]{1,0:T(8,128)(2,1)S(1)}, bf16[8,9088]{1,0:T(8,128)(2,1)S(1)}, u32[]{:S(2)}, u32[]{:S(2)}) collective-permute-start(bf16[8,9088]{1,0:T(8,128)(2,1)S(1)} %get-tuple-element.63), channel_id=1, source_target_pairs={{0,80},{4,84},{8,88},{12,92},{16,96},{20,100},{24,104},{28,108},{3... | collective-permute-start | bytes 436232 | tf_op jit(solution)/shard_map/ppermute | solution.py:395
  28.2 4.0 %collective-permute-done.2.refs_3_ = bf16[8,9088]{1,0:T(8,128)(2,1)S(1)} collective-permute-done((bf16[8,9088]{1,0:T(8,128)(2,1)S(1)}, bf16[8,9088]{1,0:T(8,128)(2,1)S(1)}, u32[]{:S(2)}, u32[]{:S(2)}) %collective-permute-start.2) | collective-permute-done | bytes 145440 | tf_op jit(solution)/shard_map/ppermute | solution.py:395
  33.7 8.5 %all-to-all-done = bf16[8,8,9088]{2,1,0:T(8,128)(2,1)S(1)} async-done(((bf16[8,8,9088]{2,1,0:T(8,128)(2,1)}), bf16[8,8,9088]{2,1,0:T(8,128)(2,1)S(1)}, u32[]{:S(2)}, u32[]{:S(2)}) %all-to-all-start) | async-done | bytes 1163296 | tf_op jit(solution)/shard_map/all_to_all | solution.py:391
  48.1 4.5 %all-to-all-start.1 = ((bf16[8,88,2560]{2,1,0:T(8,128)(2,1)}), bf16[8,88,2560]{2,1,0:T(8,128)(2,1)}, u32[]{:S(2)}, u32[]{:S(2)}) async-start(bf16[8,88,2560]{2,1,0:T(8,128)(2,1)} %bitcast.28), calls=%async_computation.1 | async-start | bytes 7208960 | tf_op jit(solution)/shard_map/all_to_all | solution.py:398
  52.6 4.3 %collective-permute-start.4 = (bf16[8,9088]{1,0:T(8,128)(2,1)S(1)}, bf16[8,9088]{1,0:T(8,128)(2,1)S(1)}, u32[]{:S(2)}, u32[]{:S(2)}) collective-permute-start(bf16[8,9088]{1,0:T(8,128)(2,1)S(1)} %get-tuple-element.71), channel_id=1, source_target_pairs={{0,130},{4,134},{8,138},{12,142},{16,146},{20,150},{24,154},{28,15... | collective-permute-start | bytes 436232 | tf_op jit(solution)/shard_map/ppermute | solution.py:395
  58.1 5.8 %collective-permute-start.6 = (bf16[8,9088]{1,0:T(8,128)(2,1)S(1)}, bf16[8,9088]{1,0:T(8,128)(2,1)S(1)}, u32[]{:S(2)}, u32[]{:S(2)}) collective-permute-start(bf16[8,9088]{1,0:T(8,128)(2,1)S(1)} %get-tuple-element.73), channel_id=1, source_target_pairs={{0,162},{4,166},{8,170},{12,174},{16,178},{20,182},{24,186},{28,19... | collective-permute-start | bytes 436232 | tf_op jit(solution)/shard_map/ppermute | solution.py:395
  67.3 5.2 %align.1 = (bf16[704,1536]{1,0:T(8,128)(2,1)S(1)}, bf16[256,1536]{1,0:T(8,128)(2,1)S(1)}) custom-call(s32[6]{0:T(128)S(1)} %stack.27.where_ref, bf16[896,1536]{1,0:T(8,128)(2,1)S(1)} %bitcast.32), custom_call_target="tpu_custom_call" | custom-call | flops 2642411520 | bytes 2949120 | tf_op jit(solution)/shard_map/align/pallas_call | solution.py:440
  74.8 3.9 %collective-permute-done.7.refs_3_ = bf16[8,9088]{1,0:T(8,128)(2,1)S(1)} collective-permute-done((bf16[8,9088]{1,0:T(8,128)(2,1)S(1)}, bf16[8,9088]{1,0:T(8,128)(2,1)S(1)}, u32[]{:S(2)}, u32[]{:S(2)}) %collective-permute-start.7) | collective-permute-done | bytes 145440 | tf_op jit(solution)/shard_map/ppermute | solution.py:395
  80.3 25.7 %all-to-all-done.1 = bf16[8,88,2560]{2,1,0:T(8,128)(2,1)} async-done(((bf16[8,88,2560]{2,1,0:T(8,128)(2,1)}), bf16[8,88,2560]{2,1,0:T(8,128)(2,1)}, u32[]{:S(2)}, u32[]{:S(2)}) %all-to-all-start.1) | async-done | bytes 3604512 | tf_op jit(solution)/shard_map/all_to_all | solution.py:398
  109.5 12.5 %expert_near.1 = (bf16[704,2560]{1,0:T(8,128)(2,1)}, bf16[704,768]{1,0:T(8,128)(2,1)}) custom-call(bf16[704,2560]{1,0:T(8,128)(2,1)} %bitcast.13.x_hbm, bf16[704,1536]{1,0:T(8,128)(2,1)} %copy-done.11, bf16[768,2560]{1,0:T(8,128)(2,1)} %bitcast.36, bf16[2560,768]{1,0:T(8,128)(2,1)} %bitcast.38), custom_call_target="tpu_custom_call" | custom-call | flops 5536481280 | bytes 15073280 | tf_op jit(solution)/shard_map/expert_near/pallas_call | solution.py:483
  125.9 4.7 %all-to-all-start.3 = ((bf16[8,88,2560]{2,1,0:T(8,128)(2,1)}), bf16[8,88,2560]{2,1,0:T(8,128)(2,1)}, u32[]{:S(2)}, u32[]{:S(2)}) async-start(bf16[8,88,2560]{2,1,0:T(8,128)(2,1)} %bitcast.40), calls=%async_computation.3 | async-start | bytes 7208960 | tf_op jit(solution)/shard_map/all_to_all | solution.py:398
  130.6 7.6 %expert_far.1 = (bf16[256,2560]{1,0:T(8,128)(2,1)}, bf16[256,768]{1,0:T(8,128)(2,1)}) custom-call(bf16[256,2560]{1,0:T(8,128)(2,1)} %bitcast.35, bf16[256,1536]{1,0:T(8,128)(2,1)} %copy-done.1, bf16[768,2560]{1,0:T(8,128)(2,1)} %bitcast.37, bf16[2560,768]{1,0:T(8,128)(2,1)} %bitcast.39), custom_call_target="tpu_custom_call" | custom-call | flops 2013265920 | bytes 10485760 | tf_op jit(solution)/shard_map/expert_far/pallas_call | solution.py:483
  138.3 31.2 %all-to-all-done.3 = bf16[8,88,2560]{2,1,0:T(8,128)(2,1)} async-done(((bf16[8,88,2560]{2,1,0:T(8,128)(2,1)}), bf16[8,88,2560]{2,1,0:T(8,128)(2,1)}, u32[]{:S(2)}, u32[]{:S(2)}) %all-to-all-start.3) | async-done | bytes 3604512 | tf_op jit(solution)/shard_map/all_to_all | solution.py:398
  169.5 4.8 %gather_near.1 = (bf16[64,8960]{1,0:T(8,128)(2,1)}, bf16[8,8960]{1,0:T(8,128)(2,1)S(1)}, bf16[8,8960]{1,0:T(8,128)(2,1)S(1)}, bf16[8,8960]{1,0:T(8,128)(2,1)}, bf16[8,8960]{1,0:T(8,128)(2,1)S(1)}) custom-call(bf16[704,2560]{1,0:T(8,128)(2,1)} %bitcast.19.rows_hbm, bf16[704,384]{1,0:T(8,128)(2,1)S(1)} %copy-done.9), custom_call_target="tpu_custom_call" | custom-call | flops 1384120320 | bytes 3604480 | tf_op jit(solution)/shard_map/gather_near/pallas_call | solution.py:413
  174.3 6.9 %all-to-all-start.4 = ((bf16[8,32,2560]{2,1,0:T(8,128)(2,1)}), bf16[8,32,2560]{2,1,0:T(8,128)(2,1)S(1)}, u32[]{:S(2)}, u32[]{:S(2)}) async-start(bf16[8,32,2560]{2,1,0:T(8,128)(2,1)} %bitcast.41), calls=%async_computation.4 | async-start | bytes 2621440 | tf_op jit(solution)/shard_map/all_to_all | solution.py:398
  181.2 6.9 %collective-permute-start.10 = (bf16[8,8960]{1,0:T(8,128)(2,1)}, bf16[8,8960]{1,0:T(8,128)(2,1)S(1)}, u32[]{:S(2)}, u32[]{:S(2)}) collective-permute-start(bf16[8,8960]{1,0:T(8,128)(2,1)} %get-tuple-element.100), channel_id=1, source_target_pairs={{96,0},{100,4},{104,8},{108,12},{112,16},{116,20},{120,24},{124,28... | collective-permute-start | bytes 430088 | tf_op jit(solution)/shard_map/ppermute | solution.py:395
  188.5 6.3 %collective-permute-start.8 = (bf16[8,8960]{1,0:T(8,128)(2,1)S(1)}, bf16[8,8960]{1,0:T(8,128)(2,1)S(1)}, u32[]{:S(2)}, u32[]{:S(2)}) collective-permute-start(bf16[8,8960]{1,0:T(8,128)(2,1)S(1)} %get-tuple-element.98), channel_id=1, source_target_pairs={{64,0},{68,4},{72,8},{76,12},{80,16},{84,20},{88,24},{92,28},{96,3... | collective-permute-start | bytes 430088 | tf_op jit(solution)/shard_map/ppermute | solution.py:395
  196.9 13.2 %all-to-all-done.4 = bf16[8,32,2560]{2,1,0:T(8,128)(2,1)S(1)} async-done(((bf16[8,32,2560]{2,1,0:T(8,128)(2,1)}), bf16[8,32,2560]{2,1,0:T(8,128)(2,1)S(1)}, u32[]{:S(2)}, u32[]{:S(2)}) %all-to-all-start.4) | async-done | bytes 1310752 | tf_op jit(solution)/shard_map/all_to_all | solution.py:398
  210.9 7.4 %all-to-all-start.5 = ((bf16[8,8,8960]{2,1,0:T(8,128)(2,1)}), bf16[8,8,8960]{2,1,0:T(8,128)(2,1)S(1)}, u32[]{:S(2)}, u32[]{:S(2)}) async-start(bf16[8,8,8960]{2,1,0:T(8,128)(2,1)} %bitcast.22), calls=%async_computation.5 | async-start | bytes 2293760 | tf_op jit(solution)/shard_map/all_to_all | solution.py:391
  220.4 4.5 %collective-permute-start.13 = (bf16[8,8960]{1,0:T(8,128)(2,1)S(1)}, bf16[8,8960]{1,0:T(8,128)(2,1)S(1)}, u32[]{:S(2)}, u32[]{:S(2)}) collective-permute-start(bf16[8,8960]{1,0:T(8,128)(2,1)S(1)} %get-tuple-element.115), channel_id=1, source_target_pairs={{146,0},{150,4},{154,8},{158,12},{162,16},{166,20},{170,24},{174,2... | collective-permute-start | bytes 430088 | tf_op jit(solution)/shard_map/ppermute | solution.py:395
  235.3 5.3 %collective-permute-done.13.refs_6_ = bf16[8,8960]{1,0:T(8,128)(2,1)S(1)} collective-permute-done((bf16[8,8960]{1,0:T(8,128)(2,1)S(1)}, bf16[8,8960]{1,0:T(8,128)(2,1)S(1)}, u32[]{:S(2)}, u32[]{:S(2)}) %collective-permute-start.13) | collective-permute-done | bytes 143392 | tf_op jit(solution)/shard_map/ppermute | solution.py:395
  240.6 13.8 %collective-permute-done.14.refs_7_ = bf16[8,8960]{1,0:T(8,128)(2,1)S(1)} collective-permute-done((bf16[8,8960]{1,0:T(8,128)(2,1)S(1)}, bf16[8,8960]{1,0:T(8,128)(2,1)S(1)}, u32[]{:S(2)}, u32[]{:S(2)}) %collective-permute-start.14) | collective-permute-done | bytes 143392 | tf_op jit(solution)/shard_map/ppermute | solution.py:395
  257.8 4.7 %collective-permute-start.16 = (bf16[128,2560]{1,0:T(8,128)(2,1)S(1)}, bf16[128,2560]{1,0:T(8,128)(2,1)S(1)}, u32[]{:S(2)}, u32[]{:S(2)}) collective-permute-start(bf16[128,2560]{1,0:T(8,128)(2,1)S(1)} %combine.1), channel_id=1, source_target_pairs={{1,0},{0,1},{3,2},{2,3},{5,4},{4,5},{7,6},{6,7},{9,8},{8,9},{11,10... | collective-permute-start | bytes 1966088 | tf_op jit(solution)/shard_map/ppermute | solution.py:475
  (61 shorter events, 56.9 us)
Async XLA Ops:
  6.3 35.8 %all-to-all-start = ((bf16[8,8,9088]{2,1,0:T(8,128)(2,1)}), bf16[8,8,9088]{2,1,0:T(8,128)(2,1)S(1)}, u32[]{:S(2)}, u32[]{:S(2)}) async-start(bf16[8,8,9088]{2,1,0:T(8,128)(2,1)} %bitcast.9), calls=%async_computation | async-start | bytes 2326528 | tf_op jit(solution)/shard_map/all_to_all | solution.py:391
  16.9 9.9 %collective-permute-start = (bf16[8,9088]{1,0:T(8,128)(2,1)S(1)}, bf16[8,9088]{1,0:T(8,128)(2,1)S(1)}, u32[]{:S(2)}, u32[]{:S(2)}) collective-permute-start(bf16[8,9088]{1,0:T(8,128)(2,1)S(1)} %get-tuple-element.62), channel_id=1, source_target_pairs={{0,64},{4,68},{8,72},{12,76},{16,80},{20,84},{24,88},{28,92},{32,9... | collective-permute-start | bytes 436232 | tf_op jit(solution)/shard_map/ppermute | solution.py:395
  16.9 11.3 %collective-permute-start.1 = (bf16[8,9088]{1,0:T(8,128)(2,1)S(1)}, bf16[8,9088]{1,0:T(8,128)(2,1)S(1)}, u32[]{:S(2)}, u32[]{:S(2)}) collective-permute-start(bf16[8,9088]{1,0:T(8,128)(2,1)S(1)} %get-tuple-element.63), channel_id=1, source_target_pairs={{0,80},{4,84},{8,88},{12,92},{16,96},{20,100},{24,104},{28,108},{3... | collective-permute-start | bytes 436232 | tf_op jit(solution)/shard_map/ppermute | solution.py:395
  21.8 10.4 %collective-permute-start.2 = (bf16[8,9088]{1,0:T(8,128)(2,1)S(1)}, bf16[8,9088]{1,0:T(8,128)(2,1)S(1)}, u32[]{:S(2)}, u32[]{:S(2)}) collective-permute-start(bf16[8,9088]{1,0:T(8,128)(2,1)S(1)} %get-tuple-element.64), channel_id=1, source_target_pairs={{0,96},{4,100},{8,104},{12,108},{16,112},{20,116},{24,120},{28,124... | collective-permute-start | bytes 436232 | tf_op jit(solution)/shard_map/ppermute | solution.py:395
  23.9 9.7 %collective-permute-start.3 = (bf16[8,9088]{1,0:T(8,128)(2,1)S(1)}, bf16[8,9088]{1,0:T(8,128)(2,1)S(1)}, u32[]{:S(2)}, u32[]{:S(2)}) collective-permute-start(bf16[8,9088]{1,0:T(8,128)(2,1)S(1)} %get-tuple-element.65), channel_id=1, source_target_pairs={{0,112},{4,116},{8,120},{12,124},{16,64},{20,68},{24,72},{28,76},{... | collective-permute-start | bytes 436232 | tf_op jit(solution)/shard_map/ppermute | solution.py:395
  48.1 57.8 %all-to-all-start.1 = ((bf16[8,88,2560]{2,1,0:T(8,128)(2,1)}), bf16[8,88,2560]{2,1,0:T(8,128)(2,1)}, u32[]{:S(2)}, u32[]{:S(2)}) async-start(bf16[8,88,2560]{2,1,0:T(8,128)(2,1)} %bitcast.28), calls=%async_computation.1 | async-start | bytes 7208960 | tf_op jit(solution)/shard_map/all_to_all | solution.py:398
  52.6 22.2 %collective-permute-start.4 = (bf16[8,9088]{1,0:T(8,128)(2,1)S(1)}, bf16[8,9088]{1,0:T(8,128)(2,1)S(1)}, u32[]{:S(2)}, u32[]{:S(2)}) collective-permute-start(bf16[8,9088]{1,0:T(8,128)(2,1)S(1)} %get-tuple-element.71), channel_id=1, source_target_pairs={{0,130},{4,134},{8,138},{12,142},{16,146},{20,150},{24,154},{28,15... | collective-permute-start | bytes 436232 | tf_op jit(solution)/shard_map/ppermute | solution.py:395
  56.9 17.9 %collective-permute-start.5 = (bf16[8,9088]{1,0:T(8,128)(2,1)S(1)}, bf16[8,9088]{1,0:T(8,128)(2,1)S(1)}, u32[]{:S(2)}, u32[]{:S(2)}) collective-permute-start(bf16[8,9088]{1,0:T(8,128)(2,1)S(1)} %get-tuple-element.72), channel_id=1, source_target_pairs={{0,146},{4,150},{8,154},{12,158},{16,162},{20,166},{24,170},{28,17... | collective-permute-start | bytes 436232 | tf_op jit(solution)/shard_map/ppermute | solution.py:395
  58.1 16.7 %collective-permute-start.6 = (bf16[8,9088]{1,0:T(8,128)(2,1)S(1)}, bf16[8,9088]{1,0:T(8,128)(2,1)S(1)}, u32[]{:S(2)}, u32[]{:S(2)}) collective-permute-start(bf16[8,9088]{1,0:T(8,128)(2,1)S(1)} %get-tuple-element.73), channel_id=1, source_target_pairs={{0,162},{4,166},{8,170},{12,174},{16,178},{20,182},{24,186},{28,19... | collective-permute-start | bytes 436232 | tf_op jit(solution)/shard_map/ppermute | solution.py:395
  64.0 14.7 %collective-permute-start.7 = (bf16[8,9088]{1,0:T(8,128)(2,1)S(1)}, bf16[8,9088]{1,0:T(8,128)(2,1)S(1)}, u32[]{:S(2)}, u32[]{:S(2)}) collective-permute-start(bf16[8,9088]{1,0:T(8,128)(2,1)S(1)} %get-tuple-element.74), channel_id=1, source_target_pairs={{0,178},{4,182},{8,186},{12,190},{16,130},{20,134},{24,138},{28,14... | collective-permute-start | bytes 436232 | tf_op jit(solution)/shard_map/ppermute | solution.py:395
  105.9 18.9 %all-to-all-start.2 = ((bf16[8,32,2560]{2,1,0:T(8,128)(2,1)}), bf16[8,32,2560]{2,1,0:T(8,128)(2,1)S(1)}, u32[]{:S(2)}, u32[]{:S(2)}) async-start(bf16[8,32,2560]{2,1,0:T(8,128)(2,1)} %bitcast.16), calls=%async_computation.2 | async-start | bytes 2621440 | tf_op jit(solution)/shard_map/all_to_all | solution.py:398
  125.9 43.6 %all-to-all-start.3 = ((bf16[8,88,2560]{2,1,0:T(8,128)(2,1)}), bf16[8,88,2560]{2,1,0:T(8,128)(2,1)}, u32[]{:S(2)}, u32[]{:S(2)}) async-start(bf16[8,88,2560]{2,1,0:T(8,128)(2,1)} %bitcast.40), calls=%async_computation.3 | async-start | bytes 7208960 | tf_op jit(solution)/shard_map/all_to_all | solution.py:398
  130.6 38.9 %copy-start.9 = (bf16[704,384]{1,0:T(8,128)(2,1)S(1)}, bf16[704,384]{1,0:T(8,128)(2,1)}, u32[]{:S(2)}) copy-start(bf16[704,384]{1,0:T(8,128)(2,1)} %copy-done.8) | copy-start | bytes 1622020
  174.3 35.8 %all-to-all-start.4 = ((bf16[8,32,2560]{2,1,0:T(8,128)(2,1)}), bf16[8,32,2560]{2,1,0:T(8,128)(2,1)S(1)}, u32[]{:S(2)}, u32[]{:S(2)}) async-start(bf16[8,32,2560]{2,1,0:T(8,128)(2,1)} %bitcast.41), calls=%async_computation.4 | async-start | bytes 2621440 | tf_op jit(solution)/shard_map/all_to_all | solution.py:398
  181.2 29.6 %collective-permute-start.10 = (bf16[8,8960]{1,0:T(8,128)(2,1)}, bf16[8,8960]{1,0:T(8,128)(2,1)S(1)}, u32[]{:S(2)}, u32[]{:S(2)}) collective-permute-start(bf16[8,8960]{1,0:T(8,128)(2,1)} %get-tuple-element.100), channel_id=1, source_target_pairs={{96,0},{100,4},{104,8},{108,12},{112,16},{116,20},{120,24},{124,28... | collective-permute-start | bytes 430088 | tf_op jit(solution)/shard_map/ppermute | solution.py:395
  188.1 22.8 %collective-permute-start.11 = (bf16[8,8960]{1,0:T(8,128)(2,1)S(1)}, bf16[8,8960]{1,0:T(8,128)(2,1)S(1)}, u32[]{:S(2)}, u32[]{:S(2)}) collective-permute-start(bf16[8,8960]{1,0:T(8,128)(2,1)S(1)} %get-tuple-element.101), channel_id=1, source_target_pairs={{112,0},{116,4},{120,8},{124,12},{64,16},{68,20},{72,24},{76,28},{... | collective-permute-start | bytes 430088 | tf_op jit(solution)/shard_map/ppermute | solution.py:395
  188.5 22.4 %collective-permute-start.8 = (bf16[8,8960]{1,0:T(8,128)(2,1)S(1)}, bf16[8,8960]{1,0:T(8,128)(2,1)S(1)}, u32[]{:S(2)}, u32[]{:S(2)}) collective-permute-start(bf16[8,8960]{1,0:T(8,128)(2,1)S(1)} %get-tuple-element.98), channel_id=1, source_target_pairs={{64,0},{68,4},{72,8},{76,12},{80,16},{84,20},{88,24},{92,28},{96,3... | collective-permute-start | bytes 430088 | tf_op jit(solution)/shard_map/ppermute | solution.py:395
  194.7 16.1 %collective-permute-start.9 = (bf16[8,8960]{1,0:T(8,128)(2,1)S(1)}, bf16[8,8960]{1,0:T(8,128)(2,1)S(1)}, u32[]{:S(2)}, u32[]{:S(2)}) collective-permute-start(bf16[8,8960]{1,0:T(8,128)(2,1)S(1)} %get-tuple-element.99), channel_id=1, source_target_pairs={{80,0},{84,4},{88,8},{92,12},{96,16},{100,20},{104,24},{108,28},{1... | collective-permute-start | bytes 430088 | tf_op jit(solution)/shard_map/ppermute | solution.py:395
  210.9 46.3 %all-to-all-start.5 = ((bf16[8,8,8960]{2,1,0:T(8,128)(2,1)}), bf16[8,8,8960]{2,1,0:T(8,128)(2,1)S(1)}, u32[]{:S(2)}, u32[]{:S(2)}) async-start(bf16[8,8,8960]{2,1,0:T(8,128)(2,1)} %bitcast.22), calls=%async_computation.5 | async-start | bytes 2293760 | tf_op jit(solution)/shard_map/all_to_all | solution.py:391
  218.3 17.0 %collective-permute-start.12 = (bf16[8,8960]{1,0:T(8,128)(2,1)S(1)}, bf16[8,8960]{1,0:T(8,128)(2,1)S(1)}, u32[]{:S(2)}, u32[]{:S(2)}) collective-permute-start(bf16[8,8960]{1,0:T(8,128)(2,1)S(1)} %get-tuple-element.114), channel_id=1, source_target_pairs={{130,0},{134,4},{138,8},{142,12},{146,16},{150,20},{154,24},{158,2... | collective-permute-start | bytes 430088 | tf_op jit(solution)/shard_map/ppermute | solution.py:395
  220.4 20.3 %collective-permute-start.13 = (bf16[8,8960]{1,0:T(8,128)(2,1)S(1)}, bf16[8,8960]{1,0:T(8,128)(2,1)S(1)}, u32[]{:S(2)}, u32[]{:S(2)}) collective-permute-start(bf16[8,8960]{1,0:T(8,128)(2,1)S(1)} %get-tuple-element.115), channel_id=1, source_target_pairs={{146,0},{150,4},{154,8},{158,12},{162,16},{166,20},{170,24},{174,2... | collective-permute-start | bytes 430088 | tf_op jit(solution)/shard_map/ppermute | solution.py:395
  224.9 29.6 %collective-permute-start.14 = (bf16[8,8960]{1,0:T(8,128)(2,1)S(1)}, bf16[8,8960]{1,0:T(8,128)(2,1)S(1)}, u32[]{:S(2)}, u32[]{:S(2)}) collective-permute-start(bf16[8,8960]{1,0:T(8,128)(2,1)S(1)} %get-tuple-element.116), channel_id=1, source_target_pairs={{162,0},{166,4},{170,8},{174,12},{178,16},{182,20},{186,24},{190,2... | collective-permute-start | bytes 430088 | tf_op jit(solution)/shard_map/ppermute | solution.py:395
  227.5 29.7 %collective-permute-start.15 = (bf16[8,8960]{1,0:T(8,128)(2,1)S(1)}, bf16[8,8960]{1,0:T(8,128)(2,1)S(1)}, u32[]{:S(2)}, u32[]{:S(2)}) collective-permute-start(bf16[8,8960]{1,0:T(8,128)(2,1)S(1)} %get-tuple-element.117), channel_id=1, source_target_pairs={{178,0},{182,4},{186,8},{190,12},{130,16},{134,20},{138,24},{142,2... | collective-permute-start | bytes 430088 | tf_op jit(solution)/shard_map/ppermute | solution.py:395
  257.8 6.4 %collective-permute-start.16 = (bf16[128,2560]{1,0:T(8,128)(2,1)S(1)}, bf16[128,2560]{1,0:T(8,128)(2,1)S(1)}, u32[]{:S(2)}, u32[]{:S(2)}) collective-permute-start(bf16[128,2560]{1,0:T(8,128)(2,1)S(1)} %combine.1), channel_id=1, source_target_pairs={{1,0},{0,1},{3,2},{2,3},{5,4},{4,5},{7,6},{6,7},{9,8},{8,9},{11,10... | collective-permute-start | bytes 1966088 | tf_op jit(solution)/shard_map/ppermute | solution.py:475
  (12 other events, 50.4 us)

commit v4 on v2

--- a/solution.py
+++ b/solution.py
@@ -92,10 +92,16 @@
     line_ref[...] = token_lines(where_ref, slots_in_group(member, group_cap))
 
 
+def send_columns(block_ref, block_hbm, sems, copies, start, width):
+    columns = (slice(None), pl.ds(start, width))
+    copies.append(pltpu.make_async_copy(block_ref.at[columns], block_hbm.at[columns], sems.at[len(copies)]))
+    copies[-1].start()
+
+
 def put_blocks(block_refs, value, start):
-    value, row = value.astype(BF16), 0
+    row = 0
     for ref in block_refs:
-        ref[:, start : start + value.shape[1]] = value[row : row + ref.shape[0]]
+        ref[:, start : start + value.shape[1]] = value[row : row + ref.shape[0]].astype(BF16)
         row += ref.shape[0]
 
 
@@ -113,7 +119,9 @@
             row, first = row + 2 * SUB, None
 
 
-def dispatch_kernel(dims, where_ref, ids_ref, w_ref, g_ref, *block_refs):
+def dispatch_kernel(dims, where_ref, ids_ref, w_ref, g_ref, near_hbm, *refs):
+    *block_refs, near_ref, sems = refs
+    block_refs, copies = [near_ref, *block_refs], []
     groups, in_group, group_cap, cap = dims
     routes, _, tok = ids_ref.shape
     features, experts = g_ref.shape[1], groups * in_group
@@ -159,6 +167,7 @@
 
     def put(value, start, width):
         put_blocks(block_refs, value, start)
+        send_columns(near_ref, near_hbm, sems, copies, start, width)
 
     for n in range(SLABS):
         for c in (0, half):
@@ -169,6 +178,8 @@
         SLABS * features, half,
     )
     put(block_fields, SLABS * features + half, FIELDS)
+    for copy in copies:
+        copy.wait()
 
 
 def spread_kernel(dims, *refs):
@@ -219,9 +230,20 @@
 
 
 def gather_kernel(rows_hbm, hit_ref, *refs):
-    *block_refs, rows_ref, sems = refs
+    *block_refs, rows_ref, sems, out_sems = refs
     features, height = rows_ref.shape[1], hit_ref.shape[1] // (SLABS + 1)
     half = features // 2
+    tall = block_refs[0].shape[0] > SUB
+    if tall:
+        block_hbm, *block_refs, block_ref = block_refs
+        block_refs = [block_ref, *block_refs]
+    outs = []
+
+    def put(value, start):
+        put_blocks(block_refs, value, start)
+        if tall:
+            send_columns(block_ref, block_hbm, out_sems, outs, start, half)
+
     copies = [
         pltpu.make_async_copy(rows_hbm.at[:, pl.ds(c, half)], rows_ref.at[:, pl.ds(c, half)], sems.at[c // half])
         for c in (0, half)
@@ -233,9 +255,11 @@
         copy.wait()
         got = t_dot(hit_ref[...], rows_ref[:, c : c + half])
         for n in range(SLABS):
-            put_blocks(block_refs, got[n * height : (n + 1) * height], n * features + c)
+            put(got[n * height : (n + 1) * height], n * features + c)
         tail += half_rows(got[SLABS * height :], c > 0)
-    put_blocks(block_refs, tail, SLABS * features)
+    put(tail, SLABS * features)
+    for copy in outs:
+        copy.wait()
 
 
 def combine_kernel(*refs):
@@ -414,9 +438,14 @@
             gather_kernel,
             name=name,
             in_specs=[hbm, vmem],
-            out_specs=[vmem] * len(shapes),
+            out_specs=[hbm if h > SUB else vmem for h in shapes],
             out_shape=[array(h, wide) for h in shapes],
-            scratch_shapes=[pltpu.VMEM(rows.shape, BF16), pltpu.SemaphoreType.DMA((2,))],
+            scratch_shapes=[
+                *(pltpu.VMEM((h, wide), BF16) for h in shapes if h > SUB),
+                pltpu.VMEM(rows.shape, BF16),
+                pltpu.SemaphoreType.DMA((2,)),
+                pltpu.SemaphoreType.DMA((2 * SLABS + 1,)),
+            ],
             compiler_params=pltpu.CompilerParams(vmem_limit_bytes=20 * 2**20),
             cost_estimate=pl.CostEstimate(
                 flops=2 * hit.shape[0] * hit.shape[1] * features, bytes_accessed=2 * rows.shape[0] * features, transcendentals=0
@@ -427,12 +456,13 @@
         *values, first = lax.optimization_barrier((*values, first))
         return first, *values
 
-    ids = route_ids[0].T.reshape(routes, 1, tok)
+    ids, weights = (jnp.transpose(a, (2, 0, 1)) for a in (route_ids, route_w))
     shapes = [8 * SUB] + [SUB] * 8
     near, *others = call(
         functools.partial(dispatch_kernel, (groups, in_group, group_cap, cap)), "dispatch", 3,
-        [array(h, sent) for h in shapes], 12, 2 * deep * tok * features,
-    )(where, ids, route_w[0].T.reshape(routes, 1, tok), grad_out[0])
+        [array(h, sent) for h in shapes], 12, 2 * deep * tok * features, [hbm] + [vmem] * 8,
+        [pltpu.VMEM((8 * SUB, sent), BF16), pltpu.SemaphoreType.DMA((2 * SLABS + 2,))],
+    )(where, ids, weights, grad_out[0])
     [line] = call(
         functools.partial(lines_kernel, (groups, in_group, group_cap)), "lines", 1,
         [array(deep, tok)], 8, 4 * deep * tok * tok,

time: 264 us -> 263 us (level)
    unnamed x23 -> x27, local copies, waits for them, and re-layouts: 12.2 us -> 12.2 us
  transfers between devices with their start and end apart: 23 -> 23, of which waited for: 18 -> 19; matrix products, arithmetic and copies ran while one was open for 0% -> 0% of each run, Pallas kernels for 9% -> 9%
where the time goes in v4:
time: 263 us
  waiting for transfers between devices  115 us (44%)
  starting transfers between devices  91.2 us (35%)
  Pallas kernels  42.9 us (16%)
  local copies, waits for them, and re-layouts  12.3 us (5%)
    all_to_all x4, waiting for transfers between devices, in_groups(): lax.all_to_all(rows.reshape(in_group, -1, features), 'inner', 0, 0, tiled...  56.8 us
    ppermute x16, starting transfers between devices, hop(): lax.ppermute(b, both, routes_over(hops, dy, back))  50.8 us
    ppermute x16, waiting for transfers between devices, hop(): lax.ppermute(b, both, routes_over(hops, dy, back))  48.2 us
    all_to_all x2, starting transfers between devices, near_swap(): lax.all_to_all(block.reshape(8, SUB, width), both, 0, 0, axis_index_group...  22 us
    pallas_call x2, Pallas kernels, expert_call(): pl.pallas_call(expert_kernel, name=name, in_specs=[hbm] * 4, out_specs=[h...  20 us
    all_to_all x4, starting transfers between devices, in_groups(): lax.all_to_all(rows.reshape(in_group, -1, features), 'inner', 0, 0, tiled...  16.5 us
    unnamed x27, local copies, waits for them, and re-layouts  12.2 us
    all_to_all x2, waiting for transfers between devices, near_swap(): lax.all_to_all(block.reshape(8, SUB, width), both, 0, 0, axis_index_group...  8.48 us
  transfers between devices with their start and end apart: 23, of which 19 were waited for; matrix products, arithmetic and copies ran while one was open for 0% of the time, Pallas kernels for 9%

profile of v4, /device:TPU:1, one launch (start us, length us, event | category | flops | bytes accessed | tf_op | source)
XLA Modules:
  0.0 262.5 jit_solution(9356048863403707432)
XLA Ops:
  6.1 10.6 %all-to-all-start = ((bf16[8,8,9088]{2,1,0:T(8,128)(2,1)}), bf16[8,8,9088]{2,1,0:T(8,128)(2,1)S(1)}, u32[]{:S(2)}, u32[]{:S(2)}) async-start(bf16[8,8,9088]{2,1,0:T(8,128)(2,1)} %bitcast.9), calls=%async_computation | async-start | bytes 2326528 | tf_op jit(solution)/shard_map/all_to_all | solution.py:415
  16.7 4.9 %collective-permute-start.1 = (bf16[8,9088]{1,0:T(8,128)(2,1)S(1)}, bf16[8,9088]{1,0:T(8,128)(2,1)S(1)}, u32[]{:S(2)}, u32[]{:S(2)}) collective-permute-start(bf16[8,9088]{1,0:T(8,128)(2,1)S(1)} %get-tuple-element.54), channel_id=1, source_target_pairs={{0,80},{4,84},{8,88},{12,92},{16,96},{20,100},{24,104},{28,108},{3... | collective-permute-start | bytes 436232 | tf_op jit(solution)/shard_map/ppermute | solution.py:419
  33.4 8.5 %all-to-all-done = bf16[8,8,9088]{2,1,0:T(8,128)(2,1)S(1)} async-done(((bf16[8,8,9088]{2,1,0:T(8,128)(2,1)}), bf16[8,8,9088]{2,1,0:T(8,128)(2,1)S(1)}, u32[]{:S(2)}, u32[]{:S(2)}) %all-to-all-start) | async-done | bytes 1163296 | tf_op jit(solution)/shard_map/all_to_all | solution.py:415
  47.8 4.5 %all-to-all-start.1 = ((bf16[8,88,2560]{2,1,0:T(8,128)(2,1)}), bf16[8,88,2560]{2,1,0:T(8,128)(2,1)}, u32[]{:S(2)}, u32[]{:S(2)}) async-start(bf16[8,88,2560]{2,1,0:T(8,128)(2,1)} %bitcast.28), calls=%async_computation.1 | async-start | bytes 7208960 | tf_op jit(solution)/shard_map/all_to_all | solution.py:422
  52.3 4.3 %collective-permute-start.4 = (bf16[8,9088]{1,0:T(8,128)(2,1)S(1)}, bf16[8,9088]{1,0:T(8,128)(2,1)S(1)}, u32[]{:S(2)}, u32[]{:S(2)}) collective-permute-start(bf16[8,9088]{1,0:T(8,128)(2,1)S(1)} %get-tuple-element.62), channel_id=1, source_target_pairs={{0,130},{4,134},{8,138},{12,142},{16,146},{20,150},{24,154},{28,15... | collective-permute-start | bytes 436232 | tf_op jit(solution)/shard_map/ppermute | solution.py:419
  57.8 5.8 %collective-permute-start.6 = (bf16[8,9088]{1,0:T(8,128)(2,1)S(1)}, bf16[8,9088]{1,0:T(8,128)(2,1)S(1)}, u32[]{:S(2)}, u32[]{:S(2)}) collective-permute-start(bf16[8,9088]{1,0:T(8,128)(2,1)S(1)} %get-tuple-element.64), channel_id=1, source_target_pairs={{0,162},{4,166},{8,170},{12,174},{16,178},{20,182},{24,186},{28,19... | collective-permute-start | bytes 436232 | tf_op jit(solution)/shard_map/ppermute | solution.py:419
  66.3 6.6 %collective-permute-done.6.refs_2_ = bf16[8,9088]{1,0:T(8,128)(2,1)S(1)} collective-permute-done((bf16[8,9088]{1,0:T(8,128)(2,1)S(1)}, bf16[8,9088]{1,0:T(8,128)(2,1)S(1)}, u32[]{:S(2)}, u32[]{:S(2)}) %collective-permute-start.6) | collective-permute-done | bytes 145440 | tf_op jit(solution)/shard_map/ppermute | solution.py:419
  72.9 5.6 %collective-permute-done.7.refs_3_ = bf16[8,9088]{1,0:T(8,128)(2,1)S(1)} collective-permute-done((bf16[8,9088]{1,0:T(8,128)(2,1)S(1)}, bf16[8,9088]{1,0:T(8,128)(2,1)S(1)}, u32[]{:S(2)}, u32[]{:S(2)}) %collective-permute-start.7) | collective-permute-done | bytes 145440 | tf_op jit(solution)/shard_map/ppermute | solution.py:419
  80.1 25.5 %all-to-all-done.1 = bf16[8,88,2560]{2,1,0:T(8,128)(2,1)} async-done(((bf16[8,88,2560]{2,1,0:T(8,128)(2,1)}), bf16[8,88,2560]{2,1,0:T(8,128)(2,1)}, u32[]{:S(2)}, u32[]{:S(2)}) %all-to-all-start.1) | async-done | bytes 3604512 | tf_op jit(solution)/shard_map/all_to_all | solution.py:422
  111.1 5.2 %align.1 = (bf16[704,1536]{1,0:T(8,128)(2,1)S(1)}, bf16[256,1536]{1,0:T(8,128)(2,1)S(1)}) custom-call(s32[6]{0:T(128)S(1)} %stack.27.where_ref, bf16[896,1536]{1,0:T(8,128)(2,1)S(1)} %bitcast.32), custom_call_target="tpu_custom_call" | custom-call | flops 2642411520 | bytes 2949120 | tf_op jit(solution)/shard_map/align/pallas_call | solution.py:470
  118.6 5.8 %all-to-all-done.2 = bf16[8,32,2560]{2,1,0:T(8,128)(2,1)S(1)} async-done(((bf16[8,32,2560]{2,1,0:T(8,128)(2,1)}), bf16[8,32,2560]{2,1,0:T(8,128)(2,1)S(1)}, u32[]{:S(2)}, u32[]{:S(2)}) %all-to-all-start.2) | async-done | bytes 1310752 | tf_op jit(solution)/shard_map/all_to_all | solution.py:422
  125.5 7.6 %expert_far.1 = (bf16[256,2560]{1,0:T(8,128)(2,1)}, bf16[256,768]{1,0:T(8,128)(2,1)}) custom-call(bf16[256,2560]{1,0:T(8,128)(2,1)} %bitcast.35, bf16[256,1536]{1,0:T(8,128)(2,1)} %copy-done.1, bf16[768,2560]{1,0:T(8,128)(2,1)} %bitcast.36, bf16[2560,768]{1,0:T(8,128)(2,1)} %bitcast.38), custom_call_target="tpu_custom_call" | custom-call | flops 2013265920 | bytes 10485760 | tf_op jit(solution)/shard_map/expert_far/pallas_call | solution.py:511
  136.6 12.4 %expert_near.1 = (bf16[704,2560]{1,0:T(8,128)(2,1)}, bf16[704,768]{1,0:T(8,128)(2,1)}) custom-call(bf16[704,2560]{1,0:T(8,128)(2,1)} %bitcast.12.x_hbm, bf16[704,1536]{1,0:T(8,128)(2,1)} %copy-done.11, bf16[768,2560]{1,0:T(8,128)(2,1)} %bitcast.37, bf16[2560,768]{1,0:T(8,128)(2,1)} %bitcast.39), custom_call_target="tpu_custom_call" | custom-call | flops 5536481280 | bytes 15073280 | tf_op jit(solution)/shard_map/expert_near/pallas_call | solution.py:511
  151.8 4.6 %all-to-all-start.4 = ((bf16[8,88,2560]{2,1,0:T(8,128)(2,1)}), bf16[8,88,2560]{2,1,0:T(8,128)(2,1)}, u32[]{:S(2)}, u32[]{:S(2)}) async-start(bf16[8,88,2560]{2,1,0:T(8,128)(2,1)} %bitcast.40), calls=%async_computation.4 | async-start | bytes 7208960 | tf_op jit(solution)/shard_map/all_to_all | solution.py:422
  156.4 5.7 %collective-permute-start.8 = (bf16[8,8960]{1,0:T(8,128)(2,1)S(1)}, bf16[8,8960]{1,0:T(8,128)(2,1)S(1)}, u32[]{:S(2)}, u32[]{:S(2)}) collective-permute-start(bf16[8,8960]{1,0:T(8,128)(2,1)S(1)} %get-tuple-element.84), channel_id=1, source_target_pairs={{130,0},{134,4},{138,8},{142,12},{146,16},{150,20},{154,24},{158,2... | collective-permute-start | bytes 430088 | tf_op jit(solution)/shard_map/ppermute | solution.py:419
  165.1 4.8 %collective-permute-start.10 = (bf16[8,8960]{1,0:T(8,128)(2,1)S(1)}, bf16[8,8960]{1,0:T(8,128)(2,1)S(1)}, u32[]{:S(2)}, u32[]{:S(2)}) collective-permute-start(bf16[8,8960]{1,0:T(8,128)(2,1)S(1)} %get-tuple-element.86), channel_id=1, source_target_pairs={{162,0},{166,4},{170,8},{174,12},{178,16},{182,20},{186,24},{190,2... | collective-permute-start | bytes 430088 | tf_op jit(solution)/shard_map/ppermute | solution.py:419
  170.4 7.6 %collective-permute-done.10.refs_7_ = bf16[8,8960]{1,0:T(8,128)(2,1)S(1)} collective-permute-done((bf16[8,8960]{1,0:T(8,128)(2,1)S(1)}, bf16[8,8960]{1,0:T(8,128)(2,1)S(1)}, u32[]{:S(2)}, u32[]{:S(2)}) %collective-permute-start.10) | collective-permute-done | bytes 143392 | tf_op jit(solution)/shard_map/ppermute | solution.py:419
  178.1 4.8 %collective-permute-done.11.refs_8_ = bf16[8,8960]{1,0:T(8,128)(2,1)S(1)} collective-permute-done((bf16[8,8960]{1,0:T(8,128)(2,1)S(1)}, bf16[8,8960]{1,0:T(8,128)(2,1)S(1)}, u32[]{:S(2)}, u32[]{:S(2)}) %collective-permute-start.11) | collective-permute-done | bytes 143392 | tf_op jit(solution)/shard_map/ppermute | solution.py:419
  182.9 23.6 %all-to-all-done.4 = bf16[8,88,2560]{2,1,0:T(8,128)(2,1)} async-done(((bf16[8,88,2560]{2,1,0:T(8,128)(2,1)}), bf16[8,88,2560]{2,1,0:T(8,128)(2,1)}, u32[]{:S(2)}, u32[]{:S(2)}) %all-to-all-start.4) | async-done | bytes 3604512 | tf_op jit(solution)/shard_map/all_to_all | solution.py:422
  206.5 4.6 %gather_near.1 = (bf16[64,8960]{1,0:T(8,128)(2,1)}, bf16[8,8960]{1,0:T(8,128)(2,1)S(1)}, bf16[8,8960]{1,0:T(8,128)(2,1)S(1)}, bf16[8,8960]{1,0:T(8,128)(2,1)S(1)}, bf16[8,8960]{1,0:T(8,128)(2,1)S(1)}) custom-call(bf16[704,2560]{1,0:T(8,128)(2,1)} %bitcast.21.rows_hbm, bf16[704,384]{1,0:T(8,128)(2,1)S(1)} %copy-done.9), custom_call_target="tpu_custom_call" | custom-call | flops 1384120320 | bytes 3604480 | tf_op jit(solution)/shard_map/gather_near/pallas_call | solution.py:437
  211.1 11.4 %all-to-all-start.5 = ((bf16[8,8,8960]{2,1,0:T(8,128)(2,1)}), bf16[8,8,8960]{2,1,0:T(8,128)(2,1)S(1)}, u32[]{:S(2)}, u32[]{:S(2)}) async-start(bf16[8,8,8960]{2,1,0:T(8,128)(2,1)} %bitcast.22), calls=%async_computation.5 | async-start | bytes 2293760 | tf_op jit(solution)/shard_map/all_to_all | solution.py:415
  226.3 5.5 %collective-permute-start.13 = (bf16[8,8960]{1,0:T(8,128)(2,1)S(1)}, bf16[8,8960]{1,0:T(8,128)(2,1)S(1)}, u32[]{:S(2)}, u32[]{:S(2)}) collective-permute-start(bf16[8,8960]{1,0:T(8,128)(2,1)S(1)} %get-tuple-element.93), channel_id=1, source_target_pairs={{80,0},{84,4},{88,8},{92,12},{96,16},{100,20},{104,24},{108,28},{1... | collective-permute-start | bytes 430088 | tf_op jit(solution)/shard_map/ppermute | solution.py:419
  231.7 4.7 %collective-permute-start.14 = (bf16[8,8960]{1,0:T(8,128)(2,1)S(1)}, bf16[8,8960]{1,0:T(8,128)(2,1)S(1)}, u32[]{:S(2)}, u32[]{:S(2)}) collective-permute-start(bf16[8,8960]{1,0:T(8,128)(2,1)S(1)} %get-tuple-element.94), channel_id=1, source_target_pairs={{96,0},{100,4},{104,8},{108,12},{112,16},{116,20},{120,24},{124,28... | collective-permute-start | bytes 430088 | tf_op jit(solution)/shard_map/ppermute | solution.py:419
  250.0 4.6 %collective-permute-done.14.refs_3_ = bf16[8,8960]{1,0:T(8,128)(2,1)S(1)} collective-permute-done((bf16[8,8960]{1,0:T(8,128)(2,1)S(1)}, bf16[8,8960]{1,0:T(8,128)(2,1)S(1)}, u32[]{:S(2)}, u32[]{:S(2)}) %collective-permute-start.14) | collective-permute-done | bytes 143392 | tf_op jit(solution)/shard_map/ppermute | solution.py:419
  (61 shorter events, 72.4 us)
Async XLA Ops:
  6.1 35.8 %all-to-all-start = ((bf16[8,8,9088]{2,1,0:T(8,128)(2,1)}), bf16[8,8,9088]{2,1,0:T(8,128)(2,1)S(1)}, u32[]{:S(2)}, u32[]{:S(2)}) async-start(bf16[8,8,9088]{2,1,0:T(8,128)(2,1)} %bitcast.9), calls=%async_computation | async-start | bytes 2326528 | tf_op jit(solution)/shard_map/all_to_all | solution.py:415
  16.7 9.9 %collective-permute-start = (bf16[8,9088]{1,0:T(8,128)(2,1)S(1)}, bf16[8,9088]{1,0:T(8,128)(2,1)S(1)}, u32[]{:S(2)}, u32[]{:S(2)}) collective-permute-start(bf16[8,9088]{1,0:T(8,128)(2,1)S(1)} %get-tuple-element.53), channel_id=1, source_target_pairs={{0,64},{4,68},{8,72},{12,76},{16,80},{20,84},{24,88},{28,92},{32,9... | collective-permute-start | bytes 436232 | tf_op jit(solution)/shard_map/ppermute | solution.py:419
  16.7 11.2 %collective-permute-start.1 = (bf16[8,9088]{1,0:T(8,128)(2,1)S(1)}, bf16[8,9088]{1,0:T(8,128)(2,1)S(1)}, u32[]{:S(2)}, u32[]{:S(2)}) collective-permute-start(bf16[8,9088]{1,0:T(8,128)(2,1)S(1)} %get-tuple-element.54), channel_id=1, source_target_pairs={{0,80},{4,84},{8,88},{12,92},{16,96},{20,100},{24,104},{28,108},{3... | collective-permute-start | bytes 436232 | tf_op jit(solution)/shard_map/ppermute | solution.py:419
  21.6 10.4 %collective-permute-start.2 = (bf16[8,9088]{1,0:T(8,128)(2,1)S(1)}, bf16[8,9088]{1,0:T(8,128)(2,1)S(1)}, u32[]{:S(2)}, u32[]{:S(2)}) collective-permute-start(bf16[8,9088]{1,0:T(8,128)(2,1)S(1)} %get-tuple-element.55), channel_id=1, source_target_pairs={{0,96},{4,100},{8,104},{12,108},{16,112},{20,116},{24,120},{28,124... | collective-permute-start | bytes 436232 | tf_op jit(solution)/shard_map/ppermute | solution.py:419
  23.7 9.7 %collective-permute-start.3 = (bf16[8,9088]{1,0:T(8,128)(2,1)S(1)}, bf16[8,9088]{1,0:T(8,128)(2,1)S(1)}, u32[]{:S(2)}, u32[]{:S(2)}) collective-permute-start(bf16[8,9088]{1,0:T(8,128)(2,1)S(1)} %get-tuple-element.56), channel_id=1, source_target_pairs={{0,112},{4,116},{8,120},{12,124},{16,64},{20,68},{24,72},{28,76},{... | collective-permute-start | bytes 436232 | tf_op jit(solution)/shard_map/ppermute | solution.py:419
  47.8 57.7 %all-to-all-start.1 = ((bf16[8,88,2560]{2,1,0:T(8,128)(2,1)}), bf16[8,88,2560]{2,1,0:T(8,128)(2,1)}, u32[]{:S(2)}, u32[]{:S(2)}) async-start(bf16[8,88,2560]{2,1,0:T(8,128)(2,1)} %bitcast.28), calls=%async_computation.1 | async-start | bytes 7208960 | tf_op jit(solution)/shard_map/all_to_all | solution.py:422
  52.3 12.9 %collective-permute-start.4 = (bf16[8,9088]{1,0:T(8,128)(2,1)S(1)}, bf16[8,9088]{1,0:T(8,128)(2,1)S(1)}, u32[]{:S(2)}, u32[]{:S(2)}) collective-permute-start(bf16[8,9088]{1,0:T(8,128)(2,1)S(1)} %get-tuple-element.62), channel_id=1, source_target_pairs={{0,130},{4,134},{8,138},{12,142},{16,146},{20,150},{24,154},{28,15... | collective-permute-start | bytes 436232 | tf_op jit(solution)/shard_map/ppermute | solution.py:419
  56.7 9.6 %collective-permute-start.5 = (bf16[8,9088]{1,0:T(8,128)(2,1)S(1)}, bf16[8,9088]{1,0:T(8,128)(2,1)S(1)}, u32[]{:S(2)}, u32[]{:S(2)}) collective-permute-start(bf16[8,9088]{1,0:T(8,128)(2,1)S(1)} %get-tuple-element.63), channel_id=1, source_target_pairs={{0,146},{4,150},{8,154},{12,158},{16,162},{20,166},{24,170},{28,17... | collective-permute-start | bytes 436232 | tf_op jit(solution)/shard_map/ppermute | solution.py:419
  57.8 15.1 %collective-permute-start.6 = (bf16[8,9088]{1,0:T(8,128)(2,1)S(1)}, bf16[8,9088]{1,0:T(8,128)(2,1)S(1)}, u32[]{:S(2)}, u32[]{:S(2)}) collective-permute-start(bf16[8,9088]{1,0:T(8,128)(2,1)S(1)} %get-tuple-element.64), channel_id=1, source_target_pairs={{0,162},{4,166},{8,170},{12,174},{16,178},{20,182},{24,186},{28,19... | collective-permute-start | bytes 436232 | tf_op jit(solution)/shard_map/ppermute | solution.py:419
  63.7 14.8 %collective-permute-start.7 = (bf16[8,9088]{1,0:T(8,128)(2,1)S(1)}, bf16[8,9088]{1,0:T(8,128)(2,1)S(1)}, u32[]{:S(2)}, u32[]{:S(2)}) collective-permute-start(bf16[8,9088]{1,0:T(8,128)(2,1)S(1)} %get-tuple-element.65), channel_id=1, source_target_pairs={{0,178},{4,182},{8,186},{12,190},{16,130},{20,134},{24,138},{28,14... | collective-permute-start | bytes 436232 | tf_op jit(solution)/shard_map/ppermute | solution.py:419
  105.6 18.9 %all-to-all-start.2 = ((bf16[8,32,2560]{2,1,0:T(8,128)(2,1)}), bf16[8,32,2560]{2,1,0:T(8,128)(2,1)S(1)}, u32[]{:S(2)}, u32[]{:S(2)}) async-start(bf16[8,32,2560]{2,1,0:T(8,128)(2,1)} %bitcast.13), calls=%async_computation.2 | async-start | bytes 2621440 | tf_op jit(solution)/shard_map/all_to_all | solution.py:422
  133.1 17.9 %all-to-all-start.3 = ((bf16[8,32,2560]{2,1,0:T(8,128)(2,1)}), bf16[8,32,2560]{2,1,0:T(8,128)(2,1)S(1)}, u32[]{:S(2)}, u32[]{:S(2)}) async-start(bf16[8,32,2560]{2,1,0:T(8,128)(2,1)} %bitcast.41), calls=%async_computation.3 | async-start | bytes 2621440 | tf_op jit(solution)/shard_map/all_to_all | solution.py:422
  151.8 54.7 %copy-start.9 = (bf16[704,384]{1,0:T(8,128)(2,1)S(1)}, bf16[704,384]{1,0:T(8,128)(2,1)}, u32[]{:S(2)}) copy-start(bf16[704,384]{1,0:T(8,128)(2,1)} %copy-done.8) | copy-start | bytes 1622020
  151.8 54.7 %all-to-all-start.4 = ((bf16[8,88,2560]{2,1,0:T(8,128)(2,1)}), bf16[8,88,2560]{2,1,0:T(8,128)(2,1)}, u32[]{:S(2)}, u32[]{:S(2)}) async-start(bf16[8,88,2560]{2,1,0:T(8,128)(2,1)} %bitcast.40), calls=%async_computation.4 | async-start | bytes 7208960 | tf_op jit(solution)/shard_map/all_to_all | solution.py:422
  156.4 13.8 %collective-permute-start.8 = (bf16[8,8960]{1,0:T(8,128)(2,1)S(1)}, bf16[8,8960]{1,0:T(8,128)(2,1)S(1)}, u32[]{:S(2)}, u32[]{:S(2)}) collective-permute-start(bf16[8,8960]{1,0:T(8,128)(2,1)S(1)} %get-tuple-element.84), channel_id=1, source_target_pairs={{130,0},{134,4},{138,8},{142,12},{146,16},{150,20},{154,24},{158,2... | collective-permute-start | bytes 430088 | tf_op jit(solution)/shard_map/ppermute | solution.py:419
  162.1 8.3 %collective-permute-start.9 = (bf16[8,8960]{1,0:T(8,128)(2,1)S(1)}, bf16[8,8960]{1,0:T(8,128)(2,1)S(1)}, u32[]{:S(2)}, u32[]{:S(2)}) collective-permute-start(bf16[8,8960]{1,0:T(8,128)(2,1)S(1)} %get-tuple-element.85), channel_id=1, source_target_pairs={{146,0},{150,4},{154,8},{158,12},{162,16},{166,20},{170,24},{174,2... | collective-permute-start | bytes 430088 | tf_op jit(solution)/shard_map/ppermute | solution.py:419
  165.1 13.0 %collective-permute-start.10 = (bf16[8,8960]{1,0:T(8,128)(2,1)S(1)}, bf16[8,8960]{1,0:T(8,128)(2,1)S(1)}, u32[]{:S(2)}, u32[]{:S(2)}) collective-permute-start(bf16[8,8960]{1,0:T(8,128)(2,1)S(1)} %get-tuple-element.86), channel_id=1, source_target_pairs={{162,0},{166,4},{170,8},{174,12},{178,16},{182,20},{186,24},{190,2... | collective-permute-start | bytes 430088 | tf_op jit(solution)/shard_map/ppermute | solution.py:419
  169.9 13.0 %collective-permute-start.11 = (bf16[8,8960]{1,0:T(8,128)(2,1)S(1)}, bf16[8,8960]{1,0:T(8,128)(2,1)S(1)}, u32[]{:S(2)}, u32[]{:S(2)}) collective-permute-start(bf16[8,8960]{1,0:T(8,128)(2,1)S(1)} %get-tuple-element.87), channel_id=1, source_target_pairs={{178,0},{182,4},{186,8},{190,12},{130,16},{134,20},{138,24},{142,2... | collective-permute-start | bytes 430088 | tf_op jit(solution)/shard_map/ppermute | solution.py:419
  211.1 46.3 %all-to-all-start.5 = ((bf16[8,8,8960]{2,1,0:T(8,128)(2,1)}), bf16[8,8,8960]{2,1,0:T(8,128)(2,1)S(1)}, u32[]{:S(2)}, u32[]{:S(2)}) async-start(bf16[8,8,8960]{2,1,0:T(8,128)(2,1)} %bitcast.22), calls=%async_computation.5 | async-start | bytes 2293760 | tf_op jit(solution)/shard_map/all_to_all | solution.py:415
  222.4 23.7 %collective-permute-start.12 = (bf16[8,8960]{1,0:T(8,128)(2,1)S(1)}, bf16[8,8960]{1,0:T(8,128)(2,1)S(1)}, u32[]{:S(2)}, u32[]{:S(2)}) collective-permute-start(bf16[8,8960]{1,0:T(8,128)(2,1)S(1)} %get-tuple-element.92), channel_id=1, source_target_pairs={{64,0},{68,4},{72,8},{76,12},{80,16},{84,20},{88,24},{92,28},{96,3... | collective-permute-start | bytes 430088 | tf_op jit(solution)/shard_map/ppermute | solution.py:419
  226.3 23.8 %collective-permute-start.13 = (bf16[8,8960]{1,0:T(8,128)(2,1)S(1)}, bf16[8,8960]{1,0:T(8,128)(2,1)S(1)}, u32[]{:S(2)}, u32[]{:S(2)}) collective-permute-start(bf16[8,8960]{1,0:T(8,128)(2,1)S(1)} %get-tuple-element.93), channel_id=1, source_target_pairs={{80,0},{84,4},{88,8},{92,12},{96,16},{100,20},{104,24},{108,28},{1... | collective-permute-start | bytes 430088 | tf_op jit(solution)/shard_map/ppermute | solution.py:419
  231.7 22.9 %collective-permute-start.14 = (bf16[8,8960]{1,0:T(8,128)(2,1)S(1)}, bf16[8,8960]{1,0:T(8,128)(2,1)S(1)}, u32[]{:S(2)}, u32[]{:S(2)}) collective-permute-start(bf16[8,8960]{1,0:T(8,128)(2,1)S(1)} %get-tuple-element.94), channel_id=1, source_target_pairs={{96,0},{100,4},{104,8},{108,12},{112,16},{116,20},{120,24},{124,28... | collective-permute-start | bytes 430088 | tf_op jit(solution)/shard_map/ppermute | solution.py:419
  236.4 21.0 %collective-permute-start.15 = (bf16[8,8960]{1,0:T(8,128)(2,1)S(1)}, bf16[8,8960]{1,0:T(8,128)(2,1)S(1)}, u32[]{:S(2)}, u32[]{:S(2)}) collective-permute-start(bf16[8,8960]{1,0:T(8,128)(2,1)S(1)} %get-tuple-element.95), channel_id=1, source_target_pairs={{112,0},{116,4},{120,8},{124,12},{64,16},{68,20},{72,24},{76,28},{... | collective-permute-start | bytes 430088 | tf_op jit(solution)/shard_map/ppermute | solution.py:419
  258.0 3.7 %collective-permute-start.16 = (bf16[128,2560]{1,0:T(8,128)(2,1)S(1)}, bf16[128,2560]{1,0:T(8,128)(2,1)S(1)}, u32[]{:S(2)}, u32[]{:S(2)}) collective-permute-start(bf16[128,2560]{1,0:T(8,128)(2,1)S(1)} %combine.1), channel_id=1, source_target_pairs={{1,0},{0,1},{3,2},{2,3},{5,4},{4,5},{7,6},{6,7},{9,8},{8,9},{11,10... | collective-permute-start | bytes 1966088 | tf_op jit(solution)/shard_map/ppermute | solution.py:503
  (12 other events, 63.5 us)

commit v5 on v4

--- a/solution.py
+++ b/solution.py
@@ -313,7 +313,7 @@
     out_ref[...] = total.astype(BF16)
 
 
-def expert_kernel(x_hbm, kept_hbm, wd_hbm, wu_hbm, out_hbm, gate_hbm, x_ref, kept_ref, wd_ref, wu_ref, up_ref, out_ref, gate_ref, sems):
+def expert_kernel(held, x_hbm, kept_hbm, wd_hbm, wu_hbm, out_hbm, gate_hbm, x_ref, kept_ref, wd_ref, wu_ref, up_ref, out_ref, gate_ref, sems):
     hidden, features = wd_ref.shape
     rows = x_ref.shape[0]
     step, wide, tall = hidden // 3, features // 5, rows // 2 if rows > 256 else rows
@@ -323,15 +323,17 @@
         return pltpu.make_async_copy(source.at[index], target.at[index], sems.at[next(count)])
 
     tops = [pl.ds(r, tall) for r in range(0, rows, tall)]
-    x = [copy(x_hbm, x_ref, t) for t in tops]
+    x = [] if held else [copy(x_hbm, x_ref, t) for t in tops]
+    x_ref = x_hbm if held else x_ref
     kept = [copy(kept_hbm, kept_ref, t) for t in tops]
     down = [copy(wd_hbm, wd_ref, pl.ds(n, step)) for n in range(0, hidden, step)]
     up = [copy(wu_hbm, wu_ref, pl.ds(n, wide)) for n in range(0, features, wide)]
-    for c in (x[0], down[0], kept[0], *down[1:], *x[1:], *kept[1:], *up):
+    for c in (*x[:1], down[0], kept[0], *down[1:], *x[1:], *kept[1:], *up):
         c.start()
     out = []
     for i, r in enumerate(range(0, rows, tall)):
-        x[i].wait()
+        if not held:
+            x[i].wait()
         for j, n in enumerate(range(0, hidden, step)):
             if i == 0:
                 down[j].wait()
@@ -507,11 +509,12 @@
 def expert_call(name, rows, kept, w_down, w_up):
     hidden, features = w_down.shape
     height = rows.shape[0]
-    hbm = pl.BlockSpec(memory_space=pltpu.HBM)
+    vmem, hbm = pl.BlockSpec(memory_space=pltpu.VMEM), pl.BlockSpec(memory_space=pltpu.HBM)
+    held = height <= 256
     return pl.pallas_call(
-        expert_kernel,
+        functools.partial(expert_kernel, held),
         name=name,
-        in_specs=[hbm] * 4,
+        in_specs=[vmem if held else hbm] + [hbm] * 3,
         out_specs=[hbm] * 2,
         out_shape=[jax.ShapeDtypeStruct((height, features), BF16), jax.ShapeDtypeStruct((height, hidden), BF16)],
         scratch_shapes=[
@@ -524,7 +527,7 @@
             pltpu.VMEM((height, hidden), BF16),
             pltpu.SemaphoreType.DMA((19,)),
         ],
-        compiler_params=pltpu.CompilerParams(vmem_limit_bytes=56 * 2**20),
+        compiler_params=pltpu.CompilerParams(vmem_limit_bytes=(51 if held else 56) * 2**20),
         cost_estimate=pl.CostEstimate(
             flops=4 * height * features * hidden, bytes_accessed=4 * (height + hidden) * features, transcendentals=0
         ),

time: 263 us -> 263 us (level)
    all_to_all x4, waiting for transfers between devices: 56.8 us -> 59.9 us  [in_groups(): lax.all_to_all(rows.reshape(in_group, -1, features), 'inner', 0, 0, tiled...]
    unnamed x27 -> x21, local copies, waits for them, and re-layouts: 12.2 us -> 10.3 us
where the time goes in v5:
time: 263 us; the launch traced here: 262 us
  waiting for transfers between devices  116 us (44%)
  starting transfers between devices  90.7 us (34%)
  Pallas kernels  44 us (17%)
  local copies, waits for them, and re-layouts  10.4 us (4%)
    all_to_all x4, waiting for transfers between devices, in_groups(): lax.all_to_all(rows.reshape(in_group, -1, features), 'inner', 0, 0, tiled...  59.9 us
    ppermute x16, starting transfers between devices, hop(): lax.ppermute(b, both, routes_over(hops, dy, back))  48.9 us
    ppermute x16, waiting for transfers between devices, hop(): lax.ppermute(b, both, routes_over(hops, dy, back))  45.9 us
    all_to_all x2, starting transfers between devices, near_swap(): lax.all_to_all(block.reshape(8, SUB, width), both, 0, 0, axis_index_group...  22.3 us
    pallas_call x2, Pallas kernels, expert_call(): pl.pallas_call(functools.partial(expert_kernel, held), name=name, in_spec...  21.1 us
    all_to_all x4, starting transfers between devices, in_groups(): lax.all_to_all(rows.reshape(in_group, -1, features), 'inner', 0, 0, tiled...  17.1 us
    unnamed x21, local copies, waits for them, and re-layouts  10.3 us
    all_to_all x2, waiting for transfers between devices, near_swap(): lax.all_to_all(block.reshape(8, SUB, width), both, 0, 0, axis_index_group...  8.48 us
  transfers between devices with their start and end apart: 23, of which 19 were waited for; matrix products, arithmetic and copies ran while one was open for 0% of the time, Pallas kernels for 9%

profile of v5, /device:TPU:1, one launch (start us, length us, event | category | flops | bytes accessed | tf_op | source)
XLA Modules:
  0.0 262.0 jit_solution(12748478311485441289)
XLA Ops:
  6.1 10.6 %all-to-all-start = ((bf16[8,8,9088]{2,1,0:T(8,128)(2,1)}), bf16[8,8,9088]{2,1,0:T(8,128)(2,1)S(1)}, u32[]{:S(2)}, u32[]{:S(2)}) async-start(bf16[8,8,9088]{2,1,0:T(8,128)(2,1)} %bitcast.9), calls=%async_computation | async-start | bytes 2326528 | tf_op jit(solution)/shard_map/all_to_all | solution.py:417
  16.7 4.9 %collective-permute-start.1 = (bf16[8,9088]{1,0:T(8,128)(2,1)S(1)}, bf16[8,9088]{1,0:T(8,128)(2,1)S(1)}, u32[]{:S(2)}, u32[]{:S(2)}) collective-permute-start(bf16[8,9088]{1,0:T(8,128)(2,1)S(1)} %get-tuple-element.54), channel_id=1, source_target_pairs={{0,80},{4,84},{8,88},{12,92},{16,96},{20,100},{24,104},{28,108},{3... | collective-permute-start | bytes 436232 | tf_op jit(solution)/shard_map/ppermute | solution.py:421
  33.4 8.5 %all-to-all-done = bf16[8,8,9088]{2,1,0:T(8,128)(2,1)S(1)} async-done(((bf16[8,8,9088]{2,1,0:T(8,128)(2,1)}), bf16[8,8,9088]{2,1,0:T(8,128)(2,1)S(1)}, u32[]{:S(2)}, u32[]{:S(2)}) %all-to-all-start) | async-done | bytes 1163296 | tf_op jit(solution)/shard_map/all_to_all | solution.py:417
  47.8 4.5 %all-to-all-start.1 = ((bf16[8,88,2560]{2,1,0:T(8,128)(2,1)}), bf16[8,88,2560]{2,1,0:T(8,128)(2,1)}, u32[]{:S(2)}, u32[]{:S(2)}) async-start(bf16[8,88,2560]{2,1,0:T(8,128)(2,1)} %bitcast.28), calls=%async_computation.1 | async-start | bytes 7208960 | tf_op jit(solution)/shard_map/all_to_all | solution.py:424
  52.3 4.4 %collective-permute-start.4 = (bf16[8,9088]{1,0:T(8,128)(2,1)S(1)}, bf16[8,9088]{1,0:T(8,128)(2,1)S(1)}, u32[]{:S(2)}, u32[]{:S(2)}) collective-permute-start(bf16[8,9088]{1,0:T(8,128)(2,1)S(1)} %get-tuple-element.62), channel_id=1, source_target_pairs={{0,130},{4,134},{8,138},{12,142},{16,146},{20,150},{24,154},{28,15... | collective-permute-start | bytes 436232 | tf_op jit(solution)/shard_map/ppermute | solution.py:421
  57.8 5.8 %collective-permute-start.6 = (bf16[8,9088]{1,0:T(8,128)(2,1)S(1)}, bf16[8,9088]{1,0:T(8,128)(2,1)S(1)}, u32[]{:S(2)}, u32[]{:S(2)}) collective-permute-start(bf16[8,9088]{1,0:T(8,128)(2,1)S(1)} %get-tuple-element.64), channel_id=1, source_target_pairs={{0,162},{4,166},{8,170},{12,174},{16,178},{20,182},{24,186},{28,19... | collective-permute-start | bytes 436232 | tf_op jit(solution)/shard_map/ppermute | solution.py:421
  66.3 6.7 %collective-permute-done.6.refs_2_ = bf16[8,9088]{1,0:T(8,128)(2,1)S(1)} collective-permute-done((bf16[8,9088]{1,0:T(8,128)(2,1)S(1)}, bf16[8,9088]{1,0:T(8,128)(2,1)S(1)}, u32[]{:S(2)}, u32[]{:S(2)}) %collective-permute-start.6) | collective-permute-done | bytes 145440 | tf_op jit(solution)/shard_map/ppermute | solution.py:421
  72.9 5.5 %collective-permute-done.7.refs_3_ = bf16[8,9088]{1,0:T(8,128)(2,1)S(1)} collective-permute-done((bf16[8,9088]{1,0:T(8,128)(2,1)S(1)}, bf16[8,9088]{1,0:T(8,128)(2,1)S(1)}, u32[]{:S(2)}, u32[]{:S(2)}) %collective-permute-start.7) | collective-permute-done | bytes 145440 | tf_op jit(solution)/shard_map/ppermute | solution.py:421
  80.0 25.5 %all-to-all-done.1 = bf16[8,88,2560]{2,1,0:T(8,128)(2,1)} async-done(((bf16[8,88,2560]{2,1,0:T(8,128)(2,1)}), bf16[8,88,2560]{2,1,0:T(8,128)(2,1)}, u32[]{:S(2)}, u32[]{:S(2)}) %all-to-all-start.1) | async-done | bytes 3604512 | tf_op jit(solution)/shard_map/all_to_all | solution.py:424
  105.5 4.4 %all-to-all-start.2 = ((bf16[8,32,2560]{2,1,0:T(8,128)(2,1)}), bf16[8,32,2560]{2,1,0:T(8,128)(2,1)}, u32[]{:S(2)}, u32[]{:S(2)}) async-start(bf16[8,32,2560]{2,1,0:T(8,128)(2,1)} %bitcast.13), calls=%async_computation.2 | async-start | bytes 2621440 | tf_op jit(solution)/shard_map/all_to_all | solution.py:424
  111.8 5.2 %align.1 = (bf16[704,1536]{1,0:T(8,128)(2,1)S(1)}, bf16[256,1536]{1,0:T(8,128)(2,1)S(1)}) custom-call(s32[6]{0:T(128)S(1)} %stack.27.where_ref, bf16[896,1536]{1,0:T(8,128)(2,1)S(1)} %bitcast.32), custom_call_target="tpu_custom_call" | custom-call | flops 2642411520 | bytes 2949120 | tf_op jit(solution)/shard_map/align/pallas_call | solution.py:472
  118.4 6.8 %all-to-all-done.2 = bf16[8,32,2560]{2,1,0:T(8,128)(2,1)} async-done(((bf16[8,32,2560]{2,1,0:T(8,128)(2,1)}), bf16[8,32,2560]{2,1,0:T(8,128)(2,1)}, u32[]{:S(2)}, u32[]{:S(2)}) %all-to-all-start.2) | async-done | bytes 1310752 | tf_op jit(solution)/shard_map/all_to_all | solution.py:424
  125.2 8.6 %expert_far.1 = (bf16[256,2560]{1,0:T(8,128)(2,1)}, bf16[256,768]{1,0:T(8,128)(2,1)S(1)}) custom-call(bf16[256,2560]{1,0:T(8,128)(2,1)} %bitcast.14.x_hbm, bf16[256,1536]{1,0:T(8,128)(2,1)S(1)} %get-tuple-element.74.kept_hbm, bf16[768,2560]{1,0:T(8,128)(2,1)} %bitcast.35, bf16[2560,768]{1,0:T(8,128)(2,1)} %bitcast.37), custom_call_target="tpu_custom_call" | custom-call | flops 2013265920 | bytes 10485760 | tf_op jit(solution)/shard_map/expert_far/pallas_call | solution.py:514
  137.4 12.5 %expert_near.1 = (bf16[704,2560]{1,0:T(8,128)(2,1)}, bf16[704,768]{1,0:T(8,128)(2,1)}) custom-call(bf16[704,2560]{1,0:T(8,128)(2,1)} %bitcast.12.x_hbm, bf16[704,1536]{1,0:T(8,128)(2,1)} %copy-done.9, bf16[768,2560]{1,0:T(8,128)(2,1)} %bitcast.36, bf16[2560,768]{1,0:T(8,128)(2,1)} %bitcast.38), custom_call_target="tpu_custom_call" | custom-call | flops 5536481280 | bytes 15073280 | tf_op jit(solution)/shard_map/expert_near/pallas_call | solution.py:514
  152.5 4.6 %all-to-all-start.4 = ((bf16[8,88,2560]{2,1,0:T(8,128)(2,1)}), bf16[8,88,2560]{2,1,0:T(8,128)(2,1)}, u32[]{:S(2)}, u32[]{:S(2)}) async-start(bf16[8,88,2560]{2,1,0:T(8,128)(2,1)} %bitcast.39), calls=%async_computation.4 | async-start | bytes 7208960 | tf_op jit(solution)/shard_map/all_to_all | solution.py:424
  157.2 5.8 %collective-permute-start.8 = (bf16[8,8960]{1,0:T(8,128)(2,1)S(1)}, bf16[8,8960]{1,0:T(8,128)(2,1)S(1)}, u32[]{:S(2)}, u32[]{:S(2)}) collective-permute-start(bf16[8,8960]{1,0:T(8,128)(2,1)S(1)} %get-tuple-element.84), channel_id=1, source_target_pairs={{130,0},{134,4},{138,8},{142,12},{146,16},{150,20},{154,24},{158,2... | collective-permute-start | bytes 430088 | tf_op jit(solution)/shard_map/ppermute | solution.py:421
  171.3 5.0 %collective-permute-done.10.refs_7_ = bf16[8,8960]{1,0:T(8,128)(2,1)S(1)} collective-permute-done((bf16[8,8960]{1,0:T(8,128)(2,1)S(1)}, bf16[8,8960]{1,0:T(8,128)(2,1)S(1)}, u32[]{:S(2)}, u32[]{:S(2)}) %collective-permute-start.10) | collective-permute-done | bytes 143392 | tf_op jit(solution)/shard_map/ppermute | solution.py:421
  176.3 5.2 %collective-permute-done.11.refs_8_ = bf16[8,8960]{1,0:T(8,128)(2,1)S(1)} collective-permute-done((bf16[8,8960]{1,0:T(8,128)(2,1)S(1)}, bf16[8,8960]{1,0:T(8,128)(2,1)S(1)}, u32[]{:S(2)}, u32[]{:S(2)}) %collective-permute-start.11) | collective-permute-done | bytes 143392 | tf_op jit(solution)/shard_map/ppermute | solution.py:421
  181.5 25.7 %all-to-all-done.4 = bf16[8,88,2560]{2,1,0:T(8,128)(2,1)} async-done(((bf16[8,88,2560]{2,1,0:T(8,128)(2,1)}), bf16[8,88,2560]{2,1,0:T(8,128)(2,1)}, u32[]{:S(2)}, u32[]{:S(2)}) %all-to-all-start.4) | async-done | bytes 3604512 | tf_op jit(solution)/shard_map/all_to_all | solution.py:424
  207.2 4.6 %gather_near.1 = (bf16[64,8960]{1,0:T(8,128)(2,1)}, bf16[8,8960]{1,0:T(8,128)(2,1)S(1)}, bf16[8,8960]{1,0:T(8,128)(2,1)S(1)}, bf16[8,8960]{1,0:T(8,128)(2,1)S(1)}, bf16[8,8960]{1,0:T(8,128)(2,1)S(1)}) custom-call(bf16[704,2560]{1,0:T(8,128)(2,1)} %bitcast.21.rows_hbm, bf16[704,384]{1,0:T(8,128)(2,1)S(1)} %copy-done.7), custom_call_target="tpu_custom_call" | custom-call | flops 1384120320 | bytes 3604480 | tf_op jit(solution)/shard_map/gather_near/pallas_call | solution.py:439
  211.8 11.7 %all-to-all-start.5 = ((bf16[8,8,8960]{2,1,0:T(8,128)(2,1)}), bf16[8,8,8960]{2,1,0:T(8,128)(2,1)S(1)}, u32[]{:S(2)}, u32[]{:S(2)}) async-start(bf16[8,8,8960]{2,1,0:T(8,128)(2,1)} %bitcast.22), calls=%async_computation.5 | async-start | bytes 2293760 | tf_op jit(solution)/shard_map/all_to_all | solution.py:417
  223.5 4.4 %collective-permute-start.12 = (bf16[8,8960]{1,0:T(8,128)(2,1)S(1)}, bf16[8,8960]{1,0:T(8,128)(2,1)S(1)}, u32[]{:S(2)}, u32[]{:S(2)}) collective-permute-start(bf16[8,8960]{1,0:T(8,128)(2,1)S(1)} %get-tuple-element.92), channel_id=1, source_target_pairs={{64,0},{68,4},{72,8},{76,12},{80,16},{84,20},{88,24},{92,28},{96,3... | collective-permute-start | bytes 430088 | tf_op jit(solution)/shard_map/ppermute | solution.py:421
  227.9 4.4 %collective-permute-start.13 = (bf16[8,8960]{1,0:T(8,128)(2,1)S(1)}, bf16[8,8960]{1,0:T(8,128)(2,1)S(1)}, u32[]{:S(2)}, u32[]{:S(2)}) collective-permute-start(bf16[8,8960]{1,0:T(8,128)(2,1)S(1)} %get-tuple-element.93), channel_id=1, source_target_pairs={{80,0},{84,4},{88,8},{92,12},{96,16},{100,20},{104,24},{108,28},{1... | collective-permute-start | bytes 430088 | tf_op jit(solution)/shard_map/ppermute | solution.py:421
  248.9 4.6 %collective-permute-done.14.refs_3_ = bf16[8,8960]{1,0:T(8,128)(2,1)S(1)} collective-permute-done((bf16[8,8960]{1,0:T(8,128)(2,1)S(1)}, bf16[8,8960]{1,0:T(8,128)(2,1)S(1)}, u32[]{:S(2)}, u32[]{:S(2)}) %collective-permute-start.14) | collective-permute-done | bytes 143392 | tf_op jit(solution)/shard_map/ppermute | solution.py:421
  (55 shorter events, 71.2 us)
Async XLA Ops:
  6.1 35.8 %all-to-all-start = ((bf16[8,8,9088]{2,1,0:T(8,128)(2,1)}), bf16[8,8,9088]{2,1,0:T(8,128)(2,1)S(1)}, u32[]{:S(2)}, u32[]{:S(2)}) async-start(bf16[8,8,9088]{2,1,0:T(8,128)(2,1)} %bitcast.9), calls=%async_computation | async-start | bytes 2326528 | tf_op jit(solution)/shard_map/all_to_all | solution.py:417
  16.7 9.9 %collective-permute-start = (bf16[8,9088]{1,0:T(8,128)(2,1)S(1)}, bf16[8,9088]{1,0:T(8,128)(2,1)S(1)}, u32[]{:S(2)}, u32[]{:S(2)}) collective-permute-start(bf16[8,9088]{1,0:T(8,128)(2,1)S(1)} %get-tuple-element.53), channel_id=1, source_target_pairs={{0,64},{4,68},{8,72},{12,76},{16,80},{20,84},{24,88},{28,92},{32,9... | collective-permute-start | bytes 436232 | tf_op jit(solution)/shard_map/ppermute | solution.py:421
  16.7 11.2 %collective-permute-start.1 = (bf16[8,9088]{1,0:T(8,128)(2,1)S(1)}, bf16[8,9088]{1,0:T(8,128)(2,1)S(1)}, u32[]{:S(2)}, u32[]{:S(2)}) collective-permute-start(bf16[8,9088]{1,0:T(8,128)(2,1)S(1)} %get-tuple-element.54), channel_id=1, source_target_pairs={{0,80},{4,84},{8,88},{12,92},{16,96},{20,100},{24,104},{28,108},{3... | collective-permute-start | bytes 436232 | tf_op jit(solution)/shard_map/ppermute | solution.py:421
  21.6 10.4 %collective-permute-start.2 = (bf16[8,9088]{1,0:T(8,128)(2,1)S(1)}, bf16[8,9088]{1,0:T(8,128)(2,1)S(1)}, u32[]{:S(2)}, u32[]{:S(2)}) collective-permute-start(bf16[8,9088]{1,0:T(8,128)(2,1)S(1)} %get-tuple-element.55), channel_id=1, source_target_pairs={{0,96},{4,100},{8,104},{12,108},{16,112},{20,116},{24,120},{28,124... | collective-permute-start | bytes 436232 | tf_op jit(solution)/shard_map/ppermute | solution.py:421
  23.7 9.7 %collective-permute-start.3 = (bf16[8,9088]{1,0:T(8,128)(2,1)S(1)}, bf16[8,9088]{1,0:T(8,128)(2,1)S(1)}, u32[]{:S(2)}, u32[]{:S(2)}) collective-permute-start(bf16[8,9088]{1,0:T(8,128)(2,1)S(1)} %get-tuple-element.56), channel_id=1, source_target_pairs={{0,112},{4,116},{8,120},{12,124},{16,64},{20,68},{24,72},{28,76},{... | collective-permute-start | bytes 436232 | tf_op jit(solution)/shard_map/ppermute | solution.py:421
  47.8 57.7 %all-to-all-start.1 = ((bf16[8,88,2560]{2,1,0:T(8,128)(2,1)}), bf16[8,88,2560]{2,1,0:T(8,128)(2,1)}, u32[]{:S(2)}, u32[]{:S(2)}) async-start(bf16[8,88,2560]{2,1,0:T(8,128)(2,1)} %bitcast.28), calls=%async_computation.1 | async-start | bytes 7208960 | tf_op jit(solution)/shard_map/all_to_all | solution.py:424
  52.3 12.9 %collective-permute-start.4 = (bf16[8,9088]{1,0:T(8,128)(2,1)S(1)}, bf16[8,9088]{1,0:T(8,128)(2,1)S(1)}, u32[]{:S(2)}, u32[]{:S(2)}) collective-permute-start(bf16[8,9088]{1,0:T(8,128)(2,1)S(1)} %get-tuple-element.62), channel_id=1, source_target_pairs={{0,130},{4,134},{8,138},{12,142},{16,146},{20,150},{24,154},{28,15... | collective-permute-start | bytes 436232 | tf_op jit(solution)/shard_map/ppermute | solution.py:421
  56.7 9.6 %collective-permute-start.5 = (bf16[8,9088]{1,0:T(8,128)(2,1)S(1)}, bf16[8,9088]{1,0:T(8,128)(2,1)S(1)}, u32[]{:S(2)}, u32[]{:S(2)}) collective-permute-start(bf16[8,9088]{1,0:T(8,128)(2,1)S(1)} %get-tuple-element.63), channel_id=1, source_target_pairs={{0,146},{4,150},{8,154},{12,158},{16,162},{20,166},{24,170},{28,17... | collective-permute-start | bytes 436232 | tf_op jit(solution)/shard_map/ppermute | solution.py:421
  57.8 15.1 %collective-permute-start.6 = (bf16[8,9088]{1,0:T(8,128)(2,1)S(1)}, bf16[8,9088]{1,0:T(8,128)(2,1)S(1)}, u32[]{:S(2)}, u32[]{:S(2)}) collective-permute-start(bf16[8,9088]{1,0:T(8,128)(2,1)S(1)} %get-tuple-element.64), channel_id=1, source_target_pairs={{0,162},{4,166},{8,170},{12,174},{16,178},{20,182},{24,186},{28,19... | collective-permute-start | bytes 436232 | tf_op jit(solution)/shard_map/ppermute | solution.py:421
  63.7 14.7 %collective-permute-start.7 = (bf16[8,9088]{1,0:T(8,128)(2,1)S(1)}, bf16[8,9088]{1,0:T(8,128)(2,1)S(1)}, u32[]{:S(2)}, u32[]{:S(2)}) collective-permute-start(bf16[8,9088]{1,0:T(8,128)(2,1)S(1)} %get-tuple-element.65), channel_id=1, source_target_pairs={{0,178},{4,182},{8,186},{12,190},{16,130},{20,134},{24,138},{28,14... | collective-permute-start | bytes 436232 | tf_op jit(solution)/shard_map/ppermute | solution.py:421
  105.5 19.6 %all-to-all-start.2 = ((bf16[8,32,2560]{2,1,0:T(8,128)(2,1)}), bf16[8,32,2560]{2,1,0:T(8,128)(2,1)}, u32[]{:S(2)}, u32[]{:S(2)}) async-start(bf16[8,32,2560]{2,1,0:T(8,128)(2,1)} %bitcast.13), calls=%async_computation.2 | async-start | bytes 2621440 | tf_op jit(solution)/shard_map/all_to_all | solution.py:424
  133.8 17.9 %all-to-all-start.3 = ((bf16[8,32,2560]{2,1,0:T(8,128)(2,1)}), bf16[8,32,2560]{2,1,0:T(8,128)(2,1)S(1)}, u32[]{:S(2)}, u32[]{:S(2)}) async-start(bf16[8,32,2560]{2,1,0:T(8,128)(2,1)} %bitcast.18), calls=%async_computation.3 | async-start | bytes 2621440 | tf_op jit(solution)/shard_map/all_to_all | solution.py:424
  152.5 54.7 %copy-start.7 = (bf16[704,384]{1,0:T(8,128)(2,1)S(1)}, bf16[704,384]{1,0:T(8,128)(2,1)}, u32[]{:S(2)}) copy-start(bf16[704,384]{1,0:T(8,128)(2,1)} %copy-done.6) | copy-start | bytes 1622020
  152.5 54.7 %all-to-all-start.4 = ((bf16[8,88,2560]{2,1,0:T(8,128)(2,1)}), bf16[8,88,2560]{2,1,0:T(8,128)(2,1)}, u32[]{:S(2)}, u32[]{:S(2)}) async-start(bf16[8,88,2560]{2,1,0:T(8,128)(2,1)} %bitcast.39), calls=%async_computation.4 | async-start | bytes 7208960 | tf_op jit(solution)/shard_map/all_to_all | solution.py:424
  157.2 13.4 %collective-permute-start.8 = (bf16[8,8960]{1,0:T(8,128)(2,1)S(1)}, bf16[8,8960]{1,0:T(8,128)(2,1)S(1)}, u32[]{:S(2)}, u32[]{:S(2)}) collective-permute-start(bf16[8,8960]{1,0:T(8,128)(2,1)S(1)} %get-tuple-element.84), channel_id=1, source_target_pairs={{130,0},{134,4},{138,8},{142,12},{146,16},{150,20},{154,24},{158,2... | collective-permute-start | bytes 430088 | tf_op jit(solution)/shard_map/ppermute | solution.py:421
  162.9 8.3 %collective-permute-start.9 = (bf16[8,8960]{1,0:T(8,128)(2,1)S(1)}, bf16[8,8960]{1,0:T(8,128)(2,1)S(1)}, u32[]{:S(2)}, u32[]{:S(2)}) collective-permute-start(bf16[8,8960]{1,0:T(8,128)(2,1)S(1)} %get-tuple-element.85), channel_id=1, source_target_pairs={{146,0},{150,4},{154,8},{158,12},{162,16},{166,20},{170,24},{174,2... | collective-permute-start | bytes 430088 | tf_op jit(solution)/shard_map/ppermute | solution.py:421
  165.5 10.7 %collective-permute-start.10 = (bf16[8,8960]{1,0:T(8,128)(2,1)S(1)}, bf16[8,8960]{1,0:T(8,128)(2,1)S(1)}, u32[]{:S(2)}, u32[]{:S(2)}) collective-permute-start(bf16[8,8960]{1,0:T(8,128)(2,1)S(1)} %get-tuple-element.86), channel_id=1, source_target_pairs={{162,0},{166,4},{170,8},{174,12},{178,16},{182,20},{186,24},{190,2... | collective-permute-start | bytes 430088 | tf_op jit(solution)/shard_map/ppermute | solution.py:421
  169.5 12.0 %collective-permute-start.11 = (bf16[8,8960]{1,0:T(8,128)(2,1)S(1)}, bf16[8,8960]{1,0:T(8,128)(2,1)S(1)}, u32[]{:S(2)}, u32[]{:S(2)}) collective-permute-start(bf16[8,8960]{1,0:T(8,128)(2,1)S(1)} %get-tuple-element.87), channel_id=1, source_target_pairs={{178,0},{182,4},{186,8},{190,12},{130,16},{134,20},{138,24},{142,2... | collective-permute-start | bytes 430088 | tf_op jit(solution)/shard_map/ppermute | solution.py:421
  211.8 44.7 %all-to-all-start.5 = ((bf16[8,8,8960]{2,1,0:T(8,128)(2,1)}), bf16[8,8,8960]{2,1,0:T(8,128)(2,1)S(1)}, u32[]{:S(2)}, u32[]{:S(2)}) async-start(bf16[8,8,8960]{2,1,0:T(8,128)(2,1)} %bitcast.22), calls=%async_computation.5 | async-start | bytes 2293760 | tf_op jit(solution)/shard_map/all_to_all | solution.py:417
  223.5 21.3 %collective-permute-start.12 = (bf16[8,8960]{1,0:T(8,128)(2,1)S(1)}, bf16[8,8960]{1,0:T(8,128)(2,1)S(1)}, u32[]{:S(2)}, u32[]{:S(2)}) collective-permute-start(bf16[8,8960]{1,0:T(8,128)(2,1)S(1)} %get-tuple-element.92), channel_id=1, source_target_pairs={{64,0},{68,4},{72,8},{76,12},{80,16},{84,20},{88,24},{92,28},{96,3... | collective-permute-start | bytes 430088 | tf_op jit(solution)/shard_map/ppermute | solution.py:421
  227.9 20.9 %collective-permute-start.13 = (bf16[8,8960]{1,0:T(8,128)(2,1)S(1)}, bf16[8,8960]{1,0:T(8,128)(2,1)S(1)}, u32[]{:S(2)}, u32[]{:S(2)}) collective-permute-start(bf16[8,8960]{1,0:T(8,128)(2,1)S(1)} %get-tuple-element.93), channel_id=1, source_target_pairs={{80,0},{84,4},{88,8},{92,12},{96,16},{100,20},{104,24},{108,28},{1... | collective-permute-start | bytes 430088 | tf_op jit(solution)/shard_map/ppermute | solution.py:421
  232.3 21.1 %collective-permute-start.14 = (bf16[8,8960]{1,0:T(8,128)(2,1)S(1)}, bf16[8,8960]{1,0:T(8,128)(2,1)S(1)}, u32[]{:S(2)}, u32[]{:S(2)}) collective-permute-start(bf16[8,8960]{1,0:T(8,128)(2,1)S(1)} %get-tuple-element.94), channel_id=1, source_target_pairs={{96,0},{100,4},{104,8},{108,12},{112,16},{116,20},{120,24},{124,28... | collective-permute-start | bytes 430088 | tf_op jit(solution)/shard_map/ppermute | solution.py:421
  236.0 20.5 %collective-permute-start.15 = (bf16[8,8960]{1,0:T(8,128)(2,1)S(1)}, bf16[8,8960]{1,0:T(8,128)(2,1)S(1)}, u32[]{:S(2)}, u32[]{:S(2)}) collective-permute-start(bf16[8,8960]{1,0:T(8,128)(2,1)S(1)} %get-tuple-element.95), channel_id=1, source_target_pairs={{112,0},{116,4},{120,8},{124,12},{64,16},{68,20},{72,24},{76,28},{... | collective-permute-start | bytes 430088 | tf_op jit(solution)/shard_map/ppermute | solution.py:421
  257.1 4.1 %collective-permute-start.16 = (bf16[128,2560]{1,0:T(8,128)(2,1)S(1)}, bf16[128,2560]{1,0:T(8,128)(2,1)S(1)}, u32[]{:S(2)}, u32[]{:S(2)}) collective-permute-start(bf16[128,2560]{1,0:T(8,128)(2,1)S(1)} %combine.1), channel_id=1, source_target_pairs={{1,0},{0,1},{3,2},{2,3},{5,4},{4,5},{7,6},{6,7},{9,8},{8,9},{11,10... | collective-permute-start | bytes 1966088 | tf_op jit(solution)/shard_map/ppermute | solution.py:505
  (9 other events, 33.9 us)

commit v6 on v5

--- a/solution.py
+++ b/solution.py
@@ -429,7 +429,7 @@
         depth = (SLABS + 1) * height
         return call(
             functools.partial(spread_kernel, (in_group, cap)), name, len(blocks),
-            [array(rows, features), array(rows, depth)], 48, 2 * rows * depth * features,
+            [array(rows, features), array(rows, depth)], 52 if rows > 256 else 48, 2 * rows * depth * features,
             [hbm, vmem],
             [pltpu.VMEM((height, sent), BF16), pltpu.VMEM((rows, features), BF16), pltpu.SemaphoreType.DMA((2,))],
             scalars=False,

time: 263 us -> 264 us (level)
  no operation moved by 1% of the time
where the time goes in v6:
time: 264 us; the launch traced here: 263 us
  waiting for transfers between devices  116 us (44%)
  starting transfers between devices  90.7 us (34%)
  Pallas kernels  45.8 us (17%)
  local copies, waits for them, and re-layouts  9.59 us (4%)
    all_to_all x4, waiting for transfers between devices, in_groups(): lax.all_to_all(rows.reshape(in_group, -1, features), 'inner', 0, 0, tiled...  60 us
    ppermute x16, starting transfers between devices, hop(): lax.ppermute(b, both, routes_over(hops, dy, back))  48.9 us
    ppermute x16, waiting for transfers between devices, hop(): lax.ppermute(b, both, routes_over(hops, dy, back))  45.8 us
    all_to_all x2, starting transfers between devices, near_swap(): lax.all_to_all(block.reshape(8, SUB, width), both, 0, 0, axis_index_group...  22.3 us
    pallas_call x2, Pallas kernels, expert_call(): pl.pallas_call(functools.partial(expert_kernel, held), name=name, in_spec...  21.1 us
    all_to_all x4, starting transfers between devices, in_groups(): lax.all_to_all(rows.reshape(in_group, -1, features), 'inner', 0, 0, tiled...  17.1 us
    unnamed x21, local copies, waits for them, and re-layouts  9.5 us
    all_to_all x2, waiting for transfers between devices, near_swap(): lax.all_to_all(block.reshape(8, SUB, width), both, 0, 0, axis_index_group...  8.48 us
  transfers between devices with their start and end apart: 23, of which 19 were waited for; matrix products, arithmetic and copies ran while one was open for 0% of the time, Pallas kernels for 9%

profile of v6, /device:TPU:1, one launch (start us, length us, event | category | flops | bytes accessed | tf_op | source)
XLA Modules:
  0.0 263.0 jit_solution(14698504233021092225)
XLA Ops:
  6.1 10.6 %all-to-all-start = ((bf16[8,8,9088]{2,1,0:T(8,128)(2,1)}), bf16[8,8,9088]{2,1,0:T(8,128)(2,1)S(1)}, u32[]{:S(2)}, u32[]{:S(2)}) async-start(bf16[8,8,9088]{2,1,0:T(8,128)(2,1)} %bitcast.9), calls=%async_computation | async-start | bytes 2326528 | tf_op jit(solution)/shard_map/all_to_all | solution.py:417
  16.7 4.9 %collective-permute-start.1 = (bf16[8,9088]{1,0:T(8,128)(2,1)S(1)}, bf16[8,9088]{1,0:T(8,128)(2,1)S(1)}, u32[]{:S(2)}, u32[]{:S(2)}) collective-permute-start(bf16[8,9088]{1,0:T(8,128)(2,1)S(1)} %get-tuple-element.54), channel_id=1, source_target_pairs={{0,80},{4,84},{8,88},{12,92},{16,96},{20,100},{24,104},{28,108},{3... | collective-permute-start | bytes 436232 | tf_op jit(solution)/shard_map/ppermute | solution.py:421
  33.4 8.5 %all-to-all-done = bf16[8,8,9088]{2,1,0:T(8,128)(2,1)S(1)} async-done(((bf16[8,8,9088]{2,1,0:T(8,128)(2,1)}), bf16[8,8,9088]{2,1,0:T(8,128)(2,1)S(1)}, u32[]{:S(2)}, u32[]{:S(2)}) %all-to-all-start) | async-done | bytes 1163296 | tf_op jit(solution)/shard_map/all_to_all | solution.py:417
  42.9 5.1 %spread_near.1 = (bf16[704,2560]{1,0:T(8,128)(2,1)}, bf16[704,384]{1,0:T(8,128)(2,1)S(1)}) custom-call(bf16[64,9088]{1,0:T(8,128)(2,1)} %bitcast.39, bf16[8,9088]{1,0:T(8,128)(2,1)S(1)} %collective-permute-done.refs_1_, bf16[8,9088]{1,0:T(8,128)(2,1)S(1)} %collective-permute-done.1.refs_2_, bf16[8,9088]{1,0:T(8,128)(2,1)S(1)} %collective-permute-done.2.refs_3_, ...), custom_call_target="tpu_custom_call" | custom-call | flops 1384120320 | bytes 4145152 | tf_op jit(solution)/shard_map/spread_near/pallas_call | solution.py:430
  48.8 4.5 %all-to-all-start.1 = ((bf16[8,88,2560]{2,1,0:T(8,128)(2,1)}), bf16[8,88,2560]{2,1,0:T(8,128)(2,1)}, u32[]{:S(2)}, u32[]{:S(2)}) async-start(bf16[8,88,2560]{2,1,0:T(8,128)(2,1)} %bitcast.38), calls=%async_computation.1 | async-start | bytes 7208960 | tf_op jit(solution)/shard_map/all_to_all | solution.py:424
  58.8 5.9 %collective-permute-start.6 = (bf16[8,9088]{1,0:T(8,128)(2,1)S(1)}, bf16[8,9088]{1,0:T(8,128)(2,1)S(1)}, u32[]{:S(2)}, u32[]{:S(2)}) collective-permute-start(bf16[8,9088]{1,0:T(8,128)(2,1)S(1)} %get-tuple-element.64), channel_id=1, source_target_pairs={{0,162},{4,166},{8,170},{12,174},{16,178},{20,182},{24,186},{28,19... | collective-permute-start | bytes 436232 | tf_op jit(solution)/shard_map/ppermute | solution.py:421
  67.3 6.6 %collective-permute-done.6.refs_2_ = bf16[8,9088]{1,0:T(8,128)(2,1)S(1)} collective-permute-done((bf16[8,9088]{1,0:T(8,128)(2,1)S(1)}, bf16[8,9088]{1,0:T(8,128)(2,1)S(1)}, u32[]{:S(2)}, u32[]{:S(2)}) %collective-permute-start.6) | collective-permute-done | bytes 145440 | tf_op jit(solution)/shard_map/ppermute | solution.py:421
  73.9 5.6 %collective-permute-done.7.refs_3_ = bf16[8,9088]{1,0:T(8,128)(2,1)S(1)} collective-permute-done((bf16[8,9088]{1,0:T(8,128)(2,1)S(1)}, bf16[8,9088]{1,0:T(8,128)(2,1)S(1)}, u32[]{:S(2)}, u32[]{:S(2)}) %collective-permute-start.7) | collective-permute-done | bytes 145440 | tf_op jit(solution)/shard_map/ppermute | solution.py:421
  81.0 25.5 %all-to-all-done.1 = bf16[8,88,2560]{2,1,0:T(8,128)(2,1)} async-done(((bf16[8,88,2560]{2,1,0:T(8,128)(2,1)}), bf16[8,88,2560]{2,1,0:T(8,128)(2,1)}, u32[]{:S(2)}, u32[]{:S(2)}) %all-to-all-start.1) | async-done | bytes 3604512 | tf_op jit(solution)/shard_map/all_to_all | solution.py:424
  106.6 4.4 %all-to-all-start.2 = ((bf16[8,32,2560]{2,1,0:T(8,128)(2,1)}), bf16[8,32,2560]{2,1,0:T(8,128)(2,1)}, u32[]{:S(2)}, u32[]{:S(2)}) async-start(bf16[8,32,2560]{2,1,0:T(8,128)(2,1)} %bitcast.13), calls=%async_computation.2 | async-start | bytes 2621440 | tf_op jit(solution)/shard_map/all_to_all | solution.py:424
  112.8 5.2 %align.1 = (bf16[704,1536]{1,0:T(8,128)(2,1)S(1)}, bf16[256,1536]{1,0:T(8,128)(2,1)S(1)}) custom-call(s32[6]{0:T(128)S(1)} %stack.27.where_ref, bf16[896,1536]{1,0:T(8,128)(2,1)S(1)} %bitcast.30), custom_call_target="tpu_custom_call" | custom-call | flops 2642411520 | bytes 2949120 | tf_op jit(solution)/shard_map/align/pallas_call | solution.py:472
  119.4 6.8 %all-to-all-done.2 = bf16[8,32,2560]{2,1,0:T(8,128)(2,1)} async-done(((bf16[8,32,2560]{2,1,0:T(8,128)(2,1)}), bf16[8,32,2560]{2,1,0:T(8,128)(2,1)}, u32[]{:S(2)}, u32[]{:S(2)}) %all-to-all-start.2) | async-done | bytes 1310752 | tf_op jit(solution)/shard_map/all_to_all | solution.py:424
  126.2 8.6 %expert_far.1 = (bf16[256,2560]{1,0:T(8,128)(2,1)}, bf16[256,768]{1,0:T(8,128)(2,1)S(1)}) custom-call(bf16[256,2560]{1,0:T(8,128)(2,1)} %bitcast.14.x_hbm, bf16[256,1536]{1,0:T(8,128)(2,1)S(1)} %get-tuple-element.74.kept_hbm, bf16[768,2560]{1,0:T(8,128)(2,1)} %bitcast.33, bf16[2560,768]{1,0:T(8,128)(2,1)} %bitcast.35), custom_call_target="tpu_custom_call" | custom-call | flops 2013265920 | bytes 10485760 | tf_op jit(solution)/shard_map/expert_far/pallas_call | solution.py:514
  138.4 12.5 %expert_near.1 = (bf16[704,2560]{1,0:T(8,128)(2,1)}, bf16[704,768]{1,0:T(8,128)(2,1)}) custom-call(bf16[704,2560]{1,0:T(8,128)(2,1)} %bitcast.12.x_hbm, bf16[704,1536]{1,0:T(8,128)(2,1)} %copy-done.8, bf16[768,2560]{1,0:T(8,128)(2,1)} %bitcast.34, bf16[2560,768]{1,0:T(8,128)(2,1)} %bitcast.36), custom_call_target="tpu_custom_call" | custom-call | flops 5536481280 | bytes 15073280 | tf_op jit(solution)/shard_map/expert_near/pallas_call | solution.py:514
  153.6 4.6 %all-to-all-start.4 = ((bf16[8,88,2560]{2,1,0:T(8,128)(2,1)}), bf16[8,88,2560]{2,1,0:T(8,128)(2,1)}, u32[]{:S(2)}, u32[]{:S(2)}) async-start(bf16[8,88,2560]{2,1,0:T(8,128)(2,1)} %bitcast.37), calls=%async_computation.4 | async-start | bytes 7208960 | tf_op jit(solution)/shard_map/all_to_all | solution.py:424
  158.2 5.7 %collective-permute-start.8 = (bf16[8,8960]{1,0:T(8,128)(2,1)S(1)}, bf16[8,8960]{1,0:T(8,128)(2,1)S(1)}, u32[]{:S(2)}, u32[]{:S(2)}) collective-permute-start(bf16[8,8960]{1,0:T(8,128)(2,1)S(1)} %get-tuple-element.84), channel_id=1, source_target_pairs={{130,0},{134,4},{138,8},{142,12},{146,16},{150,20},{154,24},{158,2... | collective-permute-start | bytes 430088 | tf_op jit(solution)/shard_map/ppermute | solution.py:421
  172.2 5.0 %collective-permute-done.10.refs_7_ = bf16[8,8960]{1,0:T(8,128)(2,1)S(1)} collective-permute-done((bf16[8,8960]{1,0:T(8,128)(2,1)S(1)}, bf16[8,8960]{1,0:T(8,128)(2,1)S(1)}, u32[]{:S(2)}, u32[]{:S(2)}) %collective-permute-start.10) | collective-permute-done | bytes 143392 | tf_op jit(solution)/shard_map/ppermute | solution.py:421
  177.3 5.2 %collective-permute-done.11.refs_8_ = bf16[8,8960]{1,0:T(8,128)(2,1)S(1)} collective-permute-done((bf16[8,8960]{1,0:T(8,128)(2,1)S(1)}, bf16[8,8960]{1,0:T(8,128)(2,1)S(1)}, u32[]{:S(2)}, u32[]{:S(2)}) %collective-permute-start.11) | collective-permute-done | bytes 143392 | tf_op jit(solution)/shard_map/ppermute | solution.py:421
  182.4 25.8 %all-to-all-done.4 = bf16[8,88,2560]{2,1,0:T(8,128)(2,1)} async-done(((bf16[8,88,2560]{2,1,0:T(8,128)(2,1)}), bf16[8,88,2560]{2,1,0:T(8,128)(2,1)}, u32[]{:S(2)}, u32[]{:S(2)}) %all-to-all-start.4) | async-done | bytes 3604512 | tf_op jit(solution)/shard_map/all_to_all | solution.py:424
  208.2 4.6 %gather_near.1 = (bf16[64,8960]{1,0:T(8,128)(2,1)}, bf16[8,8960]{1,0:T(8,128)(2,1)S(1)}, bf16[8,8960]{1,0:T(8,128)(2,1)S(1)}, bf16[8,8960]{1,0:T(8,128)(2,1)S(1)}, bf16[8,8960]{1,0:T(8,128)(2,1)S(1)}) custom-call(bf16[704,2560]{1,0:T(8,128)(2,1)} %bitcast.21.rows_hbm, bf16[704,384]{1,0:T(8,128)(2,1)S(1)} %copy-done.6), custom_call_target="tpu_custom_call" | custom-call | flops 1384120320 | bytes 3604480 | tf_op jit(solution)/shard_map/gather_near/pallas_call | solution.py:439
  212.8 11.7 %all-to-all-start.5 = ((bf16[8,8,8960]{2,1,0:T(8,128)(2,1)}), bf16[8,8,8960]{2,1,0:T(8,128)(2,1)S(1)}, u32[]{:S(2)}, u32[]{:S(2)}) async-start(bf16[8,8,8960]{2,1,0:T(8,128)(2,1)} %bitcast.22), calls=%async_computation.5 | async-start | bytes 2293760 | tf_op jit(solution)/shard_map/all_to_all | solution.py:417
  224.5 4.4 %collective-permute-start.12 = (bf16[8,8960]{1,0:T(8,128)(2,1)S(1)}, bf16[8,8960]{1,0:T(8,128)(2,1)S(1)}, u32[]{:S(2)}, u32[]{:S(2)}) collective-permute-start(bf16[8,8960]{1,0:T(8,128)(2,1)S(1)} %get-tuple-element.92), channel_id=1, source_target_pairs={{64,0},{68,4},{72,8},{76,12},{80,16},{84,20},{88,24},{92,28},{96,3... | collective-permute-start | bytes 430088 | tf_op jit(solution)/shard_map/ppermute | solution.py:421
  228.9 4.5 %collective-permute-start.13 = (bf16[8,8960]{1,0:T(8,128)(2,1)S(1)}, bf16[8,8960]{1,0:T(8,128)(2,1)S(1)}, u32[]{:S(2)}, u32[]{:S(2)}) collective-permute-start(bf16[8,8960]{1,0:T(8,128)(2,1)S(1)} %get-tuple-element.93), channel_id=1, source_target_pairs={{80,0},{84,4},{88,8},{92,12},{96,16},{100,20},{104,24},{108,28},{1... | collective-permute-start | bytes 430088 | tf_op jit(solution)/shard_map/ppermute | solution.py:421
  249.8 4.6 %collective-permute-done.14.refs_3_ = bf16[8,8960]{1,0:T(8,128)(2,1)S(1)} collective-permute-done((bf16[8,8960]{1,0:T(8,128)(2,1)S(1)}, bf16[8,8960]{1,0:T(8,128)(2,1)S(1)}, u32[]{:S(2)}, u32[]{:S(2)}) %collective-permute-start.14) | collective-permute-done | bytes 143392 | tf_op jit(solution)/shard_map/ppermute | solution.py:421
  (55 shorter events, 71.3 us)
Async XLA Ops:
  6.1 35.8 %all-to-all-start = ((bf16[8,8,9088]{2,1,0:T(8,128)(2,1)}), bf16[8,8,9088]{2,1,0:T(8,128)(2,1)S(1)}, u32[]{:S(2)}, u32[]{:S(2)}) async-start(bf16[8,8,9088]{2,1,0:T(8,128)(2,1)} %bitcast.9), calls=%async_computation | async-start | bytes 2326528 | tf_op jit(solution)/shard_map/all_to_all | solution.py:417
  16.7 9.9 %collective-permute-start = (bf16[8,9088]{1,0:T(8,128)(2,1)S(1)}, bf16[8,9088]{1,0:T(8,128)(2,1)S(1)}, u32[]{:S(2)}, u32[]{:S(2)}) collective-permute-start(bf16[8,9088]{1,0:T(8,128)(2,1)S(1)} %get-tuple-element.53), channel_id=1, source_target_pairs={{0,64},{4,68},{8,72},{12,76},{16,80},{20,84},{24,88},{28,92},{32,9... | collective-permute-start | bytes 436232 | tf_op jit(solution)/shard_map/ppermute | solution.py:421
  16.7 11.2 %collective-permute-start.1 = (bf16[8,9088]{1,0:T(8,128)(2,1)S(1)}, bf16[8,9088]{1,0:T(8,128)(2,1)S(1)}, u32[]{:S(2)}, u32[]{:S(2)}) collective-permute-start(bf16[8,9088]{1,0:T(8,128)(2,1)S(1)} %get-tuple-element.54), channel_id=1, source_target_pairs={{0,80},{4,84},{8,88},{12,92},{16,96},{20,100},{24,104},{28,108},{3... | collective-permute-start | bytes 436232 | tf_op jit(solution)/shard_map/ppermute | solution.py:421
  21.6 10.4 %collective-permute-start.2 = (bf16[8,9088]{1,0:T(8,128)(2,1)S(1)}, bf16[8,9088]{1,0:T(8,128)(2,1)S(1)}, u32[]{:S(2)}, u32[]{:S(2)}) collective-permute-start(bf16[8,9088]{1,0:T(8,128)(2,1)S(1)} %get-tuple-element.55), channel_id=1, source_target_pairs={{0,96},{4,100},{8,104},{12,108},{16,112},{20,116},{24,120},{28,124... | collective-permute-start | bytes 436232 | tf_op jit(solution)/shard_map/ppermute | solution.py:421
  23.7 9.7 %collective-permute-start.3 = (bf16[8,9088]{1,0:T(8,128)(2,1)S(1)}, bf16[8,9088]{1,0:T(8,128)(2,1)S(1)}, u32[]{:S(2)}, u32[]{:S(2)}) collective-permute-start(bf16[8,9088]{1,0:T(8,128)(2,1)S(1)} %get-tuple-element.56), channel_id=1, source_target_pairs={{0,112},{4,116},{8,120},{12,124},{16,64},{20,68},{24,72},{28,76},{... | collective-permute-start | bytes 436232 | tf_op jit(solution)/shard_map/ppermute | solution.py:421
  48.8 57.7 %all-to-all-start.1 = ((bf16[8,88,2560]{2,1,0:T(8,128)(2,1)}), bf16[8,88,2560]{2,1,0:T(8,128)(2,1)}, u32[]{:S(2)}, u32[]{:S(2)}) async-start(bf16[8,88,2560]{2,1,0:T(8,128)(2,1)} %bitcast.38), calls=%async_computation.1 | async-start | bytes 7208960 | tf_op jit(solution)/shard_map/all_to_all | solution.py:424
  53.3 12.9 %collective-permute-start.4 = (bf16[8,9088]{1,0:T(8,128)(2,1)S(1)}, bf16[8,9088]{1,0:T(8,128)(2,1)S(1)}, u32[]{:S(2)}, u32[]{:S(2)}) collective-permute-start(bf16[8,9088]{1,0:T(8,128)(2,1)S(1)} %get-tuple-element.62), channel_id=1, source_target_pairs={{0,130},{4,134},{8,138},{12,142},{16,146},{20,150},{24,154},{28,15... | collective-permute-start | bytes 436232 | tf_op jit(solution)/shard_map/ppermute | solution.py:421
  57.7 9.6 %collective-permute-start.5 = (bf16[8,9088]{1,0:T(8,128)(2,1)S(1)}, bf16[8,9088]{1,0:T(8,128)(2,1)S(1)}, u32[]{:S(2)}, u32[]{:S(2)}) collective-permute-start(bf16[8,9088]{1,0:T(8,128)(2,1)S(1)} %get-tuple-element.63), channel_id=1, source_target_pairs={{0,146},{4,150},{8,154},{12,158},{16,162},{20,166},{24,170},{28,17... | collective-permute-start | bytes 436232 | tf_op jit(solution)/shard_map/ppermute | solution.py:421
  58.8 15.1 %collective-permute-start.6 = (bf16[8,9088]{1,0:T(8,128)(2,1)S(1)}, bf16[8,9088]{1,0:T(8,128)(2,1)S(1)}, u32[]{:S(2)}, u32[]{:S(2)}) collective-permute-start(bf16[8,9088]{1,0:T(8,128)(2,1)S(1)} %get-tuple-element.64), channel_id=1, source_target_pairs={{0,162},{4,166},{8,170},{12,174},{16,178},{20,182},{24,186},{28,19... | collective-permute-start | bytes 436232 | tf_op jit(solution)/shard_map/ppermute | solution.py:421
  64.7 14.8 %collective-permute-start.7 = (bf16[8,9088]{1,0:T(8,128)(2,1)S(1)}, bf16[8,9088]{1,0:T(8,128)(2,1)S(1)}, u32[]{:S(2)}, u32[]{:S(2)}) collective-permute-start(bf16[8,9088]{1,0:T(8,128)(2,1)S(1)} %get-tuple-element.65), channel_id=1, source_target_pairs={{0,178},{4,182},{8,186},{12,190},{16,130},{20,134},{24,138},{28,14... | collective-permute-start | bytes 436232 | tf_op jit(solution)/shard_map/ppermute | solution.py:421
  106.6 19.6 %all-to-all-start.2 = ((bf16[8,32,2560]{2,1,0:T(8,128)(2,1)}), bf16[8,32,2560]{2,1,0:T(8,128)(2,1)}, u32[]{:S(2)}, u32[]{:S(2)}) async-start(bf16[8,32,2560]{2,1,0:T(8,128)(2,1)} %bitcast.13), calls=%async_computation.2 | async-start | bytes 2621440 | tf_op jit(solution)/shard_map/all_to_all | solution.py:424
  134.8 18.0 %all-to-all-start.3 = ((bf16[8,32,2560]{2,1,0:T(8,128)(2,1)}), bf16[8,32,2560]{2,1,0:T(8,128)(2,1)S(1)}, u32[]{:S(2)}, u32[]{:S(2)}) async-start(bf16[8,32,2560]{2,1,0:T(8,128)(2,1)} %bitcast.18), calls=%async_computation.3 | async-start | bytes 2621440 | tf_op jit(solution)/shard_map/all_to_all | solution.py:424
  153.6 54.7 %copy-start.6 = (bf16[704,384]{1,0:T(8,128)(2,1)S(1)}, bf16[704,384]{1,0:T(8,128)(2,1)}, u32[]{:S(2)}) copy-start(bf16[704,384]{1,0:T(8,128)(2,1)} %copy-done.5) | copy-start | bytes 1622020
  153.6 54.7 %all-to-all-start.4 = ((bf16[8,88,2560]{2,1,0:T(8,128)(2,1)}), bf16[8,88,2560]{2,1,0:T(8,128)(2,1)}, u32[]{:S(2)}, u32[]{:S(2)}) async-start(bf16[8,88,2560]{2,1,0:T(8,128)(2,1)} %bitcast.37), calls=%async_computation.4 | async-start | bytes 7208960 | tf_op jit(solution)/shard_map/all_to_all | solution.py:424
  158.2 13.4 %collective-permute-start.8 = (bf16[8,8960]{1,0:T(8,128)(2,1)S(1)}, bf16[8,8960]{1,0:T(8,128)(2,1)S(1)}, u32[]{:S(2)}, u32[]{:S(2)}) collective-permute-start(bf16[8,8960]{1,0:T(8,128)(2,1)S(1)} %get-tuple-element.84), channel_id=1, source_target_pairs={{130,0},{134,4},{138,8},{142,12},{146,16},{150,20},{154,24},{158,2... | collective-permute-start | bytes 430088 | tf_op jit(solution)/shard_map/ppermute | solution.py:421
  163.9 8.3 %collective-permute-start.9 = (bf16[8,8960]{1,0:T(8,128)(2,1)S(1)}, bf16[8,8960]{1,0:T(8,128)(2,1)S(1)}, u32[]{:S(2)}, u32[]{:S(2)}) collective-permute-start(bf16[8,8960]{1,0:T(8,128)(2,1)S(1)} %get-tuple-element.85), channel_id=1, source_target_pairs={{146,0},{150,4},{154,8},{158,12},{162,16},{166,20},{170,24},{174,2... | collective-permute-start | bytes 430088 | tf_op jit(solution)/shard_map/ppermute | solution.py:421
  166.5 10.7 %collective-permute-start.10 = (bf16[8,8960]{1,0:T(8,128)(2,1)S(1)}, bf16[8,8960]{1,0:T(8,128)(2,1)S(1)}, u32[]{:S(2)}, u32[]{:S(2)}) collective-permute-start(bf16[8,8960]{1,0:T(8,128)(2,1)S(1)} %get-tuple-element.86), channel_id=1, source_target_pairs={{162,0},{166,4},{170,8},{174,12},{178,16},{182,20},{186,24},{190,2... | collective-permute-start | bytes 430088 | tf_op jit(solution)/shard_map/ppermute | solution.py:421
  170.5 12.0 %collective-permute-start.11 = (bf16[8,8960]{1,0:T(8,128)(2,1)S(1)}, bf16[8,8960]{1,0:T(8,128)(2,1)S(1)}, u32[]{:S(2)}, u32[]{:S(2)}) collective-permute-start(bf16[8,8960]{1,0:T(8,128)(2,1)S(1)} %get-tuple-element.87), channel_id=1, source_target_pairs={{178,0},{182,4},{186,8},{190,12},{130,16},{134,20},{138,24},{142,2... | collective-permute-start | bytes 430088 | tf_op jit(solution)/shard_map/ppermute | solution.py:421
  212.8 44.7 %all-to-all-start.5 = ((bf16[8,8,8960]{2,1,0:T(8,128)(2,1)}), bf16[8,8,8960]{2,1,0:T(8,128)(2,1)S(1)}, u32[]{:S(2)}, u32[]{:S(2)}) async-start(bf16[8,8,8960]{2,1,0:T(8,128)(2,1)} %bitcast.22), calls=%async_computation.5 | async-start | bytes 2293760 | tf_op jit(solution)/shard_map/all_to_all | solution.py:417
  224.5 21.3 %collective-permute-start.12 = (bf16[8,8960]{1,0:T(8,128)(2,1)S(1)}, bf16[8,8960]{1,0:T(8,128)(2,1)S(1)}, u32[]{:S(2)}, u32[]{:S(2)}) collective-permute-start(bf16[8,8960]{1,0:T(8,128)(2,1)S(1)} %get-tuple-element.92), channel_id=1, source_target_pairs={{64,0},{68,4},{72,8},{76,12},{80,16},{84,20},{88,24},{92,28},{96,3... | collective-permute-start | bytes 430088 | tf_op jit(solution)/shard_map/ppermute | solution.py:421
  228.9 20.9 %collective-permute-start.13 = (bf16[8,8960]{1,0:T(8,128)(2,1)S(1)}, bf16[8,8960]{1,0:T(8,128)(2,1)S(1)}, u32[]{:S(2)}, u32[]{:S(2)}) collective-permute-start(bf16[8,8960]{1,0:T(8,128)(2,1)S(1)} %get-tuple-element.93), channel_id=1, source_target_pairs={{80,0},{84,4},{88,8},{92,12},{96,16},{100,20},{104,24},{108,28},{1... | collective-permute-start | bytes 430088 | tf_op jit(solution)/shard_map/ppermute | solution.py:421
  233.4 21.0 %collective-permute-start.14 = (bf16[8,8960]{1,0:T(8,128)(2,1)S(1)}, bf16[8,8960]{1,0:T(8,128)(2,1)S(1)}, u32[]{:S(2)}, u32[]{:S(2)}) collective-permute-start(bf16[8,8960]{1,0:T(8,128)(2,1)S(1)} %get-tuple-element.94), channel_id=1, source_target_pairs={{96,0},{100,4},{104,8},{108,12},{112,16},{116,20},{120,24},{124,28... | collective-permute-start | bytes 430088 | tf_op jit(solution)/shard_map/ppermute | solution.py:421
  237.0 20.5 %collective-permute-start.15 = (bf16[8,8960]{1,0:T(8,128)(2,1)S(1)}, bf16[8,8960]{1,0:T(8,128)(2,1)S(1)}, u32[]{:S(2)}, u32[]{:S(2)}) collective-permute-start(bf16[8,8960]{1,0:T(8,128)(2,1)S(1)} %get-tuple-element.95), channel_id=1, source_target_pairs={{112,0},{116,4},{120,8},{124,12},{64,16},{68,20},{72,24},{76,28},{... | collective-permute-start | bytes 430088 | tf_op jit(solution)/shard_map/ppermute | solution.py:421
  258.1 4.1 %collective-permute-start.16 = (bf16[128,2560]{1,0:T(8,128)(2,1)S(1)}, bf16[128,2560]{1,0:T(8,128)(2,1)S(1)}, u32[]{:S(2)}, u32[]{:S(2)}) collective-permute-start(bf16[128,2560]{1,0:T(8,128)(2,1)S(1)} %combine.1), channel_id=1, source_target_pairs={{1,0},{0,1},{3,2},{2,3},{5,4},{4,5},{7,6},{6,7},{9,8},{8,9},{11,10... | collective-permute-start | bytes 1966088 | tf_op jit(solution)/shard_map/ppermute | solution.py:505
  (9 other events, 33.1 us)
